TPU v7x, 32 devices: a whole 2x2x4 slice. The times are simulated.
32 devices in a mesh: grp: 4 (over z), seq: 8 (over y, x, core).
Axes of the slice: x: 2, y: 2, z: 4, core: 2. Of those that a mesh axis runs over, the one named last changes fastest.
Arguments:
- tokens: bfloat16 [2, 4608, 2304], P(None, ('grp', 'seq')), may hold values from -8 to 8
- cotangent: bfloat16 [2, 4608, 2304], P(None, ('grp', 'seq')), may hold values from -6 to 6
- segments: int32 [2, 4608], P(None, 'grp'), may hold values from 0 to 8, as said below
- attn_in: float32 [2304, 4096], P(('grp', 'seq')), may hold values from -0.1388889 to 0.1388889
- attn_out: float32 [2304, 2048], P(('grp', 'seq')), may hold values from -0.125 to 0.125
- ffn_in: float32 [2304, 18432], P(('grp', 'seq')), may hold values from -0.125 to 0.125
- ffn_out: float32 [2304, 9216], P(('grp', 'seq')), may hold values from -0.0625 to 0.0625
- gains: float32 [4, 2304], P(None, ('grp', 'seq')), may hold values from 0.5 to 1.5
- attn_in_mom: float32 [2304, 4096], P(('grp', 'seq')), may hold values from -256 to 256
- attn_out_mom: float32 [2304, 2048], P(('grp', 'seq')), may hold values from -256 to 256
- ffn_in_mom: float32 [2304, 18432], P(('grp', 'seq')), may hold values from -256 to 256
- ffn_out_mom: float32 [2304, 9216], P(('grp', 'seq')), may hold values from -256 to 256
- gains_mom: float32 [4, 2304], P(None, ('grp', 'seq')), may hold values from -512 to 512
- attn_in_avg: float32 [2304, 4096], P(('grp', 'seq')), may hold values from -0.125 to 0.125
- attn_out_avg: float32 [2304, 2048], P(('grp', 'seq')), may hold values from -0.125 to 0.125
- ffn_in_avg: float32 [2304, 18432], P(('grp', 'seq')), may hold values from -0.125 to 0.125
- ffn_out_avg: float32 [2304, 9216], P(('grp', 'seq')), may hold values from -0.0625 to 0.0625
- gains_avg: float32 [4, 2304], P(None, ('grp', 'seq')), may hold values from 0.5 to 1.5
Outputs:
- output: bfloat16 [2, 4608, 2304], P(None, ('grp', 'seq'))
- input_grad: float32 [2, 4608, 2304], P(None, ('grp', 'seq'))
- attn_in_new: float32 [2304, 4096], P(('grp', 'seq'))
- attn_in_mom_new: float32 [2304, 4096], P(('grp', 'seq'))
- attn_in_avg_new: float32 [2304, 4096], P(('grp', 'seq'))
- attn_in_copy: bfloat16 [2304, 4096], P(('grp', 'seq'))
- attn_out_new: float32 [2304, 2048], P(('grp', 'seq'))
- attn_out_mom_new: float32 [2304, 2048], P(('grp', 'seq'))
- attn_out_avg_new: float32 [2304, 2048], P(('grp', 'seq'))
- attn_out_copy: bfloat16 [2304, 2048], P(('grp', 'seq'))
- ffn_in_new: float32 [2304, 18432], P(('grp', 'seq'))
- ffn_in_mom_new: float32 [2304, 18432], P(('grp', 'seq'))
- ffn_in_avg_new: float32 [2304, 18432], P(('grp', 'seq'))
- ffn_in_copy: bfloat16 [2304, 18432], P(('grp', 'seq'))
- ffn_out_new: float32 [2304, 9216], P(('grp', 'seq'))
- ffn_out_mom_new: float32 [2304, 9216], P(('grp', 'seq'))
- ffn_out_avg_new: float32 [2304, 9216], P(('grp', 'seq'))
- ffn_out_copy: bfloat16 [2304, 9216], P(('grp', 'seq'))
- gains_new: float32 [4, 2304], P(None, ('grp', 'seq'))
- gains_mom_new: float32 [4, 2304], P(None, ('grp', 'seq'))
- gains_avg_new: float32 [4, 2304], P(None, ('grp', 'seq'))
- gains_copy: bfloat16 [4, 2304], P(None, ('grp', 'seq'))
Inputs may be any that keep to these rules, and one draw needn't show every extreme that they name: `segments`: in each group of 1152 rows the first 1024 rows are 0, the rest are 1 to 8 in rising order, each continuation one or more rows.
All inputs are finite; a program needn't handle non-finite values.
Results may differ from a plain program's by a relative error of at most 0.017.
Values may be sent and summed in bfloat16 or wider, within the bound.
No kernel may reach another device: no remote copies, remote signals or barrier semaphores. Data moves between devices by JAX's collectives and lax.ppermute only.
A program may use at most 384 MiB of HBM per device.

v0:
```python
import jax
import jax.numpy as jnp
from jax import lax
from jax.sharding import PartitionSpec as P

HEADS = 8
KV_HEADS = 4
HEAD = 256
PROMPT = 1024
CONTS = 8


eps_norm = 1e-06
soft_cap = 50.0
momentum_decay = 0.5
average_decay = 0.5
weight_rate = 0.03
gain_rate = 0.2
rope_base = 10000.0


def scaled(field, gain):
    return field * lax.rsqrt(jnp.mean(field * field, axis=-1, keepdims=True) + eps_norm) * gain


def place_tokens(seg_group, own_segment, row_index):
    levels = jnp.arange(CONTS + 1, dtype=jnp.int32)
    before = jnp.sum((seg_group[None, :] < levels[:, None]).astype(jnp.int32), axis=1)
    seg_start = jnp.sum(
        jnp.where(own_segment[:, None] == levels[None, :], before[None, :], 0), axis=1
    )
    return row_index - seg_start + jnp.where(own_segment > 0, PROMPT, 0)


def rotate(field, positions):
    half = field.shape[-1] // 2
    freqs = rope_base ** (-jnp.arange(half, dtype=jnp.float32) * 2.0 / field.shape[-1])
    angles = positions.astype(jnp.float32)[:, None] * freqs[None, :]
    cosine = jnp.cos(angles)[:, None, :]
    sine = jnp.sin(angles)[:, None, :]
    first_half = field[..., :half]
    second_half = field[..., half:]
    return jnp.concatenate(
        [first_half * cosine - second_half * sine, second_half * cosine + first_half * sine],
        axis=-1,
    )


def glu_part(gate, upper):
    return jax.nn.gelu(gate, approximate=True) * upper


def contract_rows(left, right):
    return lax.dot_general(
        left, right, (((0,), (0,)), ((), ())), preferred_element_type=jnp.float32
    )


def contract_cols(left, right):
    return lax.dot_general(
        left, right, (((1,), (1,)), ((), ())), preferred_element_type=jnp.float32
    )


def renew(weight, moment, average, gradient, step_rate):
    moment_new = momentum_decay * moment + gradient
    weight_new = weight - step_rate * (gradient + momentum_decay * moment_new)
    average_new = average_decay * average + (1.0 - average_decay) * weight_new
    return (weight_new, moment_new, average_new, weight_new.astype(jnp.bfloat16))


def local(
    tokens,
    cotangent,
    segments,
    attn_in,
    attn_out,
    ffn_in,
    ffn_out,
    gains,
    attn_in_mom,
    attn_out_mom,
    ffn_in_mom,
    ffn_out_mom,
    gains_mom,
    attn_in_avg,
    attn_out_avg,
    ffn_in_avg,
    ffn_out_avg,
    gains_avg,
):
    micro_count = tokens.shape[0]
    local_rows = tokens.shape[1]
    all_rows = micro_count * local_rows
    model_width = tokens.shape[2]
    row_offset = lax.axis_index("seq") * local_rows
    row_index = row_offset + jnp.arange(local_rows, dtype=jnp.int32)
    key_index = jnp.arange(segments.shape[1], dtype=jnp.int32)
    query_width = HEADS * HEAD
    kv_width = KV_HEADS * HEAD
    share = HEADS // KV_HEADS
    ffn_width = ffn_out.shape[1]
    own_rows = ffn_in.shape[0]
    score_scale = HEAD ** (-0.5)
    own_segments = lax.dynamic_slice_in_dim(segments, row_offset, local_rows, 1)
    positions = jax.vmap(
        lambda seg_group, own_segment: place_tokens(seg_group, own_segment, row_index)
    )(segments, own_segments).reshape(all_rows)
    visible = (key_index[None, None, :] <= row_index[None, :, None]) & (
        (segments[:, None, :] == 0) | (segments[:, None, :] == own_segments[:, :, None])
    )
    inputs = tokens.astype(jnp.float32).reshape(all_rows, model_width)
    w_qkv, w_o, gain_low = (
        lax.all_gather(attn_in.astype(jnp.bfloat16), ("grp", "seq"), axis=0, tiled=True),
        lax.all_gather(attn_out.astype(jnp.bfloat16), ("grp", "seq"), axis=0, tiled=True),
        lax.all_gather(gains.astype(jnp.bfloat16), ("grp", "seq"), axis=1, tiled=True),
    )
    gain_vals = gain_low.astype(jnp.float32)
    normed_one, norm_one_back = jax.vjp(scaled, inputs, gain_vals[0])
    normed_one = normed_one.astype(jnp.bfloat16)
    projected = jnp.dot(normed_one, w_qkv, preferred_element_type=jnp.float32)
    query_rot, query_back = jax.vjp(
        lambda field: rotate(field, positions),
        projected[:, :query_width].reshape(all_rows, HEADS, HEAD),
    )
    key_rot, key_back = jax.vjp(
        lambda field: rotate(field, positions),
        projected[:, query_width : query_width + kv_width].reshape(all_rows, KV_HEADS, HEAD),
    )
    query_low = query_rot.astype(jnp.bfloat16).reshape(
        micro_count, local_rows, KV_HEADS, share, HEAD
    )
    key_low = key_rot.astype(jnp.bfloat16).reshape(micro_count, local_rows, kv_width)
    value_low = (
        projected[:, query_width + kv_width :]
        .astype(jnp.bfloat16)
        .reshape(micro_count, local_rows, kv_width)
    )
    group_key_rows, group_values = (
        lax.all_gather(key_low, "seq", axis=1, tiled=True),
        lax.all_gather(value_low, "seq", axis=1, tiled=True),
    )
    group_key_rows = group_key_rows.reshape(micro_count, -1, KV_HEADS, HEAD)
    group_values = group_values.reshape(micro_count, -1, KV_HEADS, HEAD)

    def probabilities(raw_scores):
        capped = jnp.where(
            visible[:, None, None], soft_cap * jnp.tanh(raw_scores / soft_cap), -1e30
        )
        return jax.nn.softmax(capped, axis=-1)

    raw_scores = (
        jnp.einsum(
            "mtgrd,mkgd->mgrtk", query_low, group_key_rows, preferred_element_type=jnp.float32
        )
        * score_scale
    )
    attention, attention_back = jax.vjp(probabilities, raw_scores)
    attention_low = attention.astype(jnp.bfloat16)
    mixed_heads = jnp.einsum(
        "mgrtk,mkgd->mtgrd", attention_low, group_values, preferred_element_type=jnp.float32
    )
    mixed_low = mixed_heads.reshape(all_rows, query_width).astype(jnp.bfloat16)
    branch = contract_cols(mixed_low, w_o)
    normed_two, norm_two_back = jax.vjp(scaled, branch, gain_vals[1])
    middle = inputs + normed_two
    normed_three, norm_three_back = jax.vjp(scaled, middle, gain_vals[2])
    normed_three = normed_three.astype(jnp.bfloat16)
    grad_top = cotangent.astype(jnp.float32).reshape(all_rows, model_width)
    seq_count = lax.axis_size("seq")
    grp_count = lax.axis_size("grp")
    slice_width = ffn_width // seq_count
    stacked = jnp.concatenate(
        [
            ffn_in.astype(jnp.bfloat16).reshape(own_rows, 2, seq_count, slice_width),
            ffn_out.astype(jnp.bfloat16).reshape(own_rows, 1, seq_count, slice_width),
        ],
        axis=1,
    )
    spread = jnp.broadcast_to(
        stacked[:, :, None], (own_rows, 3, grp_count, seq_count, slice_width)
    ).reshape(own_rows, 3, grp_count * seq_count, slice_width)
    w_cols = lax.all_to_all(
        spread, ("grp", "seq"), split_axis=2, concat_axis=0, tiled=True
    ).reshape(model_width, 3, slice_width)
    w_gu_cols = w_cols[:, :2].reshape(model_width, 2 * slice_width)
    w_d_cols = w_cols[:, 2]
    norm_rows = lax.all_gather(normed_three, "seq", axis=0, tiled=True)
    gate_up = jnp.dot(norm_rows, w_gu_cols, preferred_element_type=jnp.float32)
    hidden, glu_back = jax.vjp(glu_part, gate_up[:, :slice_width], gate_up[:, slice_width:])
    hidden = hidden.astype(jnp.bfloat16)
    ffn_branch = lax.psum_scatter(
        contract_cols(hidden, w_d_cols), "seq", scatter_dimension=0, tiled=True
    )
    normed_four, norm_four_back = jax.vjp(scaled, ffn_branch, gain_vals[3])
    layer_out = (
        (middle + normed_four).astype(jnp.bfloat16).reshape(micro_count, local_rows, model_width)
    )
    d_ffn, d_gain_four = norm_four_back(grad_top)
    d_ffn_all = lax.all_gather(d_ffn.astype(jnp.bfloat16), "seq", axis=0, tiled=True)
    d_hidden = jnp.dot(d_ffn_all, w_d_cols, preferred_element_type=jnp.float32)
    grad_d_cols = contract_rows(d_ffn_all, hidden)
    d_gate, d_upper = glu_back(d_hidden)
    d_gate_up = jnp.concatenate([d_gate, d_upper], axis=1).astype(jnp.bfloat16)
    grad_gu_cols = contract_rows(norm_rows, d_gate_up)
    d_normed_three = lax.psum_scatter(
        contract_cols(d_gate_up, w_gu_cols), "seq", scatter_dimension=0, tiled=True
    )
    local_grads = jnp.concatenate(
        [grad_gu_cols.reshape(model_width, 2, slice_width), grad_d_cols[:, None, :]], axis=1
    ).reshape(model_width, 3, 1, slice_width)
    returned = lax.all_to_all(
        local_grads.astype(jnp.bfloat16), ("grp", "seq"), split_axis=0, concat_axis=2, tiled=True
    ).astype(local_grads.dtype)
    grad_ffn = jnp.sum(
        returned.reshape(own_rows, 3, grp_count, seq_count, slice_width), axis=2
    ).reshape(own_rows, 3 * ffn_width)
    d_middle_norm, d_gain_three = norm_three_back(d_normed_three)
    d_middle = grad_top + d_middle_norm
    sum_gu = grad_ffn[:, : 2 * ffn_width]
    sum_down = grad_ffn[:, 2 * ffn_width :]
    d_branch, d_gain_two = norm_two_back(d_middle)
    d_branch_low = d_branch.astype(jnp.bfloat16)
    grad_out = contract_rows(d_branch_low, mixed_low)
    d_mixed = jnp.dot(d_branch_low, w_o, preferred_element_type=jnp.float32)
    d_mixed_low = d_mixed.astype(jnp.bfloat16).reshape(
        micro_count, local_rows, KV_HEADS, share, HEAD
    )
    d_attention = jnp.einsum(
        "mtgrd,mkgd->mgrtk", d_mixed_low, group_values, preferred_element_type=jnp.float32
    )
    (d_raw,) = attention_back(d_attention)
    d_raw_low = d_raw.astype(jnp.bfloat16)
    d_query = (
        jnp.einsum(
            "mgrtk,mkgd->mtgrd", d_raw_low, group_key_rows, preferred_element_type=jnp.float32
        )
        * score_scale
    )
    d_group_keys = (
        jnp.einsum("mgrtk,mtgrd->mkgd", d_raw_low, query_low, preferred_element_type=jnp.float32)
        * score_scale
    )
    d_group_values = jnp.einsum(
        "mgrtk,mtgrd->mkgd", attention_low, d_mixed_low, preferred_element_type=jnp.float32
    )
    d_keys, d_values = (
        lax.psum_scatter(
            d_group_keys.reshape(micro_count, -1, kv_width).astype(jnp.bfloat16),
            "seq",
            scatter_dimension=1,
            tiled=True,
        ).astype(jnp.float32),
        lax.psum_scatter(
            d_group_values.reshape(micro_count, -1, kv_width).astype(jnp.bfloat16),
            "seq",
            scatter_dimension=1,
            tiled=True,
        ).astype(jnp.float32),
    )
    (d_query_raw,) = query_back(d_query.reshape(all_rows, HEADS, HEAD))
    (d_key_raw,) = key_back(d_keys.reshape(all_rows, KV_HEADS, HEAD))
    d_projected = jnp.concatenate(
        [
            d_query_raw.reshape(all_rows, query_width),
            d_key_raw.reshape(all_rows, kv_width),
            d_values.reshape(all_rows, kv_width),
        ],
        axis=1,
    ).astype(jnp.bfloat16)
    grad_qkv = contract_rows(normed_one, d_projected)
    d_normed_one = contract_cols(d_projected, w_qkv)
    d_input_norm, d_gain_one = norm_one_back(d_normed_one)
    layer_grad = (d_middle + d_input_norm).reshape(micro_count, local_rows, model_width)
    d_gains = jnp.stack([d_gain_one, d_gain_two, d_gain_three, d_gain_four])
    part_qkv, part_out, part_gain = (
        lax.psum_scatter(
            grad_qkv.astype(jnp.bfloat16), "grp", scatter_dimension=0, tiled=True
        ).astype(jnp.float32),
        lax.psum_scatter(
            grad_out.astype(jnp.bfloat16), "grp", scatter_dimension=0, tiled=True
        ).astype(jnp.float32),
        lax.psum_scatter(
            d_gains.astype(jnp.bfloat16), "grp", scatter_dimension=1, tiled=True
        ).astype(jnp.float32),
    )
    sum_qkv, sum_out, sum_gain = (
        lax.psum_scatter(
            part_qkv.astype(jnp.bfloat16), "seq", scatter_dimension=0, tiled=True
        ).astype(jnp.float32),
        lax.psum_scatter(
            part_out.astype(jnp.bfloat16), "seq", scatter_dimension=0, tiled=True
        ).astype(jnp.float32),
        lax.psum_scatter(
            part_gain.astype(jnp.bfloat16), "seq", scatter_dimension=1, tiled=True
        ).astype(jnp.float32),
    )
    token_total = micro_count * local_rows * lax.axis_size(("grp", "seq"))
    rate_mat = weight_rate * token_total ** (-0.5)
    rate_gain = gain_rate * token_total ** (-0.5)
    qkv_new, qkv_mom, qkv_avg, qkv_copy = renew(
        attn_in, attn_in_mom, attn_in_avg, sum_qkv, rate_mat
    )
    out_new, out_mom, out_avg, out_copy = renew(
        attn_out, attn_out_mom, attn_out_avg, sum_out, rate_mat
    )
    gu_new, gu_mom, gu_avg, gu_copy = renew(ffn_in, ffn_in_mom, ffn_in_avg, sum_gu, rate_mat)
    down_new, down_mom, down_avg, down_copy = renew(
        ffn_out, ffn_out_mom, ffn_out_avg, sum_down, rate_mat
    )
    gain_new, gain_mom, gain_avg, gain_copy = renew(
        gains, gains_mom, gains_avg, sum_gain, rate_gain
    )
    return (
        layer_out,
        layer_grad,
        qkv_new,
        qkv_mom,
        qkv_avg,
        qkv_copy,
        out_new,
        out_mom,
        out_avg,
        out_copy,
        gu_new,
        gu_mom,
        gu_avg,
        gu_copy,
        down_new,
        down_mom,
        down_avg,
        down_copy,
        gain_new,
        gain_mom,
        gain_avg,
        gain_copy,
    )


def solution(mesh):
    placed = (
        P(None, ("grp", "seq"), None),
        P(None, ("grp", "seq"), None),
        P(None, "grp"),
        P(("grp", "seq"), None),
        P(("grp", "seq"), None),
        P(("grp", "seq"), None),
        P(("grp", "seq"), None),
        P(None, ("grp", "seq")),
        P(("grp", "seq"), None),
        P(("grp", "seq"), None),
        P(("grp", "seq"), None),
        P(("grp", "seq"), None),
        P(None, ("grp", "seq")),
        P(("grp", "seq"), None),
        P(("grp", "seq"), None),
        P(("grp", "seq"), None),
        P(("grp", "seq"), None),
        P(None, ("grp", "seq")),
    )
    return jax.shard_map(
        local,
        mesh=mesh,
        in_specs=placed,
        out_specs=(
            P(None, ("grp", "seq"), None),
            P(None, ("grp", "seq"), None),
            P(("grp", "seq"), None),
            P(("grp", "seq"), None),
            P(("grp", "seq"), None),
            P(("grp", "seq"), None),
            P(("grp", "seq"), None),
            P(("grp", "seq"), None),
            P(("grp", "seq"), None),
            P(("grp", "seq"), None),
            P(("grp", "seq"), None),
            P(("grp", "seq"), None),
            P(("grp", "seq"), None),
            P(("grp", "seq"), None),
            P(("grp", "seq"), None),
            P(("grp", "seq"), None),
            P(("grp", "seq"), None),
            P(("grp", "seq"), None),
            P(None, ("grp", "seq")),
            P(None, ("grp", "seq")),
            P(None, ("grp", "seq")),
            P(None, ("grp", "seq")),
        ),
        check_vma=False,
    )
```

profile of v0, /device:TPU:0, one launch (start us, length us, event | category | flops | bytes accessed | tf_op | source)
XLA Modules:
  0.0 2390.8 jit_solution(18045130663046549413)
XLA Ops:
  12.9 43.6 %all-gather = bf16[32,72,4]{1,2,0:T(4,128)(2,1)S(1)} all-gather(bf16[1,72,4]{1,2,0:T(4,128)(2,1)S(1)} %convert_bitcast_fusion), channel_id=1, replica_groups=mesh['grp'=4,'seq'=8] {'grp','seq'}, dimensions={0}, use_global_device_ids=true | all-gather | bytes 19008 | tf_op jit(solution)/shard_map/all_gather | solution.py:116
  60.4 78.5 %all-gather.8.cloned.1.call-done = bf16[2304,4096]{1,0:T(8,128)(2,1)} async-done(((bf16[72,4096]{1,0:T(8,128)(2,1)}), bf16[2304,4096]{1,0:T(8,128)(2,1)}) %all-gather.8.cloned.1.call-update) | async-done | bytes 18874384 | tf_op jit(solution)/shard_map/all_gather | solution.py:114
  177.3 67.2 %all-gather.12.cloned.1.call-done = bf16[2,1152,1024]{2,1,0:T(8,128)(2,1)} async-done(((bf16[2,144,1024]{2,1,0:T(8,128)(2,1)}), bf16[2,1152,1024]{2,1,0:T(8,128)(2,1)}) %all-gather.12.cloned.1.call-update) | async-done | bytes 4718608 | tf_op jit(solution)/shard_map/all_gather | solution.py:140
  251.4 128.8 %all-gather.10.cloned.1.call-done = bf16[2,1152,1024]{2,0,1:T(2,128)(2,1)} async-done(((bf16[2,144,1024]{2,0,1:T(2,128)(2,1)}), bf16[2,1152,1024]{2,0,1:T(2,128)(2,1)}) %all-gather.10.cloned.1.call-update) | async-done | bytes 4718608 | tf_op jit(solution)/shard_map/all_gather | solution.py:141
  420.9 102.4 %all-gather.14.cloned.1.call-done = bf16[2304,2048]{1,0:T(8,128)(2,1)} async-done(((bf16[72,2048]{1,0:T(8,128)(2,1)}), bf16[2304,2048]{1,0:T(8,128)(2,1)}) %all-gather.14.cloned.1.call-update) | async-done | bytes 9437200 | tf_op jit(solution)/shard_map/all_gather | solution.py:115
  532.7 43.4 %all-to-all-done = bf16[72,3,32,1152]{3,0,1,2:T(8,128)(2,1)} async-done(((bf16[72,3,32,1152]{3,0,1,2:T(8,128)(2,1)}), bf16[72,3,32,1152]{3,0,1,2:T(8,128)(2,1)}, u32[]{:S(2)}, u32[]{:S(2)}) %all-to-all-start) | async-done | bytes 15925280 | tf_op jit(solution)/shard_map/all_to_all | solution.py:183
  595.0 15.6 copy.184
  610.6 30.3 %fusion.73 = f32[2304,2304]{0,1:T(8,128)S(1)} fusion(bf16[2304,2304]{1,0:T(8,128)(2,1)} %all-gather.16.cloned.1.call-done, bf16[2304,2304]{0,1:T(8,128)(2,1)} %bitcast.174), kind=kOutput, calls=%fused_computation.175 | convolution fusion | flops 24461180928 | bytes 42467328 | tf_op jit(solution)/shard_map/dot_general | solution.py:189
  649.6 20.6 fusion.25
  670.4 133.0 %reduce-scatter.12.cloned.1.call-done = f32[288,2304]{1,0:T(8,128)} async-done(((f32[2304,2304]{1,0:T(8,128)}), f32[288,2304]{1,0:T(8,128)}) %reduce-scatter.12.cloned.1.call-update) | async-done | bytes 2654224 | tf_op jit(solution)/shard_map/reduce_scatter | solution.py:192
  812.1 63.9 %all-gather.18.cloned.1.call-done = bf16[2304,2304]{1,0:T(8,128)(2,1)} async-done(((bf16[288,2304]{1,0:T(8,128)(2,1)}), bf16[2304,2304]{1,0:T(8,128)(2,1)}) %all-gather.18.cloned.1.call-update) | async-done | bytes 10616848 | tf_op jit(solution)/shard_map/all_gather | solution.py:200
  876.0 28.8 %fusion.7 = (bf16[2304,1152]{0,1:T(8,128)(2,1)}, bf16[2304,1152]{0,1:T(8,128)(2,1)}) fusion(f32[2304,2304]{0,1:T(8,128)} %copy-done.8, bf16[2304,2304]{1,0:T(8,128)(2,1)} %all-gather.18.cloned.1.call-done, bf16[2304,3,1152]{2,0,1:T(8,128)(2,1)} %bitcast.162), kind=kOutput, calls=%fused_computation.14 | convolution fusion | flops 12294291456 | bytes 47775744 | tf_op jit(solution)/shard_map/dot_general | solution.py:201
  904.7 32.6 %fusion.19 = f32[2304,2304]{1,0:T(8,128)} fusion(bf16[2304,2304]{0,1:T(8,128)(2,1)} %bitcast.175, bf16[2304,1152]{0,1:T(8,128)(2,1)} %get-tuple-element.50, bf16[2304,1152]{0,1:T(8,128)(2,1)} %get-tuple-element.49), kind=kOutput, calls=%fused_computation.39 | convolution fusion | flops 24482414592 | bytes 42467328 | tf_op jit(solution)/shard_map/dot_general | solution.py:60
  938.1 136.6 %reduce-scatter.14.cloned.1.call-done = f32[288,2304]{1,0:T(8,128)} async-done(((f32[2304,2304]{1,0:T(8,128)}), f32[288,2304]{1,0:T(8,128)}) %reduce-scatter.14.cloned.1.call-update) | async-done | bytes 2654224 | tf_op jit(solution)/shard_map/reduce_scatter | solution.py:206
  1154.2 33.8 %convolution_convert_fusion.1 = bf16[2304,2304]{0,1:T(8,128)(2,1)} fusion(bf16[2304,2304]{1,0:T(8,128)(2,1)} %all-gather.16.cloned.1.call-done, bf16[2304,1152]{0,1:T(8,128)(2,1)} %get-tuple-element.50, bf16[2304,1152]{0,1:T(8,128)(2,1)} %get-tuple-element.49), kind=kOutput, calls=%fused_computation.3 | convolution fusion | flops 24487723008 | bytes 31850496 | tf_op jit(solution)/shard_map/dot_general | solution.py:54
  1188.0 29.7 %copy.194 = bf16[2304,2,1,1152]{3,1,2,0:T(2,128)(2,1)} copy(bf16[2304,2,1,1152]{0,3,1,2:T(8,128)(2,1)} %bitcast.176) | data formatting | bytes 21233664 | tf_op jit(solution)/shard_map/concatenate | solution.py:209
  1217.6 18.1 fusion.16
  1235.7 35.5 %copy.195 = bf16[2304,1,1,1152]{3,1,2,0:T(2,128)(2,1)} copy(bf16[2304,1,1,1152]{3,0,2,1:T(8,128)(2,1)S(1)} %fusion.16) | data formatting | bytes 10616832 | tf_op jit(solution)/shard_map/concatenate | solution.py:209
  1282.4 14.5 convolution_convert_fusion
  1296.9 25.2 %pad_maximum_fusion = bf16[2304,3,1,1152]{3,1,2,0:T(4,128)(2,1)} fusion(bf16[2304,1,1,1152]{3,1,2,0:T(2,128)(2,1)} %copy.195, bf16[2304,2,1,1152]{3,1,2,0:T(2,128)(2,1)} %copy.194), kind=kLoop, calls=%fused_computation.2 | loop fusion | flops 31850496 | bytes 31850496 | tf_op jit(solution)/shard_map/concatenate | solution.py:209
  1327.4 871.8 %all-to-all-done.1 = bf16[2304,3,1,1152]{3,1,2,0:T(4,128)(2,1)} async-done(((bf16[2304,3,1,1152]{3,1,2,0:T(4,128)(2,1)}), bf16[2304,3,1,1152]{3,1,2,0:T(4,128)(2,1)}, u32[]{:S(2)}, u32[]{:S(2)}) %all-to-all-start.1) | async-done | bytes 15925280 | tf_op jit(solution)/shard_map/all_to_all | solution.py:212
  2222.1 15.3 reduce_sum.169
  2299.0 23.3 reduce-scatter.24.cloned.1.call-done
  2325.3 54.2 %reduce-scatter.20.cloned.1.call-done = bf16[72,4096]{1,0:T(8,128)(2,1)} async-done(((bf16[576,4096]{1,0:T(8,128)(2,1)}), bf16[72,4096]{1,0:T(8,128)(2,1)}) %reduce-scatter.20.cloned.1.call-update) | async-done | bytes 589840 | tf_op jit(solution)/shard_map/reduce_scatter | solution.py:288
  (315 shorter events, 327.2 us)
Async XLA Ops:
  7.2 131.7 %all-gather.8.cloned.1.call-start = ((), (), s32[]{:S(2)}) async-start(), calls=%async_computation.10 | async-start | bytes 19464192 | tf_op jit(solution)/shard_map/all_gather | solution.py:114
  9.5 235.0 %all-gather.12.cloned.1.call-start = ((), (), s32[]{:S(2)}) async-start(), calls=%async_computation.12 | async-start | bytes 5308416 | tf_op jit(solution)/shard_map/all_gather | solution.py:140
  58.4 471.7 %copy-start.43 = (f32[2304]{0:T(1024)}, f32[2304]{0:T(1024)S(1)}, u32[]{:S(2)}) copy-start(f32[2304]{0:T(1024)S(1)} %get-tuple-element.32) | copy-start | bytes 27652
  58.4 472.9 %copy-start.45 = (f32[2304]{0:T(1024)}, f32[2304]{0:T(1024)S(1)}, u32[]{:S(2)}) copy-start(f32[2304]{0:T(1024)S(1)} %get-tuple-element.31) | copy-start | bytes 27652
  153.6 226.6 %all-gather.10.cloned.1.call-start = ((), (), s32[]{:S(2)}) async-start(), calls=%async_computation.11 | async-start | bytes 5308416 | tf_op jit(solution)/shard_map/all_gather | solution.py:141
  156.4 366.8 %all-gather.14.cloned.1.call-start = ((), (), s32[]{:S(2)}) async-start(), calls=%async_computation.13 | async-start | bytes 9732096 | tf_op jit(solution)/shard_map/all_gather | solution.py:115
  169.1 407.1 %all-to-all-start = ((bf16[72,3,32,1152]{3,0,1,2:T(8,128)(2,1)}), bf16[72,3,32,1152]{3,0,1,2:T(8,128)(2,1)}, u32[]{:S(2)}, u32[]{:S(2)}) async-start(bf16[72,3,32,1152]{3,0,1,2:T(8,128)(2,1)} %bitcast.158), calls=%async_computation | async-start | bytes 31850496 | tf_op jit(solution)/shard_map/all_to_all | solution.py:183
  173.1 437.5 %all-gather.16.cloned.1.call-start = ((), (), s32[]{:S(2)}) async-start(), calls=%async_computation.14 | async-start | bytes 11943936 | tf_op jit(solution)/shard_map/all_gather | solution.py:188
  173.7 227.2 %copy-start.34 = (pred[2,144,1152]{2,1,0:T(8,128)(4,1)}, pred[2,144,1152]{2,1,0:T(8,128)(4,1)S(1)}, u32[]{:S(2)}) copy-start(pred[2,144,1152]{2,1,0:T(8,128)(4,1)S(1)} %or_and_fusion) | copy-start | bytes 995332
  177.3 215.6 %copy-start.27 = (bf16[288,8,128]{2,0,1:T(8,128)(2,1)}, bf16[288,8,128]{2,0,1:T(8,128)(2,1)S(1)}, u32[]{:S(2)}) copy-start(bf16[288,8,128]{2,0,1:T(8,128)(2,1)S(1)} %get-tuple-element.55) | copy-start | bytes 1769476
  177.3 215.5 %copy-start.29 = (bf16[288,8,128]{2,0,1:T(8,128)(2,1)}, bf16[288,8,128]{2,0,1:T(8,128)(2,1)S(1)}, u32[]{:S(2)}) copy-start(bf16[288,8,128]{2,0,1:T(8,128)(2,1)S(1)} %get-tuple-element.56) | copy-start | bytes 1769476
  532.7 270.7 %reduce-scatter.12.cloned.1.call-start = ((), (), s32[]{:S(2)}) async-start(), calls=%async_computation.15 | async-start | bytes 23887872 | tf_op jit(solution)/shard_map/reduce_scatter | solution.py:192
  670.1 205.8 %all-gather.18.cloned.1.call-start = ((), (), s32[]{:S(2)}) async-start(), calls=%async_computation.16 | async-start | bytes 11943936 | tf_op jit(solution)/shard_map/all_gather | solution.py:200
  812.0 262.7 %reduce-scatter.14.cloned.1.call-start = ((), (), s32[]{:S(2)}) async-start(), calls=%async_computation.17 | async-start | bytes 23887872 | tf_op jit(solution)/shard_map/reduce_scatter | solution.py:206
  937.4 137.4 %copy-start.56 = (f32[288]{0:T(512)S(1)}, f32[288]{0:T(512)}, u32[]{:S(2)}) copy-start(f32[288]{0:T(512)} %copy-done.55) | copy-start | bytes 3460
  937.4 340.8 %all-reduce.8.cloned.1.call-start = ((), (), s32[]{:S(2)}) async-start(), calls=%async_computation.24 | async-start | bytes 9437184
  938.1 139.8 %copy-start.63 = (f32[288]{0:T(512)S(1)}, f32[288]{0:T(512)}, u32[]{:S(2)}) copy-start(f32[288]{0:T(512)} %copy-done.62) | copy-start | bytes 3460
  1129.5 151.6 %reduce-scatter.16.cloned.1.call-start = ((), (), s32[]{:S(2)}) async-start(), calls=%async_computation.18 | async-start | bytes 5308416 | tf_op jit(solution)/shard_map/reduce_scatter | solution.py:254
  1143.4 1120.9 %reduce-scatter.22.cloned.1.call-start = ((), (), s32[]{:S(2)}) async-start(), calls=%async_computation.21 | async-start | bytes 11796480 | tf_op jit(solution)/shard_map/reduce_scatter | solution.py:280
  1152.3 1122.4 %reduce-scatter.18.cloned.1.call-start = ((), (), s32[]{:S(2)}) async-start(), calls=%async_computation.19 | async-start | bytes 23592960 | tf_op jit(solution)/shard_map/reduce_scatter | solution.py:277
  1322.1 877.2 %all-to-all-start.1 = ((bf16[2304,3,1,1152]{3,1,2,0:T(4,128)(2,1)}), bf16[2304,3,1,1152]{3,1,2,0:T(4,128)(2,1)}, u32[]{:S(2)}, u32[]{:S(2)}) async-start(bf16[2304,3,1,1152]{3,1,2,0:T(4,128)(2,1)} %pad_maximum_fusion), calls=%async_computation.8 | async-start | bytes 42467328 | tf_op jit(solution)/shard_map/all_to_all | solution.py:212
  1326.7 957.7 %reduce-scatter.26.cloned.1.call-start = ((), (), s32[]{:S(2)}) async-start(), calls=%async_computation.23 | async-start | bytes 737280
  2259.8 62.5 %reduce-scatter.24.cloned.1.call-start = ((), (), s32[]{:S(2)}) async-start(), calls=%async_computation.22 | async-start | bytes 2654208 | tf_op jit(solution)/shard_map/reduce_scatter | solution.py:291
  2264.3 115.2 %reduce-scatter.20.cloned.1.call-start = ((), (), s32[]{:S(2)}) async-start(), calls=%async_computation.20 | async-start | bytes 5308416 | tf_op jit(solution)/shard_map/reduce_scatter | solution.py:288
  (73 other events, 1653.2 us)
Sparse Core Ops, SparseCore 0:
  11.5 127.3 all-gather.7
  153.7 90.7 all-gather.11
  247.0 133.2 all-gather.9
  383.6 139.6 all-gather.13
  532.8 71.4 all-gather.15
  670.3 133.0 reduce-scatter.11
  812.1 63.8 all-gather.17
  937.5 137.1 reduce-scatter.13
  1129.6 86.7 all-reduce.7
  1220.7 53.9 reduce-scatter.15
  1277.1 271.4 reduce-scatter.21
  1550.8 626.8 reduce-scatter.17
  2259.9 17.9 reduce-scatter.25
  2281.4 40.8 reduce-scatter.23
  2325.6 53.8 reduce-scatter.19
where the time goes:
time: 2400 us; the launch traced here: 2390 us
  waiting for transfers between devices  1700 us (71%)
  matrix products  257 us (11%)
  local copies, waits for them, and re-layouts  201 us (8%)
  other arithmetic  147 us (6%)
  blocking collectives  55.8 us (2%)
    all_to_all x1, waiting for transfers between devices, local(): lax.all_to_all(local_grads.astype(jnp.bfloat16), ('grp', 'seq'), split_ax...  872 us
    reduce_scatter x1, waiting for transfers between devices, local(): lax.psum_scatter(contract_cols(d_gate_up, w_gu_cols), 'seq', scatter_dime...  137 us
    reduce_scatter x1, waiting for transfers between devices, local(): lax.psum_scatter(contract_cols(hidden, w_d_cols), 'seq', scatter_dimensio...  133 us
    all_gather x1, waiting for transfers between devices, local(): lax.all_gather(value_low, 'seq', axis=1, tiled=True)  129 us
    all_gather x1, waiting for transfers between devices, local(): lax.all_gather(attn_out.astype(jnp.bfloat16), ('grp', 'seq'), axis=0, til...  102 us
    all_gather x1, waiting for transfers between devices, local(): lax.all_gather(attn_in.astype(jnp.bfloat16), ('grp', 'seq'), axis=0, tile...  78.5 us
    dot_general x4, matrix products, contract_rows(): lax.dot_general(left, right, (((0,), (0,)), ((), ())), preferred_element_...  74 us
    dot_general x4, matrix products, contract_cols(): lax.dot_general(left, right, (((1,), (1,)), ((), ())), preferred_element_...  71 us
  transfers between devices with their start and end apart: 17, of which 11 were waited for; matrix products, arithmetic and copies ran while one was open for 16% of the time, Pallas kernels for 0%

commit v1 on v0

--- a/solution.py
+++ b/solution.py
@@ -69,7 +69,7 @@
     return (weight_new, moment_new, average_new, weight_new.astype(jnp.bfloat16))
 
 
-def local(
+def by_rows(
     tokens,
     cotangent,
     segments,
@@ -337,6 +337,362 @@
     )
 
 
+def permute(field, offset):
+    count = lax.axis_size("seq")
+    return lax.ppermute(field, "seq", [(i, i ^ offset) for i in range(count)])
+
+
+def offset_bits():
+    return [1 << bit for bit in range(1, lax.axis_size("seq").bit_length() - 1)]
+
+
+def gather_pieces(field):
+    half = field.shape[0] // 2
+    bits = offset_bits()
+    sides = [({0: field[:half]}, bits), ({0: field[half:]}, bits[::-1])]
+    for step in range(len(bits)):
+        for have, order in sides:
+            bit = order[step]
+            have.update({at | bit: permute(block, bit) for at, block in list(have.items())})
+    for have, _ in sides:
+        have.update({at | 1: permute(block, 1) for at, block in list(have.items())})
+    count = lax.axis_size("seq")
+    return jnp.concatenate([have[at] for at in range(count) for have, _ in sides], axis=0)
+
+
+def add_low(left, right):
+    return (left.astype(jnp.float32) + right.astype(jnp.float32)).astype(jnp.bfloat16)
+
+
+def sum_pieces(field):
+    count = lax.axis_size("seq")
+    rows = field.shape[0] // count
+    half = rows // 2
+    bits = offset_bits()
+    blocks = [field[at * rows : (at + 1) * rows] for at in range(count)]
+    pairs = {
+        at: add_low(blocks[at], permute(blocks[at | 1], 1)) for at in range(0, count, 2)
+    }
+    sides = [
+        ({at: block[:half] for at, block in pairs.items()}, bits[::-1]),
+        ({at: block[half:] for at, block in pairs.items()}, bits),
+    ]
+    for step in range(len(bits)):
+        last = step == len(bits) - 1
+        sides = [
+            (
+                {
+                    at: (jnp.add if last else add_low)(
+                        *(
+                            part.astype(jnp.float32)
+                            for part in (block, permute(have[at | order[step]], order[step]))
+                        )
+                    )
+                    for at, block in have.items()
+                    if not at & order[step]
+                },
+                order,
+            )
+            for have, order in sides
+        ]
+    return jnp.concatenate([have[0] for have, _ in sides], axis=0)
+
+
+def swap_order(field):
+    count = field.shape[0]
+    bits = count.bit_length() - 1
+    index = lax.axis_index("seq")
+    split = field.reshape((2,) * bits + field.shape[1:])
+    for bit in range(bits):
+        axis = bits - 1 - bit
+        split = jnp.where((index >> bit) & 1 == 1, jnp.flip(split, axis), split)
+    return split.reshape(field.shape)
+
+
+def spread_columns(field):
+    rows, _, columns = field.shape
+    moved = lax.all_to_all(
+        field.astype(jnp.bfloat16).transpose(1, 0, 2), "seq", split_axis=0, concat_axis=0, tiled=True
+    )
+    return moved.reshape(-1, columns)
+
+
+def gather_planes(field):
+    return lax.all_gather(field, "grp", axis=0, tiled=True)
+
+
+def sum_planes(field):
+    part = lax.psum_scatter(
+        field.astype(jnp.bfloat16), "grp", scatter_dimension=0, tiled=True
+    )
+    count = lax.axis_size("seq")
+    moved = lax.all_to_all(
+        part.reshape(count, -1, field.shape[1]), "seq", split_axis=0, concat_axis=0, tiled=True
+    )
+    return moved.transpose(1, 0, 2).astype(jnp.float32)
+
+
+def by_heads(
+    tokens,
+    cotangent,
+    segments,
+    attn_in,
+    attn_out,
+    ffn_in,
+    ffn_out,
+    gains,
+    attn_in_mom,
+    attn_out_mom,
+    ffn_in_mom,
+    ffn_out_mom,
+    gains_mom,
+    attn_in_avg,
+    attn_out_avg,
+    ffn_in_avg,
+    ffn_out_avg,
+    gains_avg,
+):
+    micro_count, local_rows, model_width = tokens.shape
+    all_rows = micro_count * local_rows
+    seq_count = lax.axis_size("seq")
+    grp_count = lax.axis_size("grp")
+    device_count = seq_count * grp_count
+    group_rows = segments.shape[1]
+    own_rows = ffn_in.shape[0]
+    ffn_width = ffn_out.shape[1]
+    slice_width = ffn_width // seq_count
+    chunks = 3
+    chunk_width = slice_width // chunks
+    score_scale = HEAD ** (-0.5)
+    core = lax.axis_index("seq") % 2
+    key_core = core == 0
+
+    qkv_cols = jnp.concatenate(
+        [
+            attn_in[:, : HEADS * HEAD].reshape(own_rows, HEADS, HEAD),
+            attn_in[:, HEADS * HEAD :]
+            .reshape(own_rows, 2, KV_HEADS, HEAD)
+            .transpose(0, 2, 1, 3)
+            .reshape(own_rows, HEADS, HEAD),
+        ],
+        axis=2,
+    )
+    w_qkv = gather_planes(spread_columns(qkv_cols))
+    all_gains = lax.all_to_all(
+        jnp.broadcast_to(gains.astype(jnp.bfloat16)[None], (device_count,) + gains.shape),
+        ("grp", "seq"),
+        split_axis=0,
+        concat_axis=0,
+        tiled=True,
+    )
+    gain_vals = all_gains.transpose(1, 0, 2).reshape(4, model_width).astype(jnp.float32)
+    token_pieces = gather_pieces(tokens.reshape(all_rows, model_width))
+    w_o = gather_planes(spread_columns(attn_out.reshape(own_rows, HEADS, HEAD)))
+    gu_split = ffn_in.reshape(own_rows, 2, seq_count, chunks, chunk_width)
+    w_gu_chunks = [
+        gather_planes(
+            spread_columns(
+                gu_split[:, :, :, at].transpose(0, 2, 1, 3).reshape(own_rows, seq_count, 2 * chunk_width)
+            )
+        )
+        for at in range(chunks)
+    ]
+    w_d = gather_planes(spread_columns(ffn_out.reshape(own_rows, seq_count, slice_width)))
+
+    row_index = jnp.arange(group_rows, dtype=jnp.int32)
+    positions = jax.vmap(lambda seg: place_tokens(seg, seg, row_index))(segments)
+    visible = (row_index[None, None, :] <= row_index[None, :, None]) & (
+        (segments[:, None, :] == 0) | (segments[:, None, :] == segments[:, :, None])
+    )
+    flat_positions = positions.reshape(-1)
+    kv_positions = jnp.where(key_core, flat_positions, 0)
+
+    def to_groups(field):
+        blocks = swap_order(field.reshape(seq_count, all_rows, -1))
+        return (
+            blocks.reshape(seq_count, micro_count, local_rows, -1)
+            .transpose(1, 0, 2, 3)
+            .reshape(micro_count * group_rows, -1)
+        )
+
+    def from_groups(field):
+        blocks = (
+            field.reshape(micro_count, seq_count, local_rows, -1)
+            .transpose(1, 0, 2, 3)
+            .reshape(seq_count, all_rows, -1)
+        )
+        return swap_order(blocks).reshape(seq_count * all_rows, -1)
+
+    normed_one = scaled(token_pieces.astype(jnp.float32), gain_vals[0]).astype(jnp.bfloat16)
+    projected = to_groups(jnp.dot(normed_one, w_qkv, preferred_element_type=jnp.float32))
+    query_rot, query_back = jax.vjp(
+        lambda field: rotate(field[:, None], flat_positions)[:, 0], projected[:, :HEAD]
+    )
+    kv_rot, kv_back = jax.vjp(
+        lambda field: rotate(field[:, None], kv_positions)[:, 0], projected[:, HEAD:]
+    )
+    queries = query_rot.astype(jnp.bfloat16).reshape(micro_count, group_rows, HEAD)
+    kv_own = kv_rot.astype(jnp.bfloat16)
+    kv_other = permute(kv_own, 1)
+    keys = jnp.where(key_core, kv_own, kv_other).reshape(micro_count, group_rows, HEAD)
+    values = jnp.where(key_core, kv_other, kv_own).reshape(micro_count, group_rows, HEAD)
+
+    def probabilities(raw_scores):
+        capped = jnp.where(visible, soft_cap * jnp.tanh(raw_scores / soft_cap), -1e30)
+        return jax.nn.softmax(capped, axis=-1)
+
+    raw_scores = (
+        jnp.einsum("mtd,mkd->mtk", queries, keys, preferred_element_type=jnp.float32) * score_scale
+    )
+    attention, attention_back = jax.vjp(probabilities, raw_scores)
+    attention_low = attention.astype(jnp.bfloat16)
+    mixed = jnp.einsum("mtk,mkd->mtd", attention_low, values, preferred_element_type=jnp.float32)
+    mixed_pieces = from_groups(mixed.astype(jnp.bfloat16))
+    branch = sum_pieces(contract_cols(mixed_pieces, w_o).astype(jnp.bfloat16))
+
+    inputs = tokens.astype(jnp.float32).reshape(all_rows, model_width)
+    grad_top = cotangent.astype(jnp.float32).reshape(all_rows, model_width)
+    normed_two, norm_two_back = jax.vjp(scaled, branch, gain_vals[1])
+    middle = inputs + normed_two
+    normed_three, norm_three_back = jax.vjp(scaled, middle, gain_vals[2])
+
+    norm_rows = gather_pieces(normed_three.astype(jnp.bfloat16))
+    gate_ups = [
+        jnp.dot(norm_rows, w_gu, preferred_element_type=jnp.float32) for w_gu in w_gu_chunks
+    ]
+    hiddens, glu_backs = zip(
+        *(jax.vjp(glu_part, part[:, :chunk_width], part[:, chunk_width:]) for part in gate_ups)
+    )
+    hidden = jnp.concatenate([part.astype(jnp.bfloat16) for part in hiddens], axis=1)
+    ffn_branch = sum_pieces(contract_cols(hidden, w_d).astype(jnp.bfloat16))
+    normed_four, norm_four_back = jax.vjp(scaled, ffn_branch, gain_vals[3])
+    layer_out = (middle + normed_four).astype(jnp.bfloat16).reshape(tokens.shape)
+    d_ffn, d_gain_four = norm_four_back(grad_top)
+    d_ffn_rows = gather_pieces(d_ffn.astype(jnp.bfloat16))
+    grad_d = sum_planes(contract_rows(d_ffn_rows, hidden))
+    d_hidden = jnp.dot(d_ffn_rows, w_d, preferred_element_type=jnp.float32)
+    d_gate_ups = []
+    for at in range(chunks):
+        d_gate, d_upper = glu_backs[at](d_hidden[:, at * chunk_width : (at + 1) * chunk_width])
+        d_gate_ups.append(jnp.concatenate([d_gate, d_upper], axis=1).astype(jnp.bfloat16))
+    d_normed_three = sum_pieces(
+        contract_cols(
+            jnp.concatenate(d_gate_ups, axis=1), jnp.concatenate(w_gu_chunks, axis=1)
+        ).astype(jnp.bfloat16)
+    )
+    grad_gus = [sum_planes(contract_rows(norm_rows, part)) for part in d_gate_ups]
+    d_middle_norm, d_gain_three = norm_three_back(d_normed_three)
+    d_middle = grad_top + d_middle_norm
+    d_branch, d_gain_two = norm_two_back(d_middle)
+
+    d_branch_rows = gather_pieces(d_branch.astype(jnp.bfloat16))
+    d_mixed = to_groups(
+        jnp.dot(d_branch_rows, w_o, preferred_element_type=jnp.float32).astype(jnp.bfloat16)
+    ).reshape(micro_count, group_rows, HEAD)
+    d_attention = jnp.einsum("mtd,mkd->mtk", d_mixed, values, preferred_element_type=jnp.float32)
+    (d_raw,) = attention_back(d_attention)
+    d_raw_low = d_raw.astype(jnp.bfloat16)
+    d_query = (
+        jnp.einsum("mtk,mkd->mtd", d_raw_low, keys, preferred_element_type=jnp.float32) * score_scale
+    ).reshape(-1, HEAD)
+    d_keys = (
+        jnp.einsum("mtk,mtd->mkd", d_raw_low, queries, preferred_element_type=jnp.float32)
+        * score_scale
+    ).reshape(-1, HEAD)
+    d_values = jnp.einsum(
+        "mtk,mtd->mkd", attention_low, d_mixed, preferred_element_type=jnp.float32
+    ).reshape(-1, HEAD)
+    d_kv = jnp.where(key_core, d_keys, d_values) + permute(
+        jnp.where(key_core, d_values, d_keys).astype(jnp.bfloat16), 1
+    ).astype(jnp.float32)
+    (d_query_raw,) = query_back(d_query)
+    (d_kv_raw,) = kv_back(d_kv)
+    d_projected = from_groups(
+        jnp.concatenate([d_query_raw, d_kv_raw], axis=1).astype(jnp.bfloat16)
+    )
+    d_normed_one = sum_pieces(contract_cols(d_projected, w_qkv).astype(jnp.bfloat16))
+    grad_attn = sum_planes(
+        jnp.concatenate(
+            [contract_rows(normed_one, d_projected), contract_rows(d_branch_rows, mixed_pieces)],
+            axis=1,
+        )
+    )
+    _, norm_one_back = jax.vjp(scaled, inputs, gain_vals[0])
+    d_input_norm, d_gain_one = norm_one_back(d_normed_one)
+    layer_grad = (d_middle + d_input_norm).reshape(tokens.shape)
+    d_gains = jnp.stack([d_gain_one, d_gain_two, d_gain_three, d_gain_four])
+    sum_gain = jnp.sum(
+        lax.all_to_all(
+            d_gains.reshape(4, device_count, -1).transpose(1, 0, 2),
+            ("grp", "seq"),
+            split_axis=0,
+            concat_axis=0,
+            tiled=True,
+        ),
+        axis=0,
+    )
+
+    sum_qkv = jnp.concatenate(
+        [
+            grad_attn[:, :, :HEAD].reshape(own_rows, HEADS * HEAD),
+            grad_attn[:, :, HEAD : 2 * HEAD]
+            .reshape(own_rows, KV_HEADS, 2, HEAD)
+            .transpose(0, 2, 1, 3)
+            .reshape(own_rows, 2 * KV_HEADS * HEAD),
+        ],
+        axis=1,
+    )
+    sum_out = grad_attn[:, :, 2 * HEAD :].reshape(own_rows, HEADS * HEAD)
+    sum_gu = (
+        jnp.stack(
+            [part.reshape(own_rows, seq_count, 2, chunk_width) for part in grad_gus], axis=3
+        )
+        .transpose(0, 2, 1, 3, 4)
+        .reshape(own_rows, 2 * ffn_width)
+    )
+    sum_down = grad_d.reshape(own_rows, ffn_width)
+    token_total = micro_count * local_rows * device_count
+    rate_mat = weight_rate * token_total ** (-0.5)
+    rate_gain = gain_rate * token_total ** (-0.5)
+    qkv_new, qkv_mom, qkv_avg, qkv_copy = renew(
+        attn_in, attn_in_mom, attn_in_avg, sum_qkv, rate_mat
+    )
+    out_new, out_mom, out_avg, out_copy = renew(
+        attn_out, attn_out_mom, attn_out_avg, sum_out, rate_mat
+    )
+    gu_new, gu_mom, gu_avg, gu_copy = renew(ffn_in, ffn_in_mom, ffn_in_avg, sum_gu, rate_mat)
+    down_new, down_mom, down_avg, down_copy = renew(
+        ffn_out, ffn_out_mom, ffn_out_avg, sum_down, rate_mat
+    )
+    gain_new, gain_mom, gain_avg, gain_copy = renew(
+        gains, gains_mom, gains_avg, sum_gain, rate_gain
+    )
+    return (
+        layer_out,
+        layer_grad,
+        qkv_new,
+        qkv_mom,
+        qkv_avg,
+        qkv_copy,
+        out_new,
+        out_mom,
+        out_avg,
+        out_copy,
+        gu_new,
+        gu_mom,
+        gu_avg,
+        gu_copy,
+        down_new,
+        down_mom,
+        down_avg,
+        down_copy,
+        gain_new,
+        gain_mom,
+        gain_avg,
+        gain_copy,
+    )
+
+
 def solution(mesh):
     placed = (
         P(None, ("grp", "seq"), None),
@@ -358,8 +714,9 @@
         P(("grp", "seq"), None),
         P(None, ("grp", "seq")),
     )
+    heads_fit = mesh.shape["seq"] == HEADS
     return jax.shard_map(
-        local,
+        by_heads if heads_fit else by_rows,
         mesh=mesh,
         in_specs=placed,
         out_specs=(

time: 2400 us -> 1130 us (0.47)
  waiting for transfers between devices: 1700 us -> 350 us
  starting transfers between devices: 9.98 us -> 118 us
  blocking collectives: 55.8 us -> 0 us
  other arithmetic: 147 us -> 200 us
    all_to_all x2 -> x13, waiting for transfers between devices: 915 us -> 51.1 us  [the longest x5 30.5 us: sum_planes(): lax.all_to_all(part.reshape(count, -1, field.shape[1]), 'seq', split_axis...]
    all_gather x6, waiting for transfers between devices: 441 us -> 23.3 us  [gather_planes(): return lax.all_gather(field, 'grp', axis=0, tiled=True)]
    reduce_scatter x7 -> x5, waiting for transfers between devices: 347 us -> 0.01 us  [sum_planes(): lax.psum_scatter(field.astype(jnp.bfloat16), 'grp', scatter_dimension=0,...]
    ppermute x0 -> x98, waiting for transfers between devices: none -> 274 us  [permute(): return lax.ppermute(field, 'seq', [(i, i ^ offset) for i in range(count)])]
    unnamed x167 -> x321, local copies, waits for them, and re-layouts: 34.1 us -> 102 us
    ppermute x0 -> x98, starting transfers between devices: none -> 66.2 us  [permute(): return lax.ppermute(field, 'seq', [(i, i ^ offset) for i in range(count)])]
    concatenate x3 -> x6, local copies, waits for them, and re-layouts: 65.7 us -> 3.97 us  [the longest x4 3.72 us: gather_pieces(): jnp.concatenate([have[at] for at in range(count) for have, _ in sides], a...]
    all_gather x1 -> x0, blocking collectives: 43.6 us -> none  [local(): lax.all_gather(gains.astype(jnp.bfloat16), ('grp', 'seq'), axis=1, tiled=...]
  transfers between devices with their start and end apart: 17 -> 122, of which waited for: 11 -> 44; matrix products, arithmetic and copies ran while one was open for 16% -> 42% of each run, Pallas kernels for 0% -> 0%
where the time goes in v1:
time: 1130 us; the launch traced here: 1120 us
  waiting for transfers between devices  350 us (31%)
  matrix products  254 us (22%)
  other arithmetic  200 us (18%)
  local copies, waits for them, and re-layouts  186 us (16%)
  starting transfers between devices  118 us (10%)
  between operations  16.4 us (1%)
    ppermute x98, waiting for transfers between devices, permute(): return lax.ppermute(field, 'seq', [(i, i ^ offset) for i in range(count)])  274 us
    unnamed x321, local copies, waits for them, and re-layouts  102 us
    dot_general x6, matrix products, contract_rows(): lax.dot_general(left, right, (((0,), (0,)), ((), ())), preferred_element_...  72.9 us
    ppermute x98, starting transfers between devices, permute(): return lax.ppermute(field, 'seq', [(i, i ^ offset) for i in range(count)])  66.2 us
    dot_general x4, matrix products, contract_cols(): lax.dot_general(left, right, (((1,), (1,)), ((), ())), preferred_element_...  62.1 us
    dot_general x3, matrix products, by_heads(): jnp.dot(norm_rows, w_gu, preferred_element_type=jnp.float32)  39.3 us
    unnamed x14, other arithmetic  34.8 us
    convert_element_type x12, other arithmetic, add_low(): (left.astype(jnp.float32) + right.astype(jnp.float32)).astype(jnp.bfloat16)  32 us
  transfers between devices with their start and end apart: 122, of which 44 were waited for; matrix products, arithmetic and copies ran while one was open for 42% of the time, Pallas kernels for 0%

profile of v1, /device:TPU:0, one launch (start us, length us, event | category | flops | bytes accessed | tf_op | source)
XLA Modules:
  0.0 1124.8 jit_solution(6654472039896698915)
XLA Ops:
  101.7 18.4 %collective-permute-done.10 = bf16[144,2304]{1,0:T(8,128)(2,1)} collective-permute-done((bf16[144,2304]{1,0:T(8,128)(2,1)}, bf16[144,2304]{1,0:T(8,128)(2,1)}, u32[]{:S(2)}, u32[]{:S(2)}) %collective-permute-start.10) | collective-permute-done | bytes 663584 | tf_op jit(solution)/shard_map/ppermute | solution.py:342
  244.5 17.8 %collective-permute-done.23 = bf16[144,2304]{1,0:T(8,128)(2,1)S(1)} collective-permute-done((bf16[144,2304]{1,0:T(8,128)(2,1)S(1)}, bf16[144,2304]{1,0:T(8,128)(2,1)S(1)}, u32[]{:S(2)}, u32[]{:S(2)}) %collective-permute-start.23) | collective-permute-done | bytes 663584 | tf_op jit(solution)/shard_map/ppermute | solution.py:342
  305.5 12.8 %collective-permute-done.27 = bf16[144,2304]{1,0:T(8,128)(2,1)S(1)} collective-permute-done((bf16[144,2304]{1,0:T(8,128)(2,1)}, bf16[144,2304]{1,0:T(8,128)(2,1)S(1)}, u32[]{:S(2)}, u32[]{:S(2)}) %collective-permute-start.27) | collective-permute-done | bytes 663584 | tf_op jit(solution)/shard_map/ppermute | solution.py:342
  359.3 12.7 %fusion.137 = f32[2304,768]{0,1:T(8,128)S(1)} fusion(bf16[2304,2304]{1,0:T(8,128)(2,1)} %constant_dynamic-update-slice_fusion.16, bf16[2304,768]{1,0:T(8,128)(2,1)} %all-gather.15.cloned.1.call-done), kind=kOutput, calls=%fused_computation.382 | convolution fusion | flops 8153726976 | bytes 21233664 | tf_op jit(solution)/shard_map/dot_general | solution.py:561
  376.0 13.1 %fusion.136 = f32[2304,768]{0,1:T(8,128)S(1)} fusion(bf16[2304,2304]{1,0:T(8,128)(2,1)} %constant_dynamic-update-slice_fusion.16, bf16[2304,768]{1,0:T(8,128)(2,1)} %all-gather.13.cloned.1.call-done), kind=kOutput, calls=%fused_computation.381 | convolution fusion | flops 8153726976 | bytes 21233664 | tf_op jit(solution)/shard_map/dot_general | solution.py:561
  393.3 13.5 %fusion.135 = f32[2304,768]{0,1:T(8,128)S(1)} fusion(bf16[2304,2304]{1,0:T(8,128)(2,1)} %constant_dynamic-update-slice_fusion.16, bf16[2304,768]{1,0:T(8,128)(2,1)} %all-gather.11.cloned.1.call-done), kind=kOutput, calls=%fused_computation.380 | convolution fusion | flops 8153726976 | bytes 21233664 | tf_op jit(solution)/shard_map/dot_general | solution.py:561
  412.2 23.3 %all-gather.17.cloned.1.call-done = bf16[2304,1152]{1,0:T(8,128)(2,1)} async-done(((bf16[576,1152]{1,0:T(8,128)(2,1)}), bf16[2304,1152]{1,0:T(8,128)(2,1)}) %all-gather.17.cloned.1.call-update) | async-done | bytes 5308432 | tf_op jit(solution)/shard_map/all_gather | solution.py:421
  435.5 19.0 %convolution_convert_fusion.2 = bf16[2304,2304]{1,0:T(8,128)(2,1)} fusion(bf16[2304,1152]{1,0:T(8,128)(2,1)} %all-gather.17.cloned.1.call-done, bf16[2304,384]{0,1:T(8,128)(2,1)S(1)} %multiply_convert_fusion.4, bf16[2304,384]{0,1:T(8,128)(2,1)S(1)} %multiply_convert_fusion.5, bf16[2304,384]{0,1:T(8,128)(2,1)} %multiply_convert_fusion.6), kind=kOutput, calls=%fused_computation.8 | convolution fusion | flops 12251824128 | bytes 21233664 | tf_op jit(solution)/shard_map/dot_general | solution.py:60
  473.8 11.9 %collective-permute-done.44 = bf16[144,2304]{1,0:T(8,128)(2,1)S(1)} collective-permute-done((bf16[144,2304]{1,0:T(8,128)(2,1)S(1)}, bf16[144,2304]{1,0:T(8,128)(2,1)S(1)}, u32[]{:S(2)}, u32[]{:S(2)}) %collective-permute-start.44) | collective-permute-done | bytes 663584 | tf_op jit(solution)/shard_map/ppermute | solution.py:342
  488.2 15.9 %collective-permute-done.47 = bf16[144,2304]{1,0:T(8,128)(2,1)S(1)} collective-permute-done((bf16[144,2304]{1,0:T(8,128)(2,1)S(1)}, bf16[144,2304]{1,0:T(8,128)(2,1)S(1)}, u32[]{:S(2)}, u32[]{:S(2)}) %collective-permute-start.47) | collective-permute-done | bytes 663584 | tf_op jit(solution)/shard_map/ppermute | solution.py:342
  537.1 14.3 %collective-permute-done.51 = bf16[144,2304]{1,0:T(8,128)(2,1)S(1)} collective-permute-done((bf16[144,2304]{1,0:T(8,128)(2,1)S(1)}, bf16[144,2304]{1,0:T(8,128)(2,1)S(1)}, u32[]{:S(2)}, u32[]{:S(2)}) %collective-permute-start.51) | collective-permute-done | bytes 663584 | tf_op jit(solution)/shard_map/ppermute | solution.py:342
  590.3 19.2 %fusion.138 = f32[2304,1152]{0,1:T(8,128)} fusion(bf16[2304,2304]{1,0:T(8,128)(2,1)} %constant_dynamic-update-slice_fusion.31, bf16[2304,1152]{1,0:T(8,128)(2,1)} %all-gather.17.cloned.1.call-done), kind=kOutput, calls=%fused_computation.383 | convolution fusion | flops 12230590464 | bytes 26542080 | tf_op jit(solution)/shard_map/dot_general | solution.py:573
  636.4 32.6 %convolution_convert_fusion.1 = bf16[2304,2304]{1,0:T(8,128)(2,1)} fusion(bf16[2304,2304]{0,1:T(8,128)(2,1)} %get-tuple-element.50, bf16[2304,768]{1,0:T(8,128)(2,1)} %all-gather.15.cloned.1.call-done, bf16[2304,768]{1,0:T(8,128)(2,1)} %all-gather.13.cloned.1.call-done, bf16[2304,768]{1,0:T(8,128)(2,1)} %all-gather.11.cloned.1.call-done), kind=kOutput, calls=%fused_computation.7 | convolution fusion | flops 24498339840 | bytes 31850496 | tf_op jit(solution)/shard_map/dot_general | solution.py:60
  675.2 12.9 %convolution_convert_fusion.7 = bf16[2304,768]{1,0:T(8,128)(2,1)} fusion(bf16[2304,2304]{1,0:T(8,128)(2,1)} %constant_dynamic-update-slice_fusion.16, bf16[2304,384]{0,1:T(8,128)(2,1)S(1)} %copy-done.58, bf16[2304,384]{0,1:T(8,128)(2,1)S(1)} %copy-done.50), kind=kOutput, calls=%fused_computation.49 | convolution fusion | flops 8162574336 | bytes 17694720 | tf_op jit(solution)/shard_map/dot_general | solution.py:54
  700.8 11.9 %collective-permute-done.68 = bf16[144,2304]{1,0:T(8,128)(2,1)S(1)} collective-permute-done((bf16[144,2304]{1,0:T(8,128)(2,1)S(1)}, bf16[144,2304]{1,0:T(8,128)(2,1)S(1)}, u32[]{:S(2)}, u32[]{:S(2)}) %collective-permute-start.68) | collective-permute-done | bytes 663584 | tf_op jit(solution)/shard_map/ppermute | solution.py:342
  713.7 17.3 %collective-permute-done.71 = bf16[144,2304]{1,0:T(8,128)(2,1)S(1)} collective-permute-done((bf16[144,2304]{1,0:T(8,128)(2,1)S(1)}, bf16[144,2304]{1,0:T(8,128)(2,1)S(1)}, u32[]{:S(2)}, u32[]{:S(2)}) %collective-permute-start.71) | collective-permute-done | bytes 663584 | tf_op jit(solution)/shard_map/ppermute | solution.py:342
  733.5 12.4 %convolution_convert_fusion.6 = bf16[2304,768]{1,0:T(8,128)(2,1)} fusion(bf16[2304,2304]{1,0:T(8,128)(2,1)} %constant_dynamic-update-slice_fusion.16, bf16[2304,384]{0,1:T(8,128)(2,1)S(1)} %copy-done.57, bf16[2304,384]{0,1:T(8,128)(2,1)S(1)} %copy-done.49), kind=kOutput, calls=%fused_computation.48 | convolution fusion | flops 8162574336 | bytes 17694720 | tf_op jit(solution)/shard_map/dot_general | solution.py:54
  770.2 12.4 %convolution_convert_fusion.5 = bf16[2304,768]{1,0:T(8,128)(2,1)} fusion(bf16[2304,2304]{1,0:T(8,128)(2,1)} %constant_dynamic-update-slice_fusion.16, bf16[2304,384]{0,1:T(8,128)(2,1)S(1)} %copy-done.56, bf16[2304,384]{0,1:T(8,128)(2,1)S(1)} %copy-done.48), kind=kOutput, calls=%fused_computation.47 | convolution fusion | flops 8162574336 | bytes 17694720 | tf_op jit(solution)/shard_map/dot_general | solution.py:54
  782.9 11.9 %collective-permute-done.75 = bf16[144,2304]{1,0:T(8,128)(2,1)S(1)} collective-permute-done((bf16[144,2304]{1,0:T(8,128)(2,1)}, bf16[144,2304]{1,0:T(8,128)(2,1)S(1)}, u32[]{:S(2)}, u32[]{:S(2)}) %collective-permute-start.75) | collective-permute-done | bytes 663584 | tf_op jit(solution)/shard_map/ppermute | solution.py:342
  846.5 11.9 %multiply_convert_fusion = bf16[2,1152,1152]{1,2,0:T(8,128)(2,1)} fusion(f32[2,1152,1152]{1,2,0:T(8,128)S(1)} %bitcast.186, f32[2,1152,1152]{1,2,0:T(8,128)} %get-tuple-element.163, f32[2,1152]{1,0:T(2,128)S(1)} %neg.23, f32[2,1152]{1,0:T(2,128)S(1)} %copy-done.89, s32[2,1152]{1,0:T(2,128)S(1)} %copy-done.75, pred[2,1152]{1,0:T(4,128)(4,1)S(1)} %copy-done.112, ...), kind=kOutput, calls=%fused_computation.20 | convolution fusion | flops 1398767616 | bytes 30258432 | tf_op jit(solution)/shard_map/mtd,mkd->mtk/dot_general | solution.py:545
  867.0 17.7 %convolution_convert_fusion.4 = bf16[2304,1152]{1,0:T(8,128)(2,1)} fusion(bf16[2304,2304]{1,0:T(8,128)(2,1)} %constant_dynamic-update-slice_fusion.31, bf16[2304,384]{0,1:T(8,128)(2,1)S(1)} %copy-done.52, bf16[2304,384]{0,1:T(8,128)(2,1)S(1)} %copy-done.54, bf16[2304,384]{0,1:T(8,128)(2,1)S(1)} %copy-done.55), kind=kOutput, calls=%fused_computation.14 | convolution fusion | flops 12249169920 | bytes 21233664 | tf_op jit(solution)/shard_map/dot_general | solution.py:54
  979.6 21.7 %collective-permute-done.96 = bf16[144,2304]{1,0:T(8,128)(2,1)} collective-permute-done((bf16[144,2304]{1,0:T(8,128)(2,1)}, bf16[144,2304]{1,0:T(8,128)(2,1)}, u32[]{:S(2)}, u32[]{:S(2)}) %collective-permute-start.96) | collective-permute-done | bytes 663584 | tf_op jit(solution)/shard_map/ppermute | solution.py:342
  1030.9 12.4 %fusion.114 = (bf16[72,18432]{1,0:T(8,128)(2,1)}, f32[72,18432]{1,0:T(8,128)}, f32[72,18432]{1,0:T(8,128)}) fusion(f32[72,18432]{1,0:T(8,128)} %param.23, f32[72,18432]{1,0:T(8,128)} %reshape.740, f32[72,18432]{1,0:T(8,128)} %param.28), kind=kLoop, calls=%fused_computation.363 | loop fusion | flops 9289728 | bytes 29196288 | tf_op jit(solution)/shard_map/convert_element_type | solution.py:69
  1076.0 12.3 %all-to-all-done.11 = bf16[8,72,1152]{2,1,0:T(8,128)(2,1)S(1)} async-done(((bf16[8,72,1152]{2,1,0:T(8,128)(2,1)}), bf16[8,72,1152]{2,1,0:T(8,128)(2,1)S(1)}, u32[]{:S(2)}, u32[]{:S(2)}) %all-to-all-start.11) | async-done | bytes 1327136 | tf_op jit(solution)/shard_map/all_to_all | solution.py:429
  (753 shorter events, 729.2 us)
Async XLA Ops:
  16.4 62.4 %collective-permute-start.7 = (bf16[144,2304]{1,0:T(8,128)(2,1)}, bf16[144,2304]{1,0:T(8,128)(2,1)}, u32[]{:S(2)}, u32[]{:S(2)}) collective-permute-start(bf16[144,2304]{1,0:T(8,128)(2,1)} %get-tuple-element.142), channel_id=1, source_target_pairs={{0,4},{1,5},{2,6},{3,7},{4,0},{5,1},{6,2},{7,3},{8,12},{9,13},{10,... | collective-permute-start | bytes 1990664 | tf_op jit(solution)/shard_map/ppermute | solution.py:342
  18.4 60.3 %collective-permute-start.3 = (bf16[144,2304]{1,0:T(8,128)(2,1)}, bf16[144,2304]{1,0:T(8,128)(2,1)}, u32[]{:S(2)}, u32[]{:S(2)}) collective-permute-start(bf16[144,2304]{1,0:T(8,128)(2,1)} %get-tuple-element.142), channel_id=1, source_target_pairs={{0,2},{1,3},{2,0},{3,1},{4,6},{5,7},{6,4},{7,5},{8,10},{9,11},{10,... | collective-permute-start | bytes 1990664 | tf_op jit(solution)/shard_map/ppermute | solution.py:342
  19.8 60.8 %collective-permute-start.1 = (bf16[144,2304]{1,0:T(8,128)(2,1)}, bf16[144,2304]{1,0:T(8,128)(2,1)}, u32[]{:S(2)}, u32[]{:S(2)}) collective-permute-start(bf16[144,2304]{1,0:T(8,128)(2,1)} %get-tuple-element.142), channel_id=1, source_target_pairs={{0,1},{1,0},{2,3},{3,2},{4,5},{5,4},{6,7},{7,6},{8,9},{9,8},{10,11... | collective-permute-start | bytes 1990664 | tf_op jit(solution)/shard_map/ppermute | solution.py:342
  19.9 54.8 %collective-permute-start.2 = (bf16[144,2304]{1,0:T(8,128)(2,1)}, bf16[144,2304]{1,0:T(8,128)(2,1)}, u32[]{:S(2)}, u32[]{:S(2)}) collective-permute-start(bf16[144,2304]{1,0:T(8,128)(2,1)} %get-tuple-element.143), channel_id=1, source_target_pairs={{0,2},{1,3},{2,0},{3,1},{4,6},{5,7},{6,4},{7,5},{8,10},{9,11},{10,... | collective-permute-start | bytes 1990664 | tf_op jit(solution)/shard_map/ppermute | solution.py:342
  20.4 56.2 %collective-permute-start = (bf16[144,2304]{1,0:T(8,128)(2,1)}, bf16[144,2304]{1,0:T(8,128)(2,1)}, u32[]{:S(2)}, u32[]{:S(2)}) collective-permute-start(bf16[144,2304]{1,0:T(8,128)(2,1)} %get-tuple-element.143), channel_id=1, source_target_pairs={{0,1},{1,0},{2,3},{3,2},{4,5},{5,4},{6,7},{7,6},{8,9},{9,8},{10,11... | collective-permute-start | bytes 1990664 | tf_op jit(solution)/shard_map/ppermute | solution.py:342
  37.8 104.6 %all-gather.7.cloned.1.call-start = ((), (), s32[]{:S(2)}) async-start(), calls=%async_computation.18 | async-start | bytes 2949120 | tf_op jit(solution)/shard_map/all_gather | solution.py:421
  61.9 133.6 %all-gather.9.cloned.1.call-start = ((), (), s32[]{:S(2)}) async-start(), calls=%async_computation.19 | async-start | bytes 1474560 | tf_op jit(solution)/shard_map/all_gather | solution.py:421
  76.6 43.5 %collective-permute-start.10 = (bf16[144,2304]{1,0:T(8,128)(2,1)}, bf16[144,2304]{1,0:T(8,128)(2,1)}, u32[]{:S(2)}, u32[]{:S(2)}) collective-permute-start(bf16[144,2304]{1,0:T(8,128)(2,1)} %collective-permute-done.2), channel_id=1, source_target_pairs={{0,4},{1,5},{2,6},{3,7},{4,0},{5,1},{6,2},{7,3},{8,12},{9,13},{10,... | collective-permute-start | bytes 1990664 | tf_op jit(solution)/shard_map/ppermute | solution.py:342
  87.9 82.3 %all-to-all-start.4 = ((bf16[8,72,768]{2,1,0:T(8,128)(2,1)}), bf16[8,72,768]{2,1,0:T(8,128)(2,1)}, u32[]{:S(2)}, u32[]{:S(2)}) async-start(bf16[8,72,768]{2,1,0:T(8,128)(2,1)} %copy.121), calls=%async_computation.4 | async-start | bytes 1769472 | tf_op jit(solution)/shard_map/all_to_all | solution.py:414
  92.2 267.1 %all-gather.15.cloned.1.call-start = ((), (), s32[]{:S(2)}) async-start(), calls=%async_computation.22 | async-start | bytes 4423680 | tf_op jit(solution)/shard_map/all_gather | solution.py:421
  92.9 283.1 %all-gather.13.cloned.1.call-start = ((), (), s32[]{:S(2)}) async-start(), calls=%async_computation.21 | async-start | bytes 4423680 | tf_op jit(solution)/shard_map/all_gather | solution.py:421
  212.0 181.3 %all-gather.11.cloned.1.call-start = ((), (), s32[]{:S(2)}) async-start(), calls=%async_computation.20 | async-start | bytes 4423680 | tf_op jit(solution)/shard_map/all_gather | solution.py:421
  270.7 164.8 %all-gather.17.cloned.1.call-start = ((), (), s32[]{:S(2)}) async-start(), calls=%async_computation.23 | async-start | bytes 6635520 | tf_op jit(solution)/shard_map/all_gather | solution.py:421
  305.5 623.2 %reduce-scatter.8.cloned.1.call-start = ((), (), s32[]{:S(2)}) async-start(), calls=%async_computation.24 | async-start | bytes 4423680 | tf_op jit(solution)/shard_map/reduce_scatter | solution.py:425
  688.0 254.3 %reduce-scatter.10.cloned.1.call-start = ((), (), s32[]{:S(2)}) async-start(), calls=%async_computation.25 | async-start | bytes 4423680 | tf_op jit(solution)/shard_map/reduce_scatter | solution.py:425
  698.2 48.5 %collective-permute-start.65 = (bf16[144,2304]{1,0:T(8,128)(2,1)}, bf16[144,2304]{1,0:T(8,128)(2,1)S(1)}, u32[]{:S(2)}, u32[]{:S(2)}) collective-permute-start(bf16[144,2304]{1,0:T(8,128)(2,1)} %slice.482), channel_id=1, source_target_pairs={{0,4},{1,5},{2,6},{3,7},{4,0},{5,1},{6,2},{7,3},{8,12},{9,13},{10,... | collective-permute-start | bytes 1990664 | tf_op jit(solution)/shard_map/ppermute | solution.py:342
  698.7 47.9 %collective-permute-start.70 = (bf16[144,2304]{1,0:T(8,128)(2,1)}, bf16[144,2304]{1,0:T(8,128)(2,1)S(1)}, u32[]{:S(2)}, u32[]{:S(2)}) collective-permute-start(bf16[144,2304]{1,0:T(8,128)(2,1)} %slice.490), channel_id=1, source_target_pairs={{0,2},{1,3},{2,0},{3,1},{4,6},{5,7},{6,4},{7,5},{8,10},{9,11},{10,... | collective-permute-start | bytes 1990664 | tf_op jit(solution)/shard_map/ppermute | solution.py:342
  746.0 225.0 %reduce-scatter.12.cloned.1.call-start = ((), (), s32[]{:S(2)}) async-start(), calls=%async_computation.26 | async-start | bytes 4423680 | tf_op jit(solution)/shard_map/reduce_scatter | solution.py:425
  782.6 283.5 %reduce-scatter.14.cloned.1.call-start = ((), (), s32[]{:S(2)}) async-start(), calls=%async_computation.27 | async-start | bytes 6635520 | tf_op jit(solution)/shard_map/reduce_scatter | solution.py:425
  950.3 143.4 %reduce-scatter.16.cloned.1.call-start = ((), (), s32[]{:S(2)}) async-start(), calls=%async_computation.28 | async-start | bytes 4423680 | tf_op jit(solution)/shard_map/reduce_scatter | solution.py:425
  967.0 83.3 %collective-permute-start.90 = (bf16[144,2304]{1,0:T(8,128)(2,1)}, bf16[144,2304]{1,0:T(8,128)(2,1)}, u32[]{:S(2)}, u32[]{:S(2)}) collective-permute-start(bf16[144,2304]{1,0:T(8,128)(2,1)} %slice.500), channel_id=1, source_target_pairs={{0,4},{1,5},{2,6},{3,7},{4,0},{5,1},{6,2},{7,3},{8,12},{9,13},{10,... | collective-permute-start | bytes 1990664 | tf_op jit(solution)/shard_map/ppermute | solution.py:342
  968.9 81.5 %collective-permute-start.95 = (bf16[144,2304]{1,0:T(8,128)(2,1)}, bf16[144,2304]{1,0:T(8,128)(2,1)}, u32[]{:S(2)}, u32[]{:S(2)}) collective-permute-start(bf16[144,2304]{1,0:T(8,128)(2,1)} %slice.508), channel_id=1, source_target_pairs={{0,2},{1,3},{2,0},{3,1},{4,6},{5,7},{6,4},{7,5},{8,10},{9,11},{10,... | collective-permute-start | bytes 1990664 | tf_op jit(solution)/shard_map/ppermute | solution.py:342
  977.6 72.8 %collective-permute-start.94 = (bf16[144,2304]{1,0:T(8,128)(2,1)}, bf16[144,2304]{1,0:T(8,128)(2,1)}, u32[]{:S(2)}, u32[]{:S(2)}) collective-permute-start(bf16[144,2304]{1,0:T(8,128)(2,1)} %add_convert_fusion.21), channel_id=1, source_target_pairs={{0,2},{1,3},{2,0},{3,1},{4,6},{5,7},{6,4},{7,5},{8,10},{9,11},{10,... | collective-permute-start | bytes 1990664 | tf_op jit(solution)/shard_map/ppermute | solution.py:342
  1003.3 47.1 %collective-permute-start.97 = (bf16[144,2304]{1,0:T(8,128)(2,1)}, bf16[144,2304]{1,0:T(8,128)(2,1)}, u32[]{:S(2)}, u32[]{:S(2)}) collective-permute-start(bf16[144,2304]{1,0:T(8,128)(2,1)} %add_convert_fusion.19), channel_id=1, source_target_pairs={{0,4},{1,5},{2,6},{3,7},{4,0},{5,1},{6,2},{7,3},{8,12},{9,13},{10,... | collective-permute-start | bytes 1990664 | tf_op jit(solution)/shard_map/ppermute | solution.py:342
  (227 other events, 3299.8 us)
Sparse Core Ops, SparseCore 0:
  40.8 52.7 all-gather.6
  95.8 29.1 all-gather.8
  126.5 69.0 all-gather.14
  197.1 68.5 all-gather.12
  267.7 68.5 all-gather.10
  337.7 97.7 all-gather.16
  688.2 63.8 reduce-scatter.7
  754.9 66.6 reduce-scatter.9
  824.5 66.6 reduce-scatter.11
  893.3 95.0 reduce-scatter.13
  990.9 66.8 reduce-scatter.15

commit v2 on v0

--- a/solution.py
+++ b/solution.py
@@ -1,6 +1,11 @@
+import functools
+
 import jax
 import jax.numpy as jnp
 from jax import lax
+from jax.experimental import pallas as pl
+from jax.experimental.layout import Layout, with_layout_constraint
+from jax.experimental.pallas import tpu as pltpu
 from jax.sharding import PartitionSpec as P
 
 HEADS = 8
@@ -17,6 +22,7 @@
 weight_rate = 0.03
 gain_rate = 0.2
 rope_base = 10000.0
+GELU_SCALE = (2.0 / 3.141592653589793) ** 0.5
 
 
 def scaled(field, gain):
@@ -69,7 +75,7 @@
     return (weight_new, moment_new, average_new, weight_new.astype(jnp.bfloat16))
 
 
-def local(
+def by_rows(
     tokens,
     cotangent,
     segments,
@@ -337,6 +343,899 @@
     )
 
 
+VMEM_LIMIT = 48 * 1024 * 1024
+
+
+def permute(field, offset):
+    count = lax.axis_size("seq")
+    return lax.ppermute(field, "seq", [(i, i ^ offset) for i in range(count)])
+
+
+def gather_near(field):
+    return field, permute(field, 2), permute(field, 4)
+
+
+def gather_mine(field, by_x, by_y):
+    half = field.shape[0] // 2
+    far = [permute(by_x[:half], 4), permute(by_y[half:], 2)]
+    return jnp.concatenate([field, by_x, by_y] + far, axis=0)
+
+
+def gather_far(field, by_x, by_y):
+    mine = gather_mine(field, by_x, by_y)
+    return [mine, permute(mine, 1)]
+
+
+def gather_pieces(field):
+    return gather_far(*gather_near(field))
+
+
+def add_low(left, right):
+    return (left.astype(jnp.float32) + right.astype(jnp.float32)).astype(jnp.bfloat16)
+
+
+def sum_far(own, by_x, by_y, far):
+    half = own.shape[0] // 2
+    far_x = permute(far[:half], 2)
+    far_y = permute(far[half:], 4)
+    by_y = jnp.concatenate([add_low(by_y[:half], far_x), by_y[half:]], axis=0)
+    by_x = jnp.concatenate([by_x[:half], add_low(by_x[half:], far_y)], axis=0)
+    return own, by_x, by_y
+
+
+def sum_near(own, by_x, by_y):
+    return own.astype(jnp.float32) + by_x.astype(jnp.float32) + by_y.astype(jnp.float32)
+
+
+def sum_pairs(*blocks):
+    own, by_x, by_y = sum_far(*blocks)
+    return sum_near(own, permute(by_x, 2), permute(by_y, 4))
+
+
+def pair_products(mine, other, weight):
+    rows = mine.shape[0] // 4
+    ends = []
+    for here in (slice(3 * rows, None), slice(None, 3 * rows)):
+        moved = permute(low(contract_cols(other[here], weight)), 1)
+        ends.append(add_low(low(contract_cols(mine[here], weight)), moved))
+    far, near = ends
+    return near[:rows], near[rows : 2 * rows], near[2 * rows :], far
+
+
+def pair_halves(mine, other, weight):
+    moved = permute(low(contract_cols(other, weight)), 1)
+    total = add_low(low(contract_cols(mine, weight)), moved)
+    rows = total.shape[0] // 4
+    return [total[at * rows : (at + 1) * rows] for at in range(4)]
+
+
+def sum_products(mine, other, weight):
+    return sum_pairs(*pair_products(mine, other, weight))
+
+
+def piece_order(blocks):
+    index = lax.axis_index("seq")
+    count = blocks.shape[0]
+    bits = count.bit_length() - 1
+    split = blocks.reshape((2,) * bits + blocks.shape[1:])
+    for bit in range(bits):
+        axis = bits - 1 - bit
+        split = jnp.where((index >> bit) & 1 == 1, jnp.flip(split, axis), split)
+    return jnp.swapaxes(split.reshape((count // 2, 2) + blocks.shape[1:]), 0, 1).reshape(blocks.shape)
+
+
+def qkv_columns(device):
+    return [device, HEADS + (device % 2) * KV_HEADS + device // 2]
+
+
+def out_columns(device):
+    return [device]
+
+
+def spread_kernel(count, blocks, field_ref, out_ref):
+    parts = len(blocks(0))
+    width = out_ref.shape[2] // parts
+    for device in range(count):
+        for part, block in enumerate(blocks(device)):
+            out_ref[device, :, part * width : (part + 1) * width] = field_ref[
+                :, block * width : (block + 1) * width
+            ].astype(jnp.bfloat16)
+
+
+def spread(field, count, blocks):
+    rows, columns = field.shape
+    return pl.pallas_call(
+        functools.partial(spread_kernel, count, blocks),
+        out_shape=jax.ShapeDtypeStruct((count, rows, columns // count), jnp.bfloat16),
+        cost_estimate=pl.CostEstimate(flops=0, transcendentals=0, bytes_accessed=6 * field.size),
+        compiler_params=pltpu.CompilerParams(vmem_limit_bytes=VMEM_LIMIT),
+        name="spread",
+    )(field)
+
+
+def row_product(weight, gradient):
+    used = weight.astype(jnp.bfloat16).astype(jnp.float32)
+    return jnp.sum(used * gradient, axis=1, keepdims=True)
+
+
+def renew_kernel(rate, w_ref, m_ref, a_ref, g_ref, w_out, m_out, a_out, c_out, product_out):
+    gradient = g_ref[0].astype(jnp.float32)
+    w_new, m_new, a_new, copy = renew(w_ref[...], m_ref[...], a_ref[...], gradient, rate)
+    product_out[...] += row_product(w_ref[...], gradient)
+    w_out[...] = w_new
+    m_out[...] = m_new
+    a_out[...] = a_new
+    c_out[...] = copy
+
+
+def renew_parts_kernel(rate, w_ref, m_ref, a_ref, *refs):
+    g_refs, outs = refs[:-5], refs[-5:]
+
+    @pl.when((pl.program_id(0) == 0) & (pl.program_id(1) == 0))
+    def _():
+        outs[-1][...] = jnp.zeros_like(outs[-1])
+
+    for part, g_ref in enumerate(g_refs):
+
+        @pl.when(pl.program_id(1) == part)
+        def _(g_ref=g_ref):
+            renew_kernel(rate, w_ref, m_ref, a_ref, g_ref, *outs)
+
+
+def renew_wide(weight, moment, average, gradients, rate):
+    rows, columns = weight.shape
+    parts = len(gradients)
+    count = gradients[0][0].shape[0]
+    width = columns // (count * parts)
+    own = pl.BlockSpec((rows, width), lambda d, p: (0, p * count + d))
+
+    def of_block(block):
+        return pl.BlockSpec((1, rows, width), lambda d, p: (d, 0, block))
+
+    return pl.pallas_call(
+        functools.partial(renew_parts_kernel, rate),
+        grid=(count, parts),
+        in_specs=[own, own, own] + [of_block(block) for _, block in gradients],
+        out_specs=[own, own, own, own, pl.BlockSpec((rows, 1), lambda d, p: (0, 0))],
+        out_shape=[jax.ShapeDtypeStruct((rows, columns), jnp.float32)] * 3
+        + [
+            jax.ShapeDtypeStruct((rows, columns), jnp.bfloat16),
+            jax.ShapeDtypeStruct((rows, 1), jnp.float32),
+        ],
+        cost_estimate=pl.CostEstimate(
+            flops=8 * weight.size, transcendentals=0, bytes_accessed=28 * weight.size
+        ),
+        compiler_params=pltpu.CompilerParams(vmem_limit_bytes=VMEM_LIMIT),
+        name="renew",
+    )(weight, moment, average, *(array for array, _ in gradients))
+
+
+def renew_heads_kernel(rate, g_ref, *refs):
+    product = jnp.zeros(refs[-1].shape, jnp.float32)
+    for device in range(g_ref.shape[0]):
+        blocks = [(0, block) for block in qkv_columns(device)] + [(1, device)]
+        for part, (which, block) in enumerate(blocks):
+            w_ref, m_ref, a_ref = refs[3 * which : 3 * which + 3]
+            outs = refs[6 + 4 * which : 10 + 4 * which]
+            here = (slice(None), slice(block * HEAD, (block + 1) * HEAD))
+            gradient = g_ref[device, :, part * HEAD : (part + 1) * HEAD].astype(jnp.float32)
+            results = renew(w_ref[here], m_ref[here], a_ref[here], gradient, rate)
+            for out, result in zip(outs, results):
+                out[here] = result
+            if which == 0:
+                product += row_product(w_ref[here], gradient)
+    refs[-1][...] = product
+
+
+def renew_heads(gradient, attn_in, attn_out, rate):
+    kinds = (jnp.float32, jnp.float32, jnp.float32, jnp.bfloat16)
+    shapes = [
+        jax.ShapeDtypeStruct(state[0].shape, kind) for state in (attn_in, attn_out) for kind in kinds
+    ]
+    size = attn_in[0].size + attn_out[0].size
+    results = pl.pallas_call(
+        functools.partial(renew_heads_kernel, rate),
+        out_shape=shapes + [jax.ShapeDtypeStruct((attn_in[0].shape[0], 1), jnp.float32)],
+        cost_estimate=pl.CostEstimate(flops=8 * size, transcendentals=0, bytes_accessed=28 * size),
+        compiler_params=pltpu.CompilerParams(vmem_limit_bytes=VMEM_LIMIT),
+        name="renew_heads",
+    )(gradient, *attn_in, *attn_out)
+    return results[:4], results[4:8], results[8]
+
+
+def glu_back_kernel(left0_ref, left1_ref, w0_ref, w1_ref, gate_up_ref, out_ref):
+    width = w0_ref.shape[1]
+    d_hidden = jnp.dot(left0_ref[...], w0_ref[...], preferred_element_type=jnp.float32)
+    d_hidden += jnp.dot(left1_ref[...], w1_ref[...], preferred_element_type=jnp.float32)
+    gate = gate_up_ref[:, :width]
+    upper = gate_up_ref[:, width:]
+    square = gate * gate
+    bent = jnp.tanh(GELU_SCALE * gate * (1.0 + 0.044715 * square))
+    rise = 0.5 * (1.0 + bent)
+    slope = rise + 0.5 * gate * (1.0 - bent * bent) * GELU_SCALE * (1.0 + 3 * 0.044715 * square)
+    out_ref[:, :width] = (d_hidden * upper * slope).astype(jnp.bfloat16)
+    out_ref[:, width:] = (d_hidden * gate * rise).astype(jnp.bfloat16)
+
+
+def glu_back_rows(left0, left1, w0, w1, gate_up):
+    rows = left0.shape[0]
+    width = w0.shape[1]
+    tile = rows // 6
+    return pl.pallas_call(
+        glu_back_kernel,
+        grid=(rows // tile,),
+        in_specs=[
+            pl.BlockSpec((tile, left0.shape[1]), lambda i: (i, 0)),
+            pl.BlockSpec((tile, left1.shape[1]), lambda i: (i, 0)),
+            pl.BlockSpec(w0.shape, lambda i: (0, 0)),
+            pl.BlockSpec(w1.shape, lambda i: (0, 0)),
+            pl.BlockSpec((tile, 2 * width), lambda i: (i, 0)),
+        ],
+        out_specs=pl.BlockSpec((tile, 2 * width), lambda i: (i, 0)),
+        out_shape=jax.ShapeDtypeStruct((rows, 2 * width), jnp.bfloat16),
+        cost_estimate=pl.CostEstimate(
+            flops=2 * rows * (w0.shape[0] + w1.shape[0]) * width,
+            transcendentals=rows * width,
+            bytes_accessed=rows * (2 * (left0.shape[1] + left1.shape[1]) + 12 * width),
+        ),
+        compiler_params=pltpu.CompilerParams(vmem_limit_bytes=VMEM_LIMIT),
+        name="glu_back",
+    )(left0, left1, w0, w1, gate_up)
+
+
+def norm_tiles(rows, width, kinds):
+    tile = rows // 3
+    return [
+        pl.BlockSpec((tile, width), lambda i: (i, 0))
+        if kind
+        else pl.BlockSpec((1, width), lambda i: (0, 0))
+        for kind in kinds
+    ]
+
+
+def norm_call(kernel, name, rows, width, fields, gains, outs):
+    specs = norm_tiles(rows, width, [1] * len(fields) + [0] * len(gains))
+    return pl.pallas_call(
+        kernel,
+        grid=(3,),
+        in_specs=specs,
+        out_specs=norm_tiles(rows, width, [out is not None for out in outs]),
+        out_shape=[
+            jax.ShapeDtypeStruct((rows, width), out)
+            if out is not None
+            else jax.ShapeDtypeStruct((1, width), jnp.float32)
+            for out in outs
+        ],
+        cost_estimate=pl.CostEstimate(
+            flops=20 * rows * width, transcendentals=0, bytes_accessed=20 * rows * width
+        ),
+        compiler_params=pltpu.CompilerParams(vmem_limit_bytes=VMEM_LIMIT // 2),
+        name=name,
+    )(*fields, *gains)
+
+
+def row_inverse(field):
+    return lax.rsqrt(jnp.mean(field * field, axis=1, keepdims=True) + eps_norm)
+
+
+def row_back(field, inverse, top):
+    inner = jnp.mean(field * top, axis=1, keepdims=True)
+    return inverse * top - field * (inverse * inverse * inverse * inner)
+
+
+def read_sum(own_ref, by_x_ref, by_y_ref):
+    return (
+        own_ref[...].astype(jnp.float32)
+        + by_x_ref[...].astype(jnp.float32)
+        + by_y_ref[...].astype(jnp.float32)
+    )
+
+
+def middle_kernel(own_ref, by_x_ref, by_y_ref, token_ref, g1_ref, g2_ref, branch_ref, middle_ref, out_ref):
+    branch = read_sum(own_ref, by_x_ref, by_y_ref)
+    branch_ref[...] = branch
+    middle = token_ref[...].astype(jnp.float32) + branch * row_inverse(branch) * g1_ref[...]
+    middle_ref[...] = middle
+    out_ref[...] = (middle * row_inverse(middle) * g2_ref[...]).astype(jnp.bfloat16)
+
+
+def middle_back_kernel(
+    own_ref,
+    by_x_ref,
+    by_y_ref,
+    top_ref,
+    branch_ref,
+    middle_ref,
+    g1_ref,
+    g2_ref,
+    d_middle_ref,
+    d_branch_ref,
+    d_gain_ref,
+):
+    middle, branch = middle_ref[...], branch_ref[...]
+    d_normed = read_sum(own_ref, by_x_ref, by_y_ref)
+    d_middle = top_ref[...].astype(jnp.float32) + row_back(
+        middle, row_inverse(middle), g2_ref[...] * d_normed
+    )
+    d_middle_ref[...] = d_middle
+    inverse = row_inverse(branch)
+    d_branch_ref[...] = row_back(branch, inverse, g1_ref[...] * d_middle).astype(jnp.bfloat16)
+
+    @pl.when(pl.program_id(0) == 0)
+    def _():
+        d_gain_ref[...] = jnp.zeros_like(d_gain_ref)
+
+    d_gain_ref[...] += jnp.sum(d_middle * (branch * inverse), axis=0, keepdims=True)
+
+
+def input_back_kernel(own_ref, by_x_ref, by_y_ref, token_ref, d_middle_ref, g0_ref, out_ref):
+    token = token_ref[...].astype(jnp.float32)
+    d_normed = read_sum(own_ref, by_x_ref, by_y_ref)
+    out_ref[...] = d_middle_ref[...] + row_back(token, row_inverse(token), g0_ref[...] * d_normed)
+
+
+def across(left, right):
+    return lax.dot_general(
+        left, right, (((1,), (1,)), ((), ())), preferred_element_type=jnp.float32
+    )
+
+
+def down(left, right):
+    return lax.dot_general(
+        left, right, (((0,), (0,)), ((), ())), preferred_element_type=jnp.float32
+    )
+
+
+def capped_scores(q, k, key_ref, query_ref):
+    bent = jnp.tanh(across(k, q) * (HEAD ** (-0.5) / soft_cap))
+    key, query = key_ref[0][:, :1], query_ref[0]
+    seg_k, seg_q = key & 15, query & 15
+    seen = ((key >> 4) <= (query >> 4)) & ((seg_k == 0) | (seg_k == seg_q))
+    return bent, jnp.where(seen, soft_cap * bent, -1e30)
+
+
+def attend_kernel(q_ref, k_ref, v_ref, key_ref, query_ref, out_ref, norm_ref):
+    _, capped = capped_scores(q_ref[0], k_ref[0], key_ref, query_ref)
+    top = jnp.max(capped, axis=0, keepdims=True)
+    powers = jnp.exp(capped - top)
+    total = jnp.sum(powers, axis=0, keepdims=True)
+    weights = (powers * (1.0 / total)).astype(jnp.bfloat16)
+    norm_ref[0] = top + jnp.log(total)
+    out_ref[0] = down(weights, v_ref[0]).astype(jnp.bfloat16)
+
+
+def attend_back_kernel(
+    q_ref, k_ref, v_ref, key_ref, query_ref, norm_ref, d_out_ref, dq_ref, dk_ref, dv_ref
+):
+    q, k, v, d_out = q_ref[0], k_ref[0], v_ref[0], d_out_ref[0]
+    bent, capped = capped_scores(q, k, key_ref, query_ref)
+    weights = jnp.exp(capped - norm_ref[0])
+    d_weights = across(v, d_out)
+    inner = jnp.sum(weights * d_weights, axis=0, keepdims=True)
+    d_raw = (weights * (d_weights - inner) * (1.0 - bent * bent)).astype(jnp.bfloat16)
+    scale = HEAD ** (-0.5)
+
+    @pl.when(pl.program_id(1) == 0)
+    def _():
+        dk_ref[...] = jnp.zeros_like(dk_ref)
+        dv_ref[...] = jnp.zeros_like(dv_ref)
+
+    dq_ref[0] = down(d_raw, k) * scale
+    dk_ref[0] += jnp.dot(d_raw, q, preferred_element_type=jnp.float32) * scale
+    dv_ref[0] += jnp.dot(weights.astype(jnp.bfloat16), d_out, preferred_element_type=jnp.float32)
+
+
+def attention_cost(micros, rows, products):
+    return pl.CostEstimate(
+        flops=2 * products * micros * rows * rows * HEAD,
+        transcendentals=2 * micros * rows * rows,
+        bytes_accessed=4 * products * micros * rows * HEAD,
+    )
+
+
+def attention_specs(rows, tile):
+    moving = pl.BlockSpec((1, tile, HEAD), lambda m, i: (m, i, 0))
+    whole = pl.BlockSpec((1, rows, HEAD), lambda m, i: (m, 0, 0))
+    lane = pl.BlockSpec((1, 1, tile), lambda m, i: (m, 0, i))
+    places = [pl.BlockSpec((1, rows, 128), lambda m, i: (m, 0, 0)), lane]
+    return moving, whole, lane, places
+
+
+def attend(q, k, v, places):
+    micros, rows, _ = q.shape
+    tile = rows // 3
+    moving, whole, lane, place_specs = attention_specs(rows, tile)
+    return pl.pallas_call(
+        attend_kernel,
+        grid=(micros, rows // tile),
+        in_specs=[moving, whole, whole] + place_specs,
+        out_specs=[moving, lane],
+        out_shape=[
+            jax.ShapeDtypeStruct(q.shape, jnp.bfloat16),
+            jax.ShapeDtypeStruct((micros, 1, rows), jnp.float32),
+        ],
+        cost_estimate=attention_cost(micros, rows, 2),
+        compiler_params=pltpu.CompilerParams(vmem_limit_bytes=VMEM_LIMIT),
+        name="attend",
+    )(q, k, v, *places)
+
+
+def attend_back(q, k, v, places, norm, d_out):
+    micros, rows, _ = q.shape
+    tile = rows // 3
+    moving, whole, lane, place_specs = attention_specs(rows, tile)
+    return pl.pallas_call(
+        attend_back_kernel,
+        grid=(micros, rows // tile),
+        in_specs=[moving, whole, whole] + place_specs + [lane, moving],
+        out_specs=[moving, whole, whole],
+        out_shape=[jax.ShapeDtypeStruct(q.shape, jnp.float32)] * 3,
+        cost_estimate=attention_cost(micros, rows, 5),
+        compiler_params=pltpu.CompilerParams(vmem_limit_bytes=VMEM_LIMIT),
+        name="attend_back",
+    )(q, k, v, *places, norm, d_out)
+
+
+def exchange(field):
+    return lax.all_to_all(field, "seq", split_axis=0, concat_axis=0, tiled=True)
+
+
+def in_order(step, *operands):
+    zeros = jax.eval_shape(step, *operands)
+    return lax.cond(
+        lax.optimization_barrier(jnp.bool_(True)),
+        step,
+        lambda *_: jax.tree.map(lambda leaf: jnp.zeros(leaf.shape, leaf.dtype), zeros),
+        *operands,
+    )
+
+
+def gather_planes(field):
+    return lax.all_gather(field, "grp", axis=0, tiled=True)
+
+
+def sum_planes(field):
+    return lax.psum_scatter(field, "grp", scatter_dimension=0, tiled=True)
+
+
+def turn(field, cosine, sine):
+    half = field.shape[-1] // 2
+    first, second = field[..., :half], field[..., half:]
+    return jnp.concatenate([first * cosine - second * sine, second * cosine + first * sine], axis=-1)
+
+
+def low(field):
+    return field.astype(jnp.bfloat16)
+
+
+def dot(left, right):
+    return jnp.dot(left, right, preferred_element_type=jnp.float32)
+
+
+def over_rows(lefts, rights):
+    return low(contract_rows(lefts[0], rights[0]) + contract_rows(lefts[1], rights[1]))
+
+
+def by_heads(
+    tokens,
+    cotangent,
+    segments,
+    attn_in,
+    attn_out,
+    ffn_in,
+    ffn_out,
+    gains,
+    attn_in_mom,
+    attn_out_mom,
+    ffn_in_mom,
+    ffn_out_mom,
+    gains_mom,
+    attn_in_avg,
+    attn_out_avg,
+    ffn_in_avg,
+    ffn_out_avg,
+    gains_avg,
+):
+    tie = lax.optimization_barrier
+    micro_count, local_rows, model_width = tokens.shape
+    all_rows = micro_count * local_rows
+    seq_count = lax.axis_size("seq")
+    grp_count = lax.axis_size("grp")
+    device_count = seq_count * grp_count
+    group_rows = segments.shape[1]
+    own_rows = ffn_in.shape[0]
+    plane_rows = own_rows * seq_count
+    cut = own_rows * 2 // 3
+    slice_width = ffn_out.shape[1] // seq_count
+    index = lax.axis_index("seq")
+    key_core = index % 2 == 0
+    token_total = micro_count * local_rows * device_count
+    rate_mat = weight_rate * token_total ** (-0.5)
+    rate_gain = gain_rate * token_total ** (-0.5)
+
+    def ffn_columns(device):
+        return [device, seq_count + device]
+
+    def by_device(part):
+        return exchange(part.reshape(seq_count, own_rows, -1))
+
+    def to_parts(field):
+        split = field.reshape(-1, device_count, own_rows)
+        return [
+            split[:, :, :cut].reshape(field.shape[0], -1),
+            split[:, :, cut:].reshape(field.shape[0], -1),
+        ]
+
+    def from_parts(parts):
+        split = [part.reshape(part.shape[0], device_count, -1) for part in parts]
+        return jnp.concatenate(split, axis=2).reshape(-1, model_width)
+
+    def to_groups(field):
+        return (
+            field.reshape(seq_count, micro_count, local_rows, -1)
+            .transpose(1, 0, 2, 3)
+            .reshape(micro_count, group_rows, -1)
+        )
+
+    def from_groups(field):
+        return (
+            field.reshape(micro_count, seq_count, local_rows, -1)
+            .transpose(1, 0, 2, 3)
+            .reshape(seq_count * all_rows, -1)
+        )
+
+    def in_two(field):
+        return [field[: field.shape[0] // 2], field[field.shape[0] // 2 :]]
+
+    def swap_cores(field):
+        first, second = in_two(permute(field, 1))
+        return jnp.concatenate([second, first], axis=0)
+
+    heads_moved = exchange(
+        jnp.concatenate(
+            [spread(attn_in, seq_count, qkv_columns), spread(attn_out, seq_count, out_columns)], axis=2
+        )
+    ).reshape(plane_rows, 3 * HEAD)
+    later_tokens, gains_low, heads_moved = tie((tokens, low(gains), heads_moved))
+    w_heads = gather_planes(heads_moved)
+    all_gains = lax.all_to_all(
+        jnp.broadcast_to(gains_low[None], (device_count,) + gains.shape),
+        ("grp", "seq"),
+        split_axis=0,
+        concat_axis=0,
+        tiled=True,
+    )
+    gain_vals = all_gains.transpose(1, 0, 2).reshape(4, model_width).astype(jnp.float32)
+    own_rows_low, by_x, by_y = gather_near(later_tokens.reshape(all_rows, model_width))
+    true_rows = jnp.arange(group_rows, dtype=jnp.int32)
+    positions = jax.vmap(lambda seg: place_tokens(seg, seg, true_rows))(segments)
+
+    def to_pieces(field):
+        return piece_order(field.reshape(micro_count, seq_count, local_rows).transpose(1, 0, 2))
+
+    place = to_pieces(positions).reshape(-1).astype(jnp.float32)
+    seg = to_pieces(segments).transpose(1, 0, 2).reshape(micro_count, group_rows)
+    row = piece_order(true_rows.reshape(seq_count, local_rows)).reshape(-1)
+    freqs = rope_base ** (-jnp.arange(HEAD // 2, dtype=jnp.float32) * 2.0 / HEAD)
+    angles = place[:, None] * freqs[None, :]
+    cosine, sine = jnp.cos(angles), jnp.sin(angles)
+    cosine, sine, kv_cosine, kv_sine, *places = tie(
+        (
+            cosine,
+            sine,
+            jnp.where(key_core, cosine, 1.0),
+            jnp.where(key_core, sine, 0.0),
+            jnp.broadcast_to((16 * row + seg)[:, :, None], seg.shape + (128,)),
+            (16 * row + seg)[:, None, :],
+        )
+    )
+
+    by_x, by_y, later_ffn_in, gain_vals, cosine = tie((by_x, by_y, ffn_in, gain_vals, cosine))
+    gu_moved = exchange(spread(later_ffn_in, seq_count, ffn_columns))
+    token_rows = gather_far(own_rows_low, by_x, by_y)
+    w_gu = gather_planes(gu_moved.reshape(plane_rows, 2 * slice_width))
+    down_low = spread(ffn_out, seq_count, out_columns)
+
+    def normed_token_rows(token_rows, inverses):
+        return [
+            low(part.astype(jnp.float32) * inverse[:, None] * gain_vals[0])
+            for part, inverse in zip(token_rows, inverses)
+        ]
+
+    def attention(token_rows, w_heads, down_low):
+        w_qkv = w_heads[:, : 2 * HEAD]
+        down_moved = exchange(down_low)
+        inverses = [
+            lax.rsqrt(jnp.mean(jnp.square(part.astype(jnp.float32)), axis=1) + eps_norm)
+            for part in token_rows
+        ]
+        projected = jnp.concatenate(
+            [dot(part, w_qkv) for part in normed_token_rows(token_rows, inverses)], axis=0
+        )
+        kv_own = low(turn(projected[:, HEAD:], kv_cosine, kv_sine))
+        kv_other = swap_cores(kv_own)
+        queries = to_groups(low(turn(projected[:, :HEAD], cosine, sine)))
+        keys = to_groups(jnp.where(key_core, kv_own, kv_other))
+        values = to_groups(jnp.where(key_core, kv_other, kv_own))
+        mixed, norm = attend(queries, keys, values, places)
+        mixed, down_moved = tie((mixed, down_moved))
+        mixed_rows = in_two(from_groups(mixed))
+        down_rows = [
+            part.reshape(-1, slice_width) for part in (down_moved[:, :cut], down_moved[:, cut:])
+        ]
+        return down_rows, inverses, (queries, keys, values, norm), mixed_rows
+
+    down_rows, inverses, state, mixed_rows = in_order(attention, token_rows, w_heads, down_low)
+    w_down0, w_down1 = gather_planes(down_rows[0]), gather_planes(down_rows[1])
+
+    def attention_out(mixed_rows, w_heads, tokens, cotangent):
+        w_o = w_heads[:, 2 * HEAD :]
+        grad_parts = to_parts(cotangent.reshape(all_rows, model_width))
+        own, by_x, by_y = sum_far(*pair_products(*mixed_rows, w_o))
+        by_x, by_y, *grad_parts = tie((permute(by_x, 2), permute(by_y, 4), *grad_parts))
+        branch, middle, normed_three = norm_call(
+            middle_kernel,
+            "middle",
+            all_rows,
+            model_width,
+            [own, by_x, by_y, tokens.reshape(all_rows, model_width)],
+            [gain_vals[1:2], gain_vals[2:3]],
+            [jnp.float32, jnp.float32, jnp.bfloat16],
+        )
+        norm_rows = jnp.concatenate(gather_pieces(normed_three), axis=0)
+        return branch, middle, norm_rows, grad_parts
+
+    branch, middle, norm_rows, grad_parts = in_order(
+        attention_out, mixed_rows, w_heads, tokens, cotangent
+    )
+    queries, keys, values, norm = state
+
+    def feed_up(norm_rows, w_gu):
+        gate_up = dot(norm_rows, w_gu)
+        return gate_up, low(glu_part(gate_up[:, :slice_width], gate_up[:, slice_width:]))
+
+    gate_up, hidden = in_order(feed_up, norm_rows, w_gu)
+
+    def feed_down(hidden, w_down0):
+        return sum_products(*in_two(hidden), w_down0)
+
+    ffn0 = in_order(feed_down, hidden, w_down0)
+    gain_parts = to_parts(gain_vals[3:])
+
+    def feed_end(hidden, w_down1, ffn0, grad_parts):
+        ffn1 = sum_products(*in_two(hidden), w_down1)
+        ffns = [ffn0, ffn1]
+        squares = sum(jnp.sum(part * part, axis=1, keepdims=True) for part in ffns)
+        inverse = lax.rsqrt(squares / model_width + eps_norm)
+        tops = [part.astype(jnp.float32) for part in grad_parts]
+        scaled_tops = [top * gain for top, gain in zip(tops, gain_parts)]
+        inner = sum(
+            jnp.sum(top * part, axis=1, keepdims=True) for top, part in zip(scaled_tops, ffns)
+        )
+        pull = inverse * inverse * inverse * (inner / model_width)
+        d_ffns = [low(top * inverse - part * pull) for top, part in zip(scaled_tops, ffns)]
+        first = jnp.concatenate(gather_pieces(d_ffns[1]), axis=0)
+        return ffn1, inverse, gather_near(d_ffns[0]), first, low(contract_rows(first, hidden))
+
+    ffn1, inverse, second_near, first, grad_down1 = in_order(feed_end, hidden, w_down1, ffn0, grad_parts)
+
+    down_part1 = sum_planes(grad_down1)
+
+    def feed_back(second_near, hidden):
+        second = jnp.concatenate(gather_far(*second_near), axis=0)
+        return second, low(contract_rows(second, hidden))
+
+    second, grad_down0 = in_order(feed_back, second_near, hidden)
+    down_part0 = sum_planes(grad_down0)
+
+    def feed_back_rows(second, first, gate_up, norm_rows, w_down0, w_down1, w_gu, down_part1):
+        second, down_part1 = tie((second, down_part1))
+        d_gate_up = glu_back_rows(second, first, w_down0, w_down1, gate_up)
+        blocks = pair_halves(*in_two(d_gate_up), w_gu)
+        grad_gate = low(contract_rows(norm_rows, d_gate_up[:, :slice_width]))
+        return d_gate_up, blocks, with_layout_constraint(grad_gate, Layout((0, 1))), down_part1
+
+    d_gate_up, d_norm_blocks, grad_gate, down_part1 = in_order(
+        feed_back_rows, second, first, gate_up, norm_rows, w_down0, w_down1, w_gu, down_part1
+    )
+    gate_part = sum_planes(grad_gate)
+
+    def middle_back(
+        d_norm_blocks, d_gate_up, norm_rows, cotangent, branch, middle, down_part0, down_part1
+    ):
+        d_gate_up, down_part0 = tie((d_gate_up, down_part0))
+        down_part = jnp.concatenate(
+            [part.reshape(seq_count, -1, slice_width) for part in (down_part0, down_part1)], axis=1
+        )
+        own, by_x, by_y = sum_far(*d_norm_blocks)
+        by_x, by_y, norm_rows = tie((by_x, by_y, norm_rows))
+        by_x, by_y = permute(by_x, 2), permute(by_y, 4)
+        grad_upper = low(contract_rows(norm_rows, d_gate_up[:, slice_width:]))
+        by_x, by_y, grad_upper = tie((by_x, by_y, grad_upper))
+        d_middle, d_branch, d_gain_two = norm_call(
+            middle_back_kernel,
+            "middle_back",
+            all_rows,
+            model_width,
+            [own, by_x, by_y, cotangent.reshape(all_rows, model_width), branch, middle],
+            [gain_vals[1:2], gain_vals[2:3]],
+            [jnp.float32, jnp.bfloat16, None],
+        )
+        return grad_upper, d_middle, d_branch, d_gain_two[0], down_part
+
+    grad_upper, d_middle, d_branch, d_gain_two, down_part = in_order(
+        middle_back,
+        d_norm_blocks,
+        d_gate_up,
+        norm_rows,
+        cotangent,
+        branch,
+        middle,
+        down_part0,
+        down_part1,
+    )
+    upper_part = sum_planes(grad_upper)
+
+    def output_rows(d_branch, middle, ffns, inverse, grad_parts):
+        own, by_x, by_y = gather_near(d_branch)
+        normeds = [part * inverse for part in ffns]
+        d_gain_four = from_parts(
+            [
+                jnp.sum(top.astype(jnp.float32) * part, axis=0)[None]
+                for top, part in zip(grad_parts, normeds)
+            ]
+        )[0]
+        normed_four = from_parts([part * gain for part, gain in zip(normeds, gain_parts)])
+        layer_out = low(middle + normed_four).reshape(tokens.shape)
+        by_x, by_y, layer_out = tie((by_x, by_y, layer_out))
+        return gather_mine(own, by_x, by_y), d_gain_four, layer_out
+
+    d_branch_mine, d_gain_four, layer_out = in_order(
+        output_rows, d_branch, middle, [ffn0, ffn1], inverse, grad_parts
+    )
+
+    def attention_back(
+        d_branch_mine,
+        mixed_rows,
+        w_heads,
+        gate_part,
+        down_part,
+        token_rows,
+        inverses,
+        queries,
+        keys,
+        values,
+        norm,
+    ):
+        gate_grad = by_device(gate_part)
+        d_branch_rows = [d_branch_mine, permute(d_branch_mine, 1)]
+        d_mixed = to_groups(
+            jnp.concatenate([low(dot(part, w_heads[:, 2 * HEAD :])) for part in d_branch_rows], axis=0)
+        )
+        d_query, d_keys, d_values = attend_back(queries, keys, values, places, norm, d_mixed)
+        d_query, d_keys, d_values, gate_grad = tie((d_query, d_keys, d_values, gate_grad))
+        d_kv = from_groups(jnp.where(key_core, d_keys, d_values)) + swap_cores(
+            from_groups(low(jnp.where(key_core, d_values, d_keys)))
+        ).astype(jnp.float32)
+        d_projected = in_two(
+            low(
+                jnp.concatenate(
+                    [turn(from_groups(d_query), cosine, -sine), turn(d_kv, kv_cosine, -kv_sine)],
+                    axis=1,
+                )
+            )
+        )
+        moved = permute(low(contract_cols(d_projected[1], w_heads[:, : 2 * HEAD])), 1)
+        down_grad = exchange(down_part)
+        grad_out = over_rows(d_branch_rows, mixed_rows)
+        grad_qkv = over_rows(normed_token_rows(token_rows, inverses), d_projected)
+        grad_heads = jnp.concatenate(
+            [with_layout_constraint(grad, Layout((0, 1))) for grad in (grad_qkv, grad_out)], axis=1
+        )
+        return d_projected[0], moved, grad_heads, gate_grad, down_grad
+
+    d_projected, moved, grad_heads, gate_grad, down_grad = in_order(
+        attention_back,
+        d_branch_mine,
+        mixed_rows,
+        w_heads,
+        gate_part,
+        down_part,
+        token_rows,
+        inverses,
+        queries,
+        keys,
+        values,
+        norm,
+    )
+    heads_part = sum_planes(grad_heads)
+
+    def update_start(d_projected, moved, w_heads, upper_part):
+        upper_grad = by_device(upper_part)
+        total = add_low(low(contract_cols(d_projected, w_heads[:, : 2 * HEAD])), moved)
+        total, upper_grad = tie((total, upper_grad))
+        rows = total.shape[0] // 4
+        return sum_far(*(total[at * rows : (at + 1) * rows] for at in range(4))), upper_grad
+
+    (own, by_x, by_y), upper_grad = in_order(
+        update_start, d_projected, moved, w_heads, upper_part
+    )
+    by_x, by_y = permute(by_x, 2), permute(by_y, 4)
+    gu_all = renew_wide(
+        ffn_in, ffn_in_mom, ffn_in_avg, [(gate_grad, 0), (upper_grad, 0)], rate_mat
+    )
+    down_all = renew_wide(ffn_out, ffn_out_mom, ffn_out_avg, [(down_grad, 0)], rate_mat)
+    gu_all, heads_part = tie((gu_all, heads_part))
+    heads_grad = by_device(heads_part)
+    heads_grad, d_gain_two = tie((heads_grad, d_gain_two))
+    sum_gains = jnp.sum(
+        lax.all_to_all(
+            jnp.stack([d_gain_two, d_gain_four]).reshape(2, device_count, -1).transpose(1, 0, 2),
+            ("grp", "seq"),
+            split_axis=0,
+            concat_axis=0,
+            tiled=True,
+        ),
+        axis=0,
+    )
+    (layer_grad,) = norm_call(
+        input_back_kernel,
+        "input_back",
+        all_rows,
+        model_width,
+        [own, by_x, by_y, tokens.reshape(all_rows, model_width), d_middle],
+        [gain_vals[:1]],
+        [jnp.float32],
+    )
+    layer_grad = layer_grad.reshape(tokens.shape)
+    qkv_all, out_all, qkv_product = renew_heads(
+        heads_grad,
+        (attn_in, attn_in_mom, attn_in_avg),
+        (attn_out, attn_out_mom, attn_out_avg),
+        rate_mat,
+    )
+    gu_new, gu_mom, gu_avg, gu_copy, gu_product = gu_all
+    down_new, down_mom, down_avg, down_copy, _ = down_all
+    out_new, out_mom, out_avg, out_copy = out_all
+    qkv_new, qkv_mom, qkv_avg, qkv_copy = qkv_all
+    own_gains = low(gains).astype(jnp.float32)
+    sum_gain = jnp.stack(
+        [
+            qkv_product[:, 0] / own_gains[0],
+            sum_gains[0],
+            gu_product[:, 0] / own_gains[2],
+            sum_gains[1],
+        ]
+    )
+    gain_new, gain_mom, gain_avg, gain_copy = renew(
+        gains, gains_mom, gains_avg, sum_gain, rate_gain
+    )
+    return (
+        layer_out,
+        layer_grad,
+        qkv_new,
+        qkv_mom,
+        qkv_avg,
+        qkv_copy,
+        out_new,
+        out_mom,
+        out_avg,
+        out_copy,
+        gu_new,
+        gu_mom,
+        gu_avg,
+        gu_copy,
+        down_new,
+        down_mom,
+        down_avg,
+        down_copy,
+        gain_new,
+        gain_mom,
+        gain_avg,
+        gain_copy,
+    )
+
+
 def solution(mesh):
     placed = (
         P(None, ("grp", "seq"), None),
@@ -358,8 +1257,9 @@
         P(("grp", "seq"), None),
         P(None, ("grp", "seq")),
     )
+    heads_fit = mesh.shape["seq"] == HEADS
     return jax.shard_map(
-        local,
+        by_heads if heads_fit else by_rows,
         mesh=mesh,
         in_specs=placed,
         out_specs=(

time: 2400 us -> 928 us (0.39)
  waiting for transfers between devices: 1700 us -> 240 us
  Pallas kernels: 0 us -> 112 us
  other arithmetic: 147 us -> 69.6 us
  starting transfers between devices: 9.98 us -> 84.3 us
  local copies, waits for them, and re-layouts: 201 us -> 144 us
  matrix products: 257 us -> 215 us
    all_to_all x2 -> x8, waiting for transfers between devices: 915 us -> 36.9 us  [the longest x6 21.1 us: exchange(): return lax.all_to_all(field, 'seq', split_axis=0, concat_axis=0, tiled=True)]
    all_gather x6 -> x4, waiting for transfers between devices: 441 us -> 0.2 us  [gather_planes(): return lax.all_gather(field, 'grp', axis=0, tiled=True)]
    reduce_scatter x7 -> x5, waiting for transfers between devices: 347 us -> 1.35 us  [sum_planes(): return lax.psum_scatter(field, 'grp', scatter_dimension=0, tiled=True)]
    ppermute x0 -> x55, waiting for transfers between devices: none -> 201 us  [permute(): return lax.ppermute(field, 'seq', [(i, i ^ offset) for i in range(count)])]
    pallas_call x0 -> x13, Pallas kernels: none -> 112 us  [the longest x2 26.3 us: renew_wide(): pl.pallas_call(functools.partial(renew_parts_kernel, rate), grid=(count,...]
    dot_general x10 -> x5, matrix products: 112 us -> 51.3 us  [dot(): return jnp.dot(left, right, preferred_element_type=jnp.float32)]
    concatenate x3 -> x9, local copies, waits for them, and re-layouts: 65.7 us -> 11.3 us  [the longest x5 4.25 us: gather_mine(): return jnp.concatenate([field, by_x, by_y] + far, axis=0)]
    ppermute x0 -> x55, starting transfers between devices: none -> 46.2 us  [permute(): return lax.ppermute(field, 'seq', [(i, i ^ offset) for i in range(count)])]
  transfers between devices with their start and end apart: 17 -> 72, of which waited for: 11 -> 41; matrix products, arithmetic and copies ran while one was open for 16% -> 42% of each run, Pallas kernels for 0% -> 12%
where the time goes in v2:
time: 928 us; the launch traced here: 917 us
  waiting for transfers between devices  240 us (26%)
  matrix products  215 us (23%)
  local copies, waits for them, and re-layouts  144 us (16%)
  Pallas kernels  112 us (12%)
  starting transfers between devices  84.3 us (9%)
  other arithmetic  69.6 us (7%)
  blocking collectives  35.8 us (4%)
  between operations  14.8 us (2%)
    ppermute x55, waiting for transfers between devices, permute(): return lax.ppermute(field, 'seq', [(i, i ^ offset) for i in range(count)])  201 us
    dot_general x8, matrix products, contract_rows(): lax.dot_general(left, right, (((0,), (0,)), ((), ())), preferred_element_...  83.7 us
    dot_general x16, matrix products, contract_cols(): lax.dot_general(left, right, (((1,), (1,)), ((), ())), preferred_element_...  80.3 us
    dot_general x5, matrix products, dot(): return jnp.dot(left, right, preferred_element_type=jnp.float32)  51.3 us
    ppermute x55, starting transfers between devices, permute(): return lax.ppermute(field, 'seq', [(i, i ^ offset) for i in range(count)])  46.2 us
    cond x121, local copies, waits for them, and re-layouts  40.4 us
    all_to_all x1, blocking collectives, exchange(): return lax.all_to_all(field, 'seq', split_axis=0, concat_axis=0, tiled=True)  35.8 us
    all_to_all x6, starting transfers between devices, exchange(): return lax.all_to_all(field, 'seq', split_axis=0, concat_axis=0, tiled=True)  26.6 us
  transfers between devices with their start and end apart: 72, of which 41 were waited for; matrix products, arithmetic and copies ran while one was open for 42% of the time, Pallas kernels for 12%

profile of v2, /device:TPU:0, one launch (start us, length us, event | category | flops | bytes accessed | tf_op | source)
XLA Modules:
  0.0 916.9 jit_solution(13426367014934881296)
XLA Ops:
  46.7 15.8 %all-to-all-done.5 = bf16[32,4,72]{2,1,0:T(4,128)(2,1)S(1)} async-done(((bf16[32,4,72]{2,1,0:T(4,128)(2,1)}), bf16[32,4,72]{2,1,0:T(4,128)(2,1)S(1)}, u32[]{:S(2)}, u32[]{:S(2)}) %all-to-all-start.5) | async-done | bytes 18464 | tf_op jit(solution)/shard_map/all_to_all | solution.py:901
  65.5 35.8 %all_to_all.41 = bf16[8,72,2304]{2,1,0:T(8,128)(2,1)} all-to-all(bf16[8,72,2304]{2,1,0:T(8,128)(2,1)S(1)} %spread.7), channel_id=1, replica_groups=mesh['grp'=4,'seq'=8] {'seq'}, dimensions={0} | all-to-all | bytes 5308416 | tf_op jit(solution)/shard_map/all_to_all | solution.py:780
  134.1 52.0 %conditional.11 = (bf16[384,1152]{1,0:T(8,128)(2,1)}, bf16[192,1152]{1,0:T(8,128)(2,1)}, f32[1152]{0:T(1024)S(1)}, f32[1152]{0:T(1024)}, bf16[2,1152,256]{2,1,0:...) conditional(s32[]{:T(128)} %convert_element_type.368, ...), branch_computations={%region_2.3_spmd, %region_3.6_spmd} | conditional | flops 8208287744 | bytes 141258256 | solution.py:785
  188.3 128.0 %conditional.12 = (f32[288,2304]{1,0:T(8,128)}, f32[288,2304]{1,0:T(8,128)}, bf16[2304,2304]{1,0:T(8,128)(2,1)}, bf16[288,1536]{0,1:T(8,128)(2,1)}, bf16[288,768]{0,1:T(8,128)(2,1)S(1)}) conditional(s32[]{:T(128)} %convert_element_type.368, () %tuple.116, (bf16[1152,256]{1,0:T(8,128)(2,1)}, bf16[2304,768]{1,0:T(8,128)(2,1)}, ...), branch_computations={%region_6.7_spmd, %region_7.8_spmd} | conditional | flops 2755067904 | bytes 197480992 | solution.py:785
  263.0 25.0 %collective-permute-done.11 = bf16[288,2304]{1,0:T(8,128)(2,1)S(1)} collective-permute-done((bf16[288,2304]{1,0:T(8,128)(2,1)S(1)}, bf16[288,2304]{1,0:T(8,128)(2,1)S(1)}, u32[]{:S(2)}, u32[]{:S(2)}) %collective-permute-start.11) | collective-permute-done | bytes 1327136 | tf_op jit(solution)/shard_map/cond/branch_1_fun/ppermute | solution.py:351
  316.3 40.7 %conditional.13 = (f32[2304,2304]{1,0:T(8,128)}, bf16[2304,1152]{1,0:T(8,128)(2,1)}) conditional(s32[]{:T(128)} %convert_element_type.368, () %tuple.115, (bf16[2304,2304]{1,0:T(8,128)(2,1)}, bf16[2304,2304]{1,0:T(8,128)(2,1)}) %tuple.123), branch_computations={%region_8.9_spmd, %region_9.10_spmd} | conditional | flops 24487723008 | bytes 153944112 | solution.py:785
  316.3 32.0 %fusion.114 = f32[2304,2304]{1,0:T(8,128)S(1)} fusion(bf16[2304,2304]{1,0:T(8,128)(2,1)} %get-tuple-element.209, bf16[2304,2304]{1,0:T(8,128)(2,1)} %get-tuple-element.210), kind=kOutput, calls=%fused_computation.278 | convolution fusion | flops 24461180928 | bytes 42467328 | tf_op jit(solution)/shard_map/cond/branch_1_fun/dot_general | solution.py:812
  357.2 51.6 %conditional.14 = (f32[288,1536]{1,0:T(8,128)}) conditional(s32[]{:T(128)} %convert_element_type.368, () %tuple.124, (bf16[2304,1152]{1,0:T(8,128)(2,1)}, bf16[1536,1152]{1,0:T(8,128)(2,1)}) %tuple.125), branch_computations={%region_10.11_spmd, %region_11.12_spmd} | conditional | flops 8171864064 | bytes 83165464 | solution.py:785
  388.4 18.5 %collective-permute-done.26 = bf16[288,1536]{1,0:T(8,128)(2,1)S(1)} collective-permute-done((bf16[288,1536]{1,0:T(8,128)(2,1)S(1)}, bf16[288,1536]{1,0:T(8,128)(2,1)S(1)}, u32[]{:S(2)}, u32[]{:S(2)}) %collective-permute-start.26) | collective-permute-done | bytes 884768 | tf_op jit(solution)/shard_map/cond/branch_1_fun/ppermute | solution.py:351
  408.9 79.0 %conditional.15 = (f32[288,768]{1,0:T(8,128)S(1)}, f32[288,1]{0,1:T(1,128)}, bf16[288,1536]{1,0:T(8,128)(2,1)}, bf16[288,1536]{1,0:T(8,128)(2,1)}, bf16[288,1536...) conditional(s32[]{:T(128)} %convert_element_type.368, () %tuple.114, ...), branch_computations={%region_12.13_spmd, %region_13.18_spmd} | conditional | flops 8171643904 | bytes 116460360 | solution.py:785
  488.8 39.3 %conditional.16 = (bf16[2304,1536]{1,0:T(8,128)(2,1)}, bf16[1536,1152]{1,0:T(8,128)(2,1)}) conditional(s32[]{:T(128)} %convert_element_type.368, () %tuple.113, (bf16[288,1536]{1,0:T(8,128)(2,1)}, bf16[288,1536]{1,0:T(8,128)(2,1)}, bf16[288,1536]{1,0:T(8,128)(2,1)}, bf16[2304,1152]{1,0:T(8,128)(2,1)}) %tuple.127), branch_computations={%region_18.19_spmd, %region_19.20_spmd} | conditional | flops 8155496448 | bytes 53084296 | solution.py:785
  513.6 14.5 %convolution_convert_fusion.8 = bf16[1536,1152]{1,0:T(8,128)(2,1)} fusion(bf16[2304,1536]{1,0:T(8,128)(2,1)} %constant_dynamic-update-slice_fusion.16, bf16[2304,1152]{1,0:T(8,128)(2,1)} %get-tuple-element.223), kind=kOutput, calls=%fused_computation.56 | convolution fusion | flops 8155496448 | bytes 15925248 | tf_op jit(solution)/shard_map/cond/branch_1_fun/dot_general | solution.py:60
  528.2 77.2 %conditional.17 = (bf16[2304,2304]{1,0:T(8,128)(2,1)}, bf16[288,2304]{1,0:T(8,128)(2,1)}, bf16[288,2304]{1,0:T(8,128)(2,1)}, bf16[288,2304]{1,0:T(8,128)(2,1)}, ...) conditional(s32[]{:T(128)} %convert_element_type.368, () %tuple.112, ...), branch_computations={%region_21.22_spmd, %region_22.23_spmd} | conditional | flops 48940941312 | bytes 188448928 | solution.py:785
  528.2 25.2 %glu_back.1 = bf16[2304,2304]{1,0:T(8,128)(2,1)} custom-call(bf16[2304,1536]{1,0:T(8,128)(2,1)} %get-tuple-element.226.left0_ref, bf16[2304,768]{1,0:T(8,128)(2,1)} %get-tuple-element.227.left1_ref, bf16[1536,1152]{1,0:T(8,128)(2,1)} %get-tuple-element.228.w0_ref, bf16[768,1152]{1,0:T(8,128)(2,1)} %get-tuple-element.229.w1_ref, ...), custom_call_target="tpu_custom_call" | custom-call | flops 12230590464 | bytes 42467328 | tf_op jit(solution)/shard_map/cond/branch_1_fun/glu_back/pallas_call | solution.py:564
  553.4 14.5 %convolution_convert_fusion.10 = bf16[1152,2304]{1,0:T(8,128)(2,1)S(1)} fusion(bf16[2304,2304]{1,0:T(8,128)(2,1)S(1)} %copy-done.82, bf16[2304,2304]{1,0:T(8,128)(2,1)} %glu_back.1), kind=kOutput, calls=%fused_computation.69 | convolution fusion | flops 12233244672 | bytes 21233664 | tf_op jit(solution)/shard_map/cond/branch_1_fun/dot_general | solution.py:66
  568.2 19.2 %fusion.28 = bf16[2304,1152]{1,0:T(8,128)(2,1)} fusion(bf16[2304,2304]{1,0:T(8,128)(2,1)} %get-tuple-element.232, bf16[2304,2304]{1,0:T(8,128)(2,1)} %glu_back.1), kind=kOutput, calls=%fused_computation.73 | convolution fusion | flops 12233244672 | bytes 21233664 | tf_op jit(solution)/shard_map/cond/branch_1_fun/dot_general | solution.py:60
  587.4 15.5 %add_convert_fusion.8 = bf16[1152,2304]{1,0:T(8,128)(2,1)S(1)} fusion(bf16[1152,2304]{1,0:T(8,128)(2,1)} %collective-permute-done.43, bf16[2304,2304]{1,0:T(8,128)(2,1)S(1)} %copy-done.82, bf16[2304,2304]{1,0:T(8,128)(2,1)} %glu_back.1), kind=kOutput, calls=%fused_computation.72 | convolution fusion | flops 12243861504 | bytes 26542080 | tf_op jit(solution)/shard_map/cond/branch_1_fun/dot_general | solution.py:66
  606.1 59.5 %conditional.18 = (bf16[2304,1152]{1,0:T(8,128)(2,1)}, f32[288,2304]{1,0:T(8,128)}, bf16[288,2304]{1,0:T(8,128)(2,1)}, f32[2304]{0:T(1024)S(1)}, bf16[8,72,1152]{2,1,0:T(8,128)(2,1)}) conditional(s32[]{:T(128)} %convert_element_type.368, () %tuple.111, (bf16[288,2304]{1,0:T(8,128)(2,1)}, bf16[288,2304]{1,0:T(8,128)(2,1)}, ...), branch_computations={%region_24.25_spmd, %region_25.26_spmd} | conditional | flops 12257132544 | bytes 76585216 | solution.py:785
  629.7 19.3 %convolution_convert_fusion.16 = bf16[2304,1152]{1,0:T(8,128)(2,1)} fusion(bf16[2304,2304]{1,0:T(8,128)(2,1)} %get-tuple-element.240, bf16[2304,2304]{1,0:T(8,128)(2,1)} %get-tuple-element.243), kind=kOutput, calls=%fused_computation.168 | convolution fusion | flops 12233244672 | bytes 21233664 | tf_op jit(solution)/shard_map/cond/branch_1_fun/dot_general | solution.py:60
  667.4 50.9 %conditional.19 = (bf16[1152,2304]{1,0:T(8,128)(2,1)}, bf16[2,144,2304]{2,1,0:T(8,128)(2,1)}, f32[1,32,72]{2,1,0:T(8,128)}) conditional(s32[]{:T(128)} %convert_element_type.368, () %tuple.110, (bf16[288,2304]{1,0:T(8,128)(2,1)}, f32[288,1]{0,1:T(1,128)}, f32[288,1536]{1,0:T(8,128)}, f32[1,1536]{1,0:T(1,128)}, f32[288,768]{1,0:T(8,128)S(1)}, ...), branch_computations={%region_26.27_spmd, %region_27.30_spmd} | conditional | flops 5308416 | bytes 71771416 | solution.py:785
  718.2 84.5 %conditional.20 = (bf16[1152,512]{1,0:T(8,128)(2,1)}, bf16[1152,2304]{1,0:T(8,128)(2,1)}, bf16[2304,768]{1,0:T(8,128)(2,1)}, bf16[8,72,1152]{2,1,0:T(8,128)(2,1)}, bf16[8,72,1152]{2,1,0:T(8,128)(2,1)}) conditional(s32[]{:T(128)} %convert_element_type.368, () %tuple.132, (bf16[2304,768]{1,0:T(8,128)(2,1)}, bf16[1152,2304]{1,0:T(8,128)(2,1)}, ...), branch_computations={%region_32.33_spmd, %region_33.34_spmd} | conditional | flops 20440645632 | bytes 300089568 | solution.py:785
  733.1 21.6 %attend_back.1 = (f32[2,1152,256]{2,1,0:T(8,128)S(1)}, f32[2,1152,256]{2,1,0:T(8,128)S(1)}, f32[2,1152,256]{2,1,0:T(8,128)}) custom-call(bf16[2,1152,256]{2,1,0:T(8,128)(2,1)} %get-tuple-element.269.q_ref, bf16[2,1152,256]{2,1,0:T(8,128)(2,1)} %get-tuple-element.270.k_ref, bf16[2,1152,256]{2,1,0:T(8,128)(2,1)} %get-tuple-element.271.v_ref, ...), custom_call_target="tpu_custom_call" | custom-call | flops 6794772480 | bytes 11796480 | tf_op jit(solution)/shard_map/cond/branch_1_fun/attend_back/pallas_call | solution.py:767
  802.8 44.2 %conditional.21 = (bf16[288,2304]{1,0:T(8,128)(2,1)}, bf16[288,2304]{1,0:T(8,128)(2,1)}, bf16[288,2304]{1,0:T(8,128)(2,1)}, bf16[8,72,1152]{2,1,0:T(8,128)(2,1)}) conditional(s32[]{:T(128)} %convert_element_type.368, () %tuple.131, (bf16[2304,768]{1,0:T(8,128)(2,1)}, bf16[1152,512]{1,0:T(8,128)(2,1)}, bf16[1152,2304]{1,0:T(8,128)(2,1)}, ...), branch_computations={%region_34.35_spmd, %region_35.36_spmd} | conditional | flops 2739142656 | bytes 61931692 | solution.py:785
  850.3 18.4 %renew.2 = (f32[72,18432]{1,0:T(8,128)}, f32[72,18432]{1,0:T(8,128)}, f32[72,18432]{1,0:T(8,128)}, bf16[72,18432]{1,0:T(8,128)(2,1)}, f32[72,1]{1,0:T(8,128)S(1)}) custom-call(f32[72,18432]{1,0:T(8,128)S(1)} %copy-done, f32[72,18432]{1,0:T(8,128)} %m_ref.2, f32[72,18432]{1,0:T(8,128)} %a_ref.2, bf16[8,72,1152]{2,1,0:T(8,128)(2,1)} %get-tuple-element.474.refs_0_, ...), custom_call_target="tpu_custom_call" | custom-call | flops 10616832 | bytes 37158912 | tf_op jit(solution)/shard_map/renew/pallas_call | solution.py:495
  (532 shorter events, 625.7 us)
Async XLA Ops:
  15.8 110.4 %all-gather.5.cloned.1.call-start = ((), (), s32[]{:S(2)}) async-start(), calls=%async_computation.14 | async-start | bytes 4423680 | tf_op jit(solution)/shard_map/all_gather | solution.py:794
  31.1 31.6 %collective-permute-start.49 = (bf16[288,2304]{1,0:T(8,128)(2,1)S(1)}, bf16[288,2304]{1,0:T(8,128)(2,1)}, u32[]{:S(2)}, u32[]{:S(2)}) collective-permute-start(bf16[288,2304]{1,0:T(8,128)(2,1)S(1)} %bitcast.121), channel_id=1, source_target_pairs={{0,4},{1,5},{2,6},{3,7},{4,0},{5,1},{6,2},{7,3},{8,12},{9,13},{10,... | collective-permute-start | bytes 3981320 | tf_op jit(solution)/shard_map/ppermute | solution.py:351
  31.7 31.0 %collective-permute-start.48 = (bf16[288,2304]{1,0:T(8,128)(2,1)S(1)}, bf16[288,2304]{1,0:T(8,128)(2,1)}, u32[]{:S(2)}, u32[]{:S(2)}) collective-permute-start(bf16[288,2304]{1,0:T(8,128)(2,1)S(1)} %bitcast.122), channel_id=1, source_target_pairs={{0,2},{1,3},{2,0},{3,1},{4,6},{5,7},{6,4},{7,5},{8,10},{9,11},{10,... | collective-permute-start | bytes 3981320 | tf_op jit(solution)/shard_map/ppermute | solution.py:351
  45.3 271.0 %all-gather.7.cloned.1.call-start = ((), (), s32[]{:S(2)}) async-start(), calls=%async_computation.15 | async-start | bytes 13271040 | tf_op jit(solution)/shard_map/all_gather | solution.py:794
  101.3 255.9 %all-gather.11.cloned.1.call-start = ((), (), s32[]{:S(2)}) async-start(), calls=%async_computation.17 | async-start | bytes 4423680 | tf_op jit(solution)/shard_map/all_gather | solution.py:794
  186.1 222.8 %all-gather.9.cloned.1.call-start = ((), (), s32[]{:S(2)}) async-start(), calls=%async_computation.16 | async-start | bytes 2211840 | tf_op jit(solution)/shard_map/all_gather | solution.py:794
  186.7 341.5 %reduce-scatter.6.cloned.1.call-start = ((), (), s32[]{:S(2)}) async-start(), calls=%async_computation.18 | async-start | bytes 2211840 | tf_op jit(solution)/shard_map/reduce_scatter | solution.py:798
  221.7 30.4 %collective-permute-start.7 = (bf16[288,2304]{1,0:T(8,128)(2,1)}, bf16[288,2304]{1,0:T(8,128)(2,1)}, u32[]{:S(2)}, u32[]{:S(2)}) collective-permute-start(bf16[288,2304]{1,0:T(8,128)(2,1)} %pad_maximum_fusion), channel_id=1, source_target_pairs={{0,2},{1,3},{2,0},{3,1},{4,6},{5,7},{6,4},{7,5},{8,10},{9,11},{10,... | collective-permute-start | bytes 3981320 | tf_op jit(solution)/shard_map/cond/branch_1_fun/ppermute | solution.py:351
  223.2 30.4 %collective-permute-start.9 = (bf16[288,2304]{1,0:T(8,128)(2,1)}, bf16[288,2304]{1,0:T(8,128)(2,1)}, u32[]{:S(2)}, u32[]{:S(2)}) collective-permute-start(bf16[288,2304]{1,0:T(8,128)(2,1)} %pad_maximum_fusion.1), channel_id=1, source_target_pairs={{0,4},{1,5},{2,6},{3,7},{4,0},{5,1},{6,2},{7,3},{8,12},{9,13},{10,... | collective-permute-start | bytes 3981320 | tf_op jit(solution)/shard_map/cond/branch_1_fun/ppermute | solution.py:351
  258.9 29.2 %collective-permute-start.11 = (bf16[288,2304]{1,0:T(8,128)(2,1)S(1)}, bf16[288,2304]{1,0:T(8,128)(2,1)S(1)}, u32[]{:S(2)}, u32[]{:S(2)}) collective-permute-start(bf16[288,2304]{1,0:T(8,128)(2,1)S(1)} %get-tuple-element.206), channel_id=1, source_target_pairs={{0,4},{1,5},{2,6},{3,7},{4,0},{5,1},{6,2},{7,3},{8,12},{9,13},{10,... | collective-permute-start | bytes 3981320 | tf_op jit(solution)/shard_map/cond/branch_1_fun/ppermute | solution.py:351
  260.4 29.7 %collective-permute-start.10 = (bf16[288,2304]{1,0:T(8,128)(2,1)S(1)}, bf16[288,2304]{1,0:T(8,128)(2,1)S(1)}, u32[]{:S(2)}, u32[]{:S(2)}) collective-permute-start(bf16[288,2304]{1,0:T(8,128)(2,1)S(1)} %get-tuple-element.206), channel_id=1, source_target_pairs={{0,2},{1,3},{2,0},{3,1},{4,6},{5,7},{6,4},{7,5},{8,10},{9,11},{10,... | collective-permute-start | bytes 3981320 | tf_op jit(solution)/shard_map/cond/branch_1_fun/ppermute | solution.py:351
  487.9 117.6 %reduce-scatter.8.cloned.1.call-start = ((), (), s32[]{:S(2)}) async-start(), calls=%async_computation.19 | async-start | bytes 4423680 | tf_op jit(solution)/shard_map/reduce_scatter | solution.py:798
  528.1 190.1 %reduce-scatter.10.cloned.1.call-start = ((), (), s32[]{:S(2)}) async-start(), calls=%async_computation.20 | async-start | bytes 6635520 | tf_op jit(solution)/shard_map/reduce_scatter | solution.py:798
  605.4 197.4 %reduce-scatter.12.cloned.1.call-start = ((), (), s32[]{:S(2)}) async-start(), calls=%async_computation.21 | async-start | bytes 6635520 | tf_op jit(solution)/shard_map/reduce_scatter | solution.py:798
  627.7 30.9 %collective-permute-start.17 = (bf16[288,2304]{1,0:T(8,128)(2,1)S(1)}, bf16[288,2304]{1,0:T(8,128)(2,1)S(1)}, u32[]{:S(2)}, u32[]{:S(2)}) collective-permute-start(bf16[288,2304]{1,0:T(8,128)(2,1)S(1)} %pad_maximum_fusion.13), channel_id=1, source_target_pairs={{0,2},{1,3},{2,0},{3,1},{4,6},{5,7},{6,4},{7,5},{8,10},{9,11},{10,... | collective-permute-start | bytes 3981320 | tf_op jit(solution)/shard_map/cond/branch_1_fun/ppermute | solution.py:351
  628.3 30.4 %collective-permute-start.18 = (bf16[288,2304]{1,0:T(8,128)(2,1)S(1)}, bf16[288,2304]{1,0:T(8,128)(2,1)S(1)}, u32[]{:S(2)}, u32[]{:S(2)}) collective-permute-start(bf16[288,2304]{1,0:T(8,128)(2,1)S(1)} %pad_maximum_fusion.14), channel_id=1, source_target_pairs={{0,4},{1,5},{2,6},{3,7},{4,0},{5,1},{6,2},{7,3},{8,12},{9,13},{10,... | collective-permute-start | bytes 3981320 | tf_op jit(solution)/shard_map/cond/branch_1_fun/ppermute | solution.py:351
  666.2 204.4 %reduce-scatter.14.cloned.1.call-start = ((), (), s32[]{:S(2)}) async-start(), calls=%async_computation.22 | async-start | bytes 4423680 | tf_op jit(solution)/shard_map/reduce_scatter | solution.py:798
  667.4 31.5 %collective-permute-start.1 = (bf16[288,2304]{1,0:T(8,128)(2,1)}, bf16[288,2304]{1,0:T(8,128)(2,1)}, u32[]{:S(2)}, u32[]{:S(2)}) collective-permute-start(bf16[288,2304]{1,0:T(8,128)(2,1)} %get-tuple-element.257), channel_id=1, source_target_pairs={{0,4},{1,5},{2,6},{3,7},{4,0},{5,1},{6,2},{7,3},{8,12},{9,13},{10,... | collective-permute-start | bytes 3981320 | tf_op jit(solution)/shard_map/cond/branch_1_fun/ppermute | solution.py:351
  668.7 30.2 %collective-permute-start = (bf16[288,2304]{1,0:T(8,128)(2,1)}, bf16[288,2304]{1,0:T(8,128)(2,1)}, u32[]{:S(2)}, u32[]{:S(2)}) collective-permute-start(bf16[288,2304]{1,0:T(8,128)(2,1)} %get-tuple-element.257), channel_id=1, source_target_pairs={{0,2},{1,3},{2,0},{3,1},{4,6},{5,7},{6,4},{7,5},{8,10},{9,11},{10,... | collective-permute-start | bytes 3981320 | tf_op jit(solution)/shard_map/cond/branch_1_fun/ppermute | solution.py:351
  718.2 39.3 %all-to-all-start.1 = ((bf16[8,72,1152]{2,1,0:T(8,128)(2,1)}), bf16[8,72,1152]{2,1,0:T(8,128)(2,1)}, u32[]{:S(2)}, u32[]{:S(2)}) async-start(bf16[8,72,1152]{2,1,0:T(8,128)(2,1)} %bitcast.143), calls=%async_computation.1 | async-start | bytes 2654208 | tf_op jit(solution)/shard_map/cond/branch_1_fun/all_to_all | solution.py:780
  773.0 29.7 %collective-permute-start.46 = (bf16[1152,2304]{1,0:T(8,128)(2,1)}, bf16[1152,2304]{1,0:T(8,128)(2,1)}, u32[]{:S(2)}, u32[]{:S(2)}) collective-permute-start(bf16[1152,2304]{1,0:T(8,128)(2,1)} %convolution_convert_fusion.17), channel_id=1, source_target_pairs={{0,1},{1,0},{2,3},{3,2},{4,5},{5,4},{6,7},{7,6},{8,9},{9,8},{10,11... | collective-permute-start | bytes 15925256 | tf_op jit(solution)/shard_map/cond/branch_1_fun/ppermute | solution.py:351
  773.1 29.6 %all-to-all-start.2 = ((bf16[8,72,1152]{2,1,0:T(8,128)(2,1)}), bf16[8,72,1152]{2,1,0:T(8,128)(2,1)}, u32[]{:S(2)}, u32[]{:S(2)}) async-start(bf16[8,72,1152]{2,1,0:T(8,128)(2,1)} %get-tuple-element.297), calls=%async_computation.2 | async-start | bytes 2654208 | tf_op jit(solution)/shard_map/cond/branch_1_fun/all_to_all | solution.py:780
  847.0 36.9 %collective-permute-start.53 = (bf16[288,2304]{1,0:T(8,128)(2,1)}, bf16[288,2304]{1,0:T(8,128)(2,1)}, u32[]{:S(2)}, u32[]{:S(2)}) collective-permute-start(bf16[288,2304]{1,0:T(8,128)(2,1)} %get-tuple-element.471), channel_id=1, source_target_pairs={{0,2},{1,3},{2,0},{3,1},{4,6},{5,7},{6,4},{7,5},{8,10},{9,11},{10,... | collective-permute-start | bytes 3981320 | tf_op jit(solution)/shard_map/ppermute | solution.py:351
  847.4 36.6 %collective-permute-start.54 = (bf16[288,2304]{1,0:T(8,128)(2,1)}, bf16[288,2304]{1,0:T(8,128)(2,1)}, u32[]{:S(2)}, u32[]{:S(2)}) collective-permute-start(bf16[288,2304]{1,0:T(8,128)(2,1)} %get-tuple-element.472), channel_id=1, source_target_pairs={{0,4},{1,5},{2,6},{3,7},{4,0},{5,1},{6,2},{7,3},{8,12},{9,13},{10,... | collective-permute-start | bytes 3981320 | tf_op jit(solution)/shard_map/ppermute | solution.py:351
  (131 other events, 1361.0 us)
Sparse Core Ops, SparseCore 0:
  30.5 70.0 all-gather.4
  102.1 184.6 all-gather.6
  289.0 68.1 all-gather.10
  359.2 38.8 all-gather.8
  488.0 38.4 reduce-scatter.5
  528.7 65.8 reduce-scatter.7
  605.5 94.9 reduce-scatter.9
  703.3 95.3 reduce-scatter.11
  802.9 67.6 reduce-scatter.13

commit v3 on v2

--- a/solution.py
+++ b/solution.py
@@ -518,7 +518,9 @@
             w_ref, m_ref, a_ref = refs[3 * which : 3 * which + 3]
             outs = refs[6 + 4 * which : 10 + 4 * which]
             here = (slice(None), slice(block * HEAD, (block + 1) * HEAD))
-            gradient = g_ref[device, :, part * HEAD : (part + 1) * HEAD].astype(jnp.float32)
+            gradient = g_ref[device, : w_ref.shape[0], part * HEAD : (part + 1) * HEAD].astype(
+                jnp.float32
+            )
             results = renew(w_ref[here], m_ref[here], a_ref[here], gradient, rate)
             for out, result in zip(outs, results):
                 out[here] = result
@@ -541,6 +543,44 @@
         name="renew_heads",
     )(gradient, *attn_in, *attn_out)
     return results[:4], results[4:8], results[8]
+
+
+def glu_kernel(rows_ref, w_ref, gate_up_ref, hidden_ref):
+    width = hidden_ref.shape[1]
+    gate_up = jnp.dot(rows_ref[...], w_ref[...], preferred_element_type=jnp.float32)
+    gate_up_ref[...] = gate_up
+    gate, upper = gate_up[:, :width], gate_up[:, width:]
+    bent = jnp.tanh(GELU_SCALE * gate * (1.0 + 0.044715 * gate * gate))
+    hidden_ref[...] = (0.5 * gate * (1.0 + bent) * upper).astype(jnp.bfloat16)
+
+
+def glu_rows(field, weight):
+    rows, depth = field.shape
+    width = weight.shape[1] // 2
+    tile = rows // 6
+    return pl.pallas_call(
+        glu_kernel,
+        grid=(rows // tile,),
+        in_specs=[
+            pl.BlockSpec((tile, depth), lambda i: (i, 0)),
+            pl.BlockSpec(weight.shape, lambda i: (0, 0)),
+        ],
+        out_specs=[
+            pl.BlockSpec((tile, 2 * width), lambda i: (i, 0)),
+            pl.BlockSpec((tile, width), lambda i: (i, 0)),
+        ],
+        out_shape=[
+            jax.ShapeDtypeStruct((rows, 2 * width), jnp.float32),
+            jax.ShapeDtypeStruct((rows, width), jnp.bfloat16),
+        ],
+        cost_estimate=pl.CostEstimate(
+            flops=4 * rows * depth * width,
+            transcendentals=rows * width,
+            bytes_accessed=rows * (2 * depth + 10 * width) + 4 * depth * width,
+        ),
+        compiler_params=pltpu.CompilerParams(vmem_limit_bytes=VMEM_LIMIT),
+        name="glu",
+    )(field, weight)
 
 
 def glu_back_kernel(left0_ref, left1_ref, w0_ref, w1_ref, gate_up_ref, out_ref):
@@ -686,43 +726,64 @@
     )
 
 
-def capped_scores(q, k, key_ref, query_ref):
-    bent = jnp.tanh(across(k, q) * (HEAD ** (-0.5) / soft_cap))
+def attend_kernel(q_ref, k_ref, v_ref, key_ref, query_ref, out_ref, weights_ref, slopes_ref):
+    bent = jnp.tanh(across(k_ref[0], q_ref[0]) * (HEAD ** (-0.5) / soft_cap))
     key, query = key_ref[0][:, :1], query_ref[0]
     seg_k, seg_q = key & 15, query & 15
     seen = ((key >> 4) <= (query >> 4)) & ((seg_k == 0) | (seg_k == seg_q))
-    return bent, jnp.where(seen, soft_cap * bent, -1e30)
-
-
-def attend_kernel(q_ref, k_ref, v_ref, key_ref, query_ref, out_ref, norm_ref):
-    _, capped = capped_scores(q_ref[0], k_ref[0], key_ref, query_ref)
+    capped = jnp.where(seen, soft_cap * bent, -1e30)
     top = jnp.max(capped, axis=0, keepdims=True)
     powers = jnp.exp(capped - top)
-    total = jnp.sum(powers, axis=0, keepdims=True)
-    weights = (powers * (1.0 / total)).astype(jnp.bfloat16)
-    norm_ref[0] = top + jnp.log(total)
-    out_ref[0] = down(weights, v_ref[0]).astype(jnp.bfloat16)
+    weights = powers * (1.0 / jnp.sum(powers, axis=0, keepdims=True))
+    weights_low = weights.astype(jnp.bfloat16)
+    weights_ref[0] = weights_low
+    slopes_ref[0] = (weights * (1.0 - bent * bent)).astype(jnp.bfloat16)
+    out_ref[0] = down(weights_low, v_ref[0]).astype(jnp.bfloat16)
 
 
 def attend_back_kernel(
-    q_ref, k_ref, v_ref, key_ref, query_ref, norm_ref, d_out_ref, dq_ref, dk_ref, dv_ref
+    q_ref,
+    k_ref,
+    v_ref,
+    weights_ref,
+    slopes_ref,
+    cosine_ref,
+    sine_ref,
+    core_ref,
+    d_out_ref,
+    dq_ref,
+    keep_ref,
+    send_ref,
+    dk_sum,
+    dv_sum,
 ):
     q, k, v, d_out = q_ref[0], k_ref[0], v_ref[0], d_out_ref[0]
-    bent, capped = capped_scores(q, k, key_ref, query_ref)
-    weights = jnp.exp(capped - norm_ref[0])
+    weights = weights_ref[0]
     d_weights = across(v, d_out)
-    inner = jnp.sum(weights * d_weights, axis=0, keepdims=True)
-    d_raw = (weights * (d_weights - inner) * (1.0 - bent * bent)).astype(jnp.bfloat16)
+    inner = jnp.sum(weights.astype(jnp.float32) * d_weights, axis=0, keepdims=True)
+    d_raw = (slopes_ref[0].astype(jnp.float32) * (d_weights - inner)).astype(jnp.bfloat16)
     scale = HEAD ** (-0.5)
 
     @pl.when(pl.program_id(1) == 0)
     def _():
-        dk_ref[...] = jnp.zeros_like(dk_ref)
-        dv_ref[...] = jnp.zeros_like(dv_ref)
-
-    dq_ref[0] = down(d_raw, k) * scale
-    dk_ref[0] += jnp.dot(d_raw, q, preferred_element_type=jnp.float32) * scale
-    dv_ref[0] += jnp.dot(weights.astype(jnp.bfloat16), d_out, preferred_element_type=jnp.float32)
+        dk_sum[...] = jnp.zeros_like(dk_sum)
+        dv_sum[...] = jnp.zeros_like(dv_sum)
+
+    dq = down(d_raw, k) * scale
+    half = HEAD // 2
+    cosine, sine = cosine_ref[0], sine_ref[0]
+    first, second = dq[:, :half], dq[:, half:]
+    dq_ref[0, :, :half] = (first * cosine + second * sine).astype(jnp.bfloat16)
+    dq_ref[0, :, half:] = (second * cosine - first * sine).astype(jnp.bfloat16)
+    dk_sum[...] += jnp.dot(d_raw, q, preferred_element_type=jnp.float32)
+    dv_sum[...] += jnp.dot(weights, d_out, preferred_element_type=jnp.float32)
+
+    @pl.when(pl.program_id(1) == pl.num_programs(1) - 1)
+    def _():
+        holds_keys = core_ref[:, :1] == 0
+        dk, dv = dk_sum[...] * scale, dv_sum[...]
+        keep_ref[0] = jnp.where(holds_keys, dk, dv)
+        send_ref[0] = jnp.where(holds_keys, dv, dk).astype(jnp.bfloat16)
 
 
 def attention_cost(micros, rows, products):
@@ -736,44 +797,54 @@
 def attention_specs(rows, tile):
     moving = pl.BlockSpec((1, tile, HEAD), lambda m, i: (m, i, 0))
     whole = pl.BlockSpec((1, rows, HEAD), lambda m, i: (m, 0, 0))
-    lane = pl.BlockSpec((1, 1, tile), lambda m, i: (m, 0, i))
-    places = [pl.BlockSpec((1, rows, 128), lambda m, i: (m, 0, 0)), lane]
-    return moving, whole, lane, places
+    scores = pl.BlockSpec((1, rows, tile), lambda m, i: (m, 0, i))
+    return moving, whole, scores
 
 
 def attend(q, k, v, places):
     micros, rows, _ = q.shape
     tile = rows // 3
-    moving, whole, lane, place_specs = attention_specs(rows, tile)
+    moving, whole, scores = attention_specs(rows, tile)
     return pl.pallas_call(
         attend_kernel,
         grid=(micros, rows // tile),
-        in_specs=[moving, whole, whole] + place_specs,
-        out_specs=[moving, lane],
-        out_shape=[
-            jax.ShapeDtypeStruct(q.shape, jnp.bfloat16),
-            jax.ShapeDtypeStruct((micros, 1, rows), jnp.float32),
+        in_specs=[
+            moving,
+            whole,
+            whole,
+            pl.BlockSpec((1, rows, 128), lambda m, i: (m, 0, 0)),
+            pl.BlockSpec((1, 1, tile), lambda m, i: (m, 0, i)),
         ],
+        out_specs=[moving, scores, scores],
+        out_shape=[jax.ShapeDtypeStruct(q.shape, jnp.bfloat16)]
+        + [jax.ShapeDtypeStruct((micros, rows, rows), jnp.bfloat16)] * 2,
         cost_estimate=attention_cost(micros, rows, 2),
         compiler_params=pltpu.CompilerParams(vmem_limit_bytes=VMEM_LIMIT),
         name="attend",
     )(q, k, v, *places)
 
 
-def attend_back(q, k, v, places, norm, d_out):
+def attend_back(q, k, v, weights, slopes, tables, core, d_out):
     micros, rows, _ = q.shape
     tile = rows // 3
-    moving, whole, lane, place_specs = attention_specs(rows, tile)
+    moving, whole, scores = attention_specs(rows, tile)
+    turning = pl.BlockSpec((1, tile, HEAD // 2), lambda m, i: (m, i, 0))
     return pl.pallas_call(
         attend_back_kernel,
         grid=(micros, rows // tile),
-        in_specs=[moving, whole, whole] + place_specs + [lane, moving],
+        in_specs=[moving, whole, whole, scores, scores, turning, turning]
+        + [pl.BlockSpec((1, 128), lambda m, i: (0, 0)), moving],
         out_specs=[moving, whole, whole],
-        out_shape=[jax.ShapeDtypeStruct(q.shape, jnp.float32)] * 3,
-        cost_estimate=attention_cost(micros, rows, 5),
+        out_shape=[
+            jax.ShapeDtypeStruct(q.shape, jnp.bfloat16),
+            jax.ShapeDtypeStruct(q.shape, jnp.float32),
+            jax.ShapeDtypeStruct(q.shape, jnp.bfloat16),
+        ],
+        scratch_shapes=[pltpu.VMEM((rows, HEAD), jnp.float32)] * 2,
+        cost_estimate=attention_cost(micros, rows, 4),
         compiler_params=pltpu.CompilerParams(vmem_limit_bytes=VMEM_LIMIT),
         name="attend_back",
-    )(q, k, v, *places, norm, d_out)
+    )(q, k, v, weights, slopes, *tables, core, d_out)
 
 
 def exchange(field):
@@ -957,15 +1028,19 @@
         queries = to_groups(low(turn(projected[:, :HEAD], cosine, sine)))
         keys = to_groups(jnp.where(key_core, kv_own, kv_other))
         values = to_groups(jnp.where(key_core, kv_other, kv_own))
-        mixed, norm = attend(queries, keys, values, places)
+        mixed, weights, slopes = attend(queries, keys, values, places)
         mixed, down_moved = tie((mixed, down_moved))
         mixed_rows = in_two(from_groups(mixed))
         down_rows = [
             part.reshape(-1, slice_width) for part in (down_moved[:, :cut], down_moved[:, cut:])
         ]
-        return down_rows, inverses, (queries, keys, values, norm), mixed_rows
-
-    down_rows, inverses, state, mixed_rows = in_order(attention, token_rows, w_heads, down_low)
+        turn_tables = [to_groups(cosine), to_groups(sine)]
+        state = (queries, keys, values, weights, slopes)
+        return down_rows, inverses, state, mixed_rows, turn_tables
+
+    down_rows, inverses, state, mixed_rows, turn_tables = in_order(
+        attention, token_rows, w_heads, down_low
+    )
     w_down0, w_down1 = gather_planes(down_rows[0]), gather_planes(down_rows[1])
 
     def attention_out(mixed_rows, w_heads, tokens, cotangent):
@@ -988,11 +1063,10 @@
     branch, middle, norm_rows, grad_parts = in_order(
         attention_out, mixed_rows, w_heads, tokens, cotangent
     )
-    queries, keys, values, norm = state
+    queries, keys, values, weights, slopes = state
 
     def feed_up(norm_rows, w_gu):
-        gate_up = dot(norm_rows, w_gu)
-        return gate_up, low(glu_part(gate_up[:, :slice_width], gate_up[:, slice_width:]))
+        return glu_rows(norm_rows, w_gu)
 
     gate_up, hidden = in_order(feed_up, norm_rows, w_gu)
 
@@ -1031,27 +1105,36 @@
     def feed_back_rows(second, first, gate_up, norm_rows, w_down0, w_down1, w_gu, down_part1):
         second, down_part1 = tie((second, down_part1))
         d_gate_up = glu_back_rows(second, first, w_down0, w_down1, gate_up)
-        blocks = pair_halves(*in_two(d_gate_up), w_gu)
+        moved = permute(low(contract_cols(d_gate_up[d_gate_up.shape[0] // 2 :], w_gu)), 1)
         grad_gate = low(contract_rows(norm_rows, d_gate_up[:, :slice_width]))
-        return d_gate_up, blocks, with_layout_constraint(grad_gate, Layout((0, 1))), down_part1
-
-    d_gate_up, d_norm_blocks, grad_gate, down_part1 = in_order(
+        return d_gate_up, moved, with_layout_constraint(grad_gate, Layout((0, 1))), down_part1
+
+    d_gate_up, d_norm_moved, grad_gate, down_part1 = in_order(
         feed_back_rows, second, first, gate_up, norm_rows, w_down0, w_down1, w_gu, down_part1
     )
     gate_part = sum_planes(grad_gate)
 
     def middle_back(
-        d_norm_blocks, d_gate_up, norm_rows, cotangent, branch, middle, down_part0, down_part1
+        d_norm_moved,
+        d_gate_up,
+        norm_rows,
+        cotangent,
+        branch,
+        middle,
+        w_heads,
+        w_gu,
     ):
-        d_gate_up, down_part0 = tie((d_gate_up, down_part0))
-        down_part = jnp.concatenate(
-            [part.reshape(seq_count, -1, slice_width) for part in (down_part0, down_part1)], axis=1
-        )
-        own, by_x, by_y = sum_far(*d_norm_blocks)
+        w_qkv = w_heads[:, : 2 * HEAD]
+        w_pair = jnp.concatenate([w_qkv, permute(w_qkv, 1)], axis=1)
+        total = add_low(
+            low(contract_cols(d_gate_up[: d_gate_up.shape[0] // 2], w_gu)), d_norm_moved
+        )
+        rows = total.shape[0] // 4
+        own, by_x, by_y = sum_far(*(total[at * rows : (at + 1) * rows] for at in range(4)))
         by_x, by_y, norm_rows = tie((by_x, by_y, norm_rows))
         by_x, by_y = permute(by_x, 2), permute(by_y, 4)
         grad_upper = low(contract_rows(norm_rows, d_gate_up[:, slice_width:]))
-        by_x, by_y, grad_upper = tie((by_x, by_y, grad_upper))
+        by_x, by_y, grad_upper, w_pair = tie((by_x, by_y, grad_upper, w_pair))
         d_middle, d_branch, d_gain_two = norm_call(
             middle_back_kernel,
             "middle_back",
@@ -1061,22 +1144,24 @@
             [gain_vals[1:2], gain_vals[2:3]],
             [jnp.float32, jnp.bfloat16, None],
         )
-        return grad_upper, d_middle, d_branch, d_gain_two[0], down_part
-
-    grad_upper, d_middle, d_branch, d_gain_two, down_part = in_order(
+        return grad_upper, d_middle, d_branch, d_gain_two[0], w_pair
+
+    grad_upper, d_middle, d_branch, d_gain_two, w_pair = in_order(
         middle_back,
-        d_norm_blocks,
+        d_norm_moved,
         d_gate_up,
         norm_rows,
         cotangent,
         branch,
         middle,
-        down_part0,
-        down_part1,
+        w_heads,
+        w_gu,
     )
     upper_part = sum_planes(grad_upper)
 
-    def output_rows(d_branch, middle, ffns, inverse, grad_parts):
+    core_row = jnp.broadcast_to(index % 2, (1, 128)).astype(jnp.int32)
+
+    def output_rows(d_branch, d_gain_two, middle, ffns, inverse, grad_parts):
         own, by_x, by_y = gather_near(d_branch)
         normeds = [part * inverse for part in ffns]
         d_gain_four = from_parts(
@@ -1087,11 +1172,16 @@
         )[0]
         normed_four = from_parts([part * gain for part, gain in zip(normeds, gain_parts)])
         layer_out = low(middle + normed_four).reshape(tokens.shape)
-        by_x, by_y, layer_out = tie((by_x, by_y, layer_out))
-        return gather_mine(own, by_x, by_y), d_gain_four, layer_out
-
-    d_branch_mine, d_gain_four, layer_out = in_order(
-        output_rows, d_branch, middle, [ffn0, ffn1], inverse, grad_parts
+        gain_rows = jnp.concatenate(
+            [low(gain).reshape(grp_count, seq_count, own_rows) for gain in (d_gain_two, d_gain_four)],
+            axis=2,
+        )
+        gain_rows = jnp.pad(gain_rows, ((0, 0), (0, 0), (0, 3 * HEAD - 2 * own_rows)))
+        by_x, by_y, layer_out, gain_rows = tie((by_x, by_y, layer_out, gain_rows))
+        return gather_mine(own, by_x, by_y), gain_rows, layer_out
+
+    d_branch_mine, gain_rows, layer_out = in_order(
+        output_rows, d_branch, d_gain_two, middle, [ffn0, ffn1], inverse, grad_parts
     )
 
     def attention_back(
@@ -1099,39 +1189,45 @@
         mixed_rows,
         w_heads,
         gate_part,
-        down_part,
+        down_parts,
+        gain_rows,
         token_rows,
         inverses,
         queries,
         keys,
         values,
-        norm,
+        weights,
+        slopes,
     ):
         gate_grad = by_device(gate_part)
         d_branch_rows = [d_branch_mine, permute(d_branch_mine, 1)]
         d_mixed = to_groups(
             jnp.concatenate([low(dot(part, w_heads[:, 2 * HEAD :])) for part in d_branch_rows], axis=0)
         )
-        d_query, d_keys, d_values = attend_back(queries, keys, values, places, norm, d_mixed)
-        d_query, d_keys, d_values, gate_grad = tie((d_query, d_keys, d_values, gate_grad))
-        d_kv = from_groups(jnp.where(key_core, d_keys, d_values)) + swap_cores(
-            from_groups(low(jnp.where(key_core, d_values, d_keys)))
-        ).astype(jnp.float32)
+        d_query, keep, send = attend_back(
+            queries, keys, values, weights, slopes, turn_tables, core_row, d_mixed
+        )
+        d_query, keep, send, gate_grad = tie((d_query, keep, send, gate_grad))
+        d_kv = from_groups(keep) + swap_cores(from_groups(send)).astype(jnp.float32)
         d_projected = in_two(
-            low(
-                jnp.concatenate(
-                    [turn(from_groups(d_query), cosine, -sine), turn(d_kv, kv_cosine, -kv_sine)],
-                    axis=1,
-                )
+            jnp.concatenate(
+                [from_groups(d_query), low(turn(d_kv, kv_cosine, -kv_sine))], axis=1
             )
         )
-        moved = permute(low(contract_cols(d_projected[1], w_heads[:, : 2 * HEAD])), 1)
-        down_grad = exchange(down_part)
+        moved = permute(d_projected[1], 1)
+        down_grad = exchange(
+            jnp.concatenate(
+                [part.reshape(seq_count, -1, slice_width) for part in down_parts], axis=1
+            )
+        )
         grad_out = over_rows(d_branch_rows, mixed_rows)
         grad_qkv = over_rows(normed_token_rows(token_rows, inverses), d_projected)
         grad_heads = jnp.concatenate(
             [with_layout_constraint(grad, Layout((0, 1))) for grad in (grad_qkv, grad_out)], axis=1
         )
+        grad_heads = jnp.concatenate(
+            [grad_heads.reshape(grp_count, plane_rows, 3 * HEAD), gain_rows], axis=1
+        ).reshape(-1, 3 * HEAD)
         return d_projected[0], moved, grad_heads, gate_grad, down_grad
 
     d_projected, moved, grad_heads, gate_grad, down_grad = in_order(
@@ -1140,25 +1236,27 @@
         mixed_rows,
         w_heads,
         gate_part,
-        down_part,
+        [down_part0, down_part1],
+        gain_rows,
         token_rows,
         inverses,
         queries,
         keys,
         values,
-        norm,
+        weights,
+        slopes,
     )
     heads_part = sum_planes(grad_heads)
 
-    def update_start(d_projected, moved, w_heads, upper_part):
+    def update_start(d_projected, moved, w_pair, upper_part):
         upper_grad = by_device(upper_part)
-        total = add_low(low(contract_cols(d_projected, w_heads[:, : 2 * HEAD])), moved)
+        total = low(contract_cols(jnp.concatenate([d_projected, moved], axis=1), w_pair))
         total, upper_grad = tie((total, upper_grad))
         rows = total.shape[0] // 4
         return sum_far(*(total[at * rows : (at + 1) * rows] for at in range(4))), upper_grad
 
     (own, by_x, by_y), upper_grad = in_order(
-        update_start, d_projected, moved, w_heads, upper_part
+        update_start, d_projected, moved, w_pair, upper_part
     )
     by_x, by_y = permute(by_x, 2), permute(by_y, 4)
     gu_all = renew_wide(
@@ -1166,18 +1264,17 @@
     )
     down_all = renew_wide(ffn_out, ffn_out_mom, ffn_out_avg, [(down_grad, 0)], rate_mat)
     gu_all, heads_part = tie((gu_all, heads_part))
-    heads_grad = by_device(heads_part)
-    heads_grad, d_gain_two = tie((heads_grad, d_gain_two))
-    sum_gains = jnp.sum(
-        lax.all_to_all(
-            jnp.stack([d_gain_two, d_gain_four]).reshape(2, device_count, -1).transpose(1, 0, 2),
-            ("grp", "seq"),
-            split_axis=0,
-            concat_axis=0,
-            tiled=True,
-        ),
-        axis=0,
-    )
+    heads_grad = exchange(
+        jnp.concatenate(
+            [
+                heads_part[:plane_rows].reshape(seq_count, own_rows, 3 * HEAD),
+                jnp.pad(heads_part[plane_rows:, None], ((0, 0), (0, 7), (0, 0))),
+            ],
+            axis=1,
+        )
+    )
+    sum_gains = jnp.sum(heads_grad[:, own_rows, : 2 * own_rows].astype(jnp.float32), axis=0)
+    sum_gains = sum_gains.reshape(2, own_rows)
     (layer_grad,) = norm_call(
         input_back_kernel,
         "input_back",

time: 928 us -> 905 us (0.975)
  matrix products: 215 us -> 171 us
  Pallas kernels: 112 us -> 143 us
    pallas_call x0 -> x1, Pallas kernels: none -> 33 us  [glu_rows(): pl.pallas_call(glu_kernel, grid=(rows // tile,), in_specs=[pl.BlockSpec((...]
    dot_general x5 -> x4, matrix products: 51.3 us -> 19.4 us  [dot(): return jnp.dot(left, right, preferred_element_type=jnp.float32)]
    dot_general x16 -> x15, matrix products: 80.3 us -> 71.3 us  [contract_cols(): lax.dot_general(left, right, (((1,), (1,)), ((), ())), preferred_element_...]
    ppermute x55 -> x56, waiting for transfers between devices: 201 us -> 206 us  [permute(): return lax.ppermute(field, 'seq', [(i, i ^ offset) for i in range(count)])]
    cond x121 -> x123, local copies, waits for them, and re-layouts: 40.4 us -> 35.3 us
    unnamed x66 -> x62, local copies, waits for them, and re-layouts: 25.9 us -> 21.9 us
    ppermute x55 -> x56, starting transfers between devices: 46.2 us -> 46.8 us  [permute(): return lax.ppermute(field, 'seq', [(i, i ^ offset) for i in range(count)])]
  transfers between devices with their start and end apart: 72 -> 72, of which waited for: 41 -> 40; matrix products, arithmetic and copies ran while one was open for 42% -> 38% of each run, Pallas kernels for 12% -> 15%
where the time goes in v3:
time: 905 us; the launch traced here: 895 us
  waiting for transfers between devices  248 us (27%)
  matrix products  171 us (19%)
  Pallas kernels  143 us (16%)
  local copies, waits for them, and re-layouts  139 us (15%)
  starting transfers between devices  80.4 us (9%)
  other arithmetic  61.3 us (7%)
  blocking collectives  35.7 us (4%)
  between operations  14.6 us (2%)
    ppermute x56, waiting for transfers between devices, permute(): return lax.ppermute(field, 'seq', [(i, i ^ offset) for i in range(count)])  206 us
    dot_general x8, matrix products, contract_rows(): lax.dot_general(left, right, (((0,), (0,)), ((), ())), preferred_element_...  80.6 us
    dot_general x15, matrix products, contract_cols(): lax.dot_general(left, right, (((1,), (1,)), ((), ())), preferred_element_...  71.3 us
    ppermute x56, starting transfers between devices, permute(): return lax.ppermute(field, 'seq', [(i, i ^ offset) for i in range(count)])  46.8 us
    all_to_all x1, blocking collectives, exchange(): return lax.all_to_all(field, 'seq', split_axis=0, concat_axis=0, tiled=True)  35.7 us
    cond x123, local copies, waits for them, and re-layouts  35.3 us
    pallas_call x1, Pallas kernels, glu_rows(): pl.pallas_call(glu_kernel, grid=(rows // tile,), in_specs=[pl.BlockSpec((...  33 us
    all_to_all x6, starting transfers between devices, exchange(): return lax.all_to_all(field, 'seq', split_axis=0, concat_axis=0, tiled=True)  27.5 us
  transfers between devices with their start and end apart: 72, of which 40 were waited for; matrix products, arithmetic and copies ran while one was open for 38% of the time, Pallas kernels for 15%

profile of v3, /device:TPU:0, one launch (start us, length us, event | category | flops | bytes accessed | tf_op | source)
XLA Modules:
  0.0 894.6 jit_solution(11099199108829522505)
XLA Ops:
  46.7 15.8 %all-to-all-done.5 = bf16[32,4,72]{2,1,0:T(4,128)(2,1)S(1)} async-done(((bf16[32,4,72]{2,1,0:T(4,128)(2,1)}), bf16[32,4,72]{2,1,0:T(4,128)(2,1)S(1)}, u32[]{:S(2)}, u32[]{:S(2)}) %all-to-all-start.5) | async-done | bytes 18464 | tf_op jit(solution)/shard_map/all_to_all | solution.py:972
  65.5 35.7 %all_to_all.36 = bf16[8,72,2304]{2,1,0:T(8,128)(2,1)} all-to-all(bf16[8,72,2304]{2,1,0:T(8,128)(2,1)S(1)} %spread.7), channel_id=1, replica_groups=mesh['grp'=4,'seq'=8] {'seq'}, dimensions={0} | all-to-all | bytes 5308416 | tf_op jit(solution)/shard_map/all_to_all | solution.py:851
  134.1 56.9 %conditional.11 = (bf16[384,1152]{1,0:T(8,128)(2,1)}, bf16[192,1152]{1,0:T(8,128)(2,1)}, f32[1152]{0:T(1024)S(1)}, f32[1152]{0:T(1024)}, bf16[2,1152,256]{2,1,0:...) conditional(s32[]{:T(128)} %convert_element_type.363, ...), branch_computations={%region_2.3_spmd, %region_3.6_spmd} | conditional | flops 8208287744 | bytes 155414144 | solution.py:856
  169.3 14.8 %attend.1 = (bf16[2,1152,256]{2,1,0:T(8,128)(2,1)S(1)}, bf16[2,1152,1152]{2,1,0:T(8,128)(2,1)}, bf16[2,1152,1152]{2,1,0:T(8,128)(2,1)}) custom-call(bf16[2,1152,256]{2,1,0:T(8,128)(2,1)} %bitcast.3.q_ref, bf16[2,1152,256]{2,1,0:T(8,128)(2,1)} %bitcast.8.k_ref, bf16[2,1152,256]{2,1,0:T(8,128)(2,1)} %bitcast.10.v_ref, s32[2,1152,128]{2,1,0:T(8,128)S(1)} %copy-done.51, ...), custom_call_target="tpu_custom_call" | custom-call | flops 2717908992 | bytes 4718592 | tf_op jit(solution)/shard_map/cond/branch_1_fun/attend/pallas_call | solution.py:808
  193.2 128.0 %conditional.12 = (f32[288,2304]{1,0:T(8,128)}, f32[288,2304]{1,0:T(8,128)}, bf16[2304,2304]{1,0:T(8,128)(2,1)}, bf16[288,1536]{0,1:T(8,128)(2,1)}, bf16[288,768]{0,1:T(8,128)(2,1)S(1)}) conditional(s32[]{:T(128)} %convert_element_type.363, () %tuple.111, (bf16[1152,256]{1,0:T(8,128)(2,1)}, bf16[2304,768]{1,0:T(8,128)(2,1)}, ...), branch_computations={%region_6.7_spmd, %region_7.8_spmd} | conditional | flops 2755067904 | bytes 197480992 | solution.py:856
  268.0 25.0 %collective-permute-done.11 = bf16[288,2304]{1,0:T(8,128)(2,1)S(1)} collective-permute-done((bf16[288,2304]{1,0:T(8,128)(2,1)S(1)}, bf16[288,2304]{1,0:T(8,128)(2,1)S(1)}, u32[]{:S(2)}, u32[]{:S(2)}) %collective-permute-start.11) | collective-permute-done | bytes 1327136 | tf_op jit(solution)/shard_map/cond/branch_1_fun/ppermute | solution.py:351
  321.3 33.0 %conditional.13 = ((f32[2304,2304]{1,0:T(8,128)}, bf16[2304,1152]{1,0:T(8,128)(2,1)})) conditional(s32[]{:T(128)} %convert_element_type.363, () %tuple.110, (bf16[2304,2304]{1,0:T(8,128)(2,1)}, bf16[2304,2304]{1,0:T(8,128)(2,1)}) %tuple.118), branch_computations={%region_8.9_spmd, %region_9.10_spmd} | conditional | flops 24461180928 | bytes 47775752 | solution.py:856
  321.3 33.0 %glu.1 = (f32[2304,2304]{1,0:T(8,128)}, bf16[2304,1152]{1,0:T(8,128)(2,1)}) custom-call(bf16[2304,2304]{1,0:T(8,128)(2,1)} %get-tuple-element.208.rows_ref, bf16[2304,2304]{1,0:T(8,128)(2,1)} %get-tuple-element.209.w_ref), custom_call_target="tpu_custom_call" | custom-call | flops 24461180928 | bytes 47775744 | tf_op jit(solution)/shard_map/cond/branch_1_fun/glu/pallas_call | solution.py:561
  357.2 50.5 %conditional.14 = (f32[288,1536]{1,0:T(8,128)}) conditional(s32[]{:T(128)} %convert_element_type.363, () %tuple.119, (bf16[2304,1152]{1,0:T(8,128)(2,1)}, bf16[1536,1152]{1,0:T(8,128)(2,1)}) %tuple.120), branch_computations={%region_10.11_spmd, %region_11.12_spmd} | conditional | flops 8171864064 | bytes 104399152 | solution.py:856
  387.3 18.5 %collective-permute-done.20 = bf16[288,1536]{1,0:T(8,128)(2,1)S(1)} collective-permute-done((bf16[288,1536]{1,0:T(8,128)(2,1)S(1)}, bf16[288,1536]{1,0:T(8,128)(2,1)S(1)}, u32[]{:S(2)}, u32[]{:S(2)}) %collective-permute-start.20) | collective-permute-done | bytes 884768 | tf_op jit(solution)/shard_map/cond/branch_1_fun/ppermute | solution.py:351
  407.7 77.0 %conditional.15 = (f32[288,768]{1,0:T(8,128)S(1)}, f32[288,1]{0,1:T(1,128)}, bf16[288,1536]{1,0:T(8,128)(2,1)}, bf16[288,1536]{1,0:T(8,128)(2,1)}, bf16[288,1536...) conditional(s32[]{:T(128)} %convert_element_type.363, () %tuple.109, ...), branch_computations={%region_12.13_spmd, %region_13.18_spmd} | conditional | flops 8171643904 | bytes 153619360 | solution.py:856
  485.7 38.3 %conditional.16 = (bf16[2304,1536]{1,0:T(8,128)(2,1)}, bf16[1536,1152]{1,0:T(8,128)(2,1)}) conditional(s32[]{:T(128)} %convert_element_type.363, () %tuple.108, (bf16[288,1536]{1,0:T(8,128)(2,1)}, bf16[288,1536]{1,0:T(8,128)(2,1)}, bf16[288,1536]{1,0:T(8,128)(2,1)}, bf16[2304,1152]{1,0:T(8,128)(2,1)}) %tuple.122), branch_computations={%region_18.19_spmd, %region_19.20_spmd} | conditional | flops 8155496448 | bytes 69009592 | solution.py:856
  524.0 59.9 %conditional.17 = (bf16[2304,2304]{1,0:T(8,128)(2,1)}, bf16[1152,2304]{1,0:T(8,128)(2,1)}, bf16[2304,1152]{1,0:T(8,128)(2,1)}, bf16[192,1152]{1,0:T(8,128)(2,1)}) conditional(s32[]{:T(128)} %convert_element_type.363, () %tuple.107, (bf16[2304,1536]{1,0:T(8,128)(2,1)}, bf16[192,1152]{1,0:T(8,128)(2,1)}, bf16[2304,768]{1,0:T(8,128)(2,1)}, ...), branch_computations={%region_21.22_spmd, %region_22.23_spmd} | conditional | flops 36697079808 | bytes 151289984 | solution.py:856
  524.1 25.2 %glu_back.1 = bf16[2304,2304]{1,0:T(8,128)(2,1)} custom-call(bf16[2304,1536]{1,0:T(8,128)(2,1)} %get-tuple-element.225.left0_ref, bf16[2304,768]{1,0:T(8,128)(2,1)} %get-tuple-element.226.left1_ref, bf16[1536,1152]{1,0:T(8,128)(2,1)} %get-tuple-element.227.w0_ref, bf16[768,1152]{1,0:T(8,128)(2,1)} %get-tuple-element.228.w1_ref, ...), custom_call_target="tpu_custom_call" | custom-call | flops 12230590464 | bytes 42467328 | tf_op jit(solution)/shard_map/cond/branch_1_fun/glu_back/pallas_call | solution.py:604
  564.7 19.2 %fusion.18 = bf16[2304,1152]{1,0:T(8,128)(2,1)} fusion(bf16[2304,2304]{1,0:T(8,128)(2,1)} %get-tuple-element.231, bf16[2304,2304]{1,0:T(8,128)(2,1)} %glu_back.1), kind=kOutput, calls=%fused_computation.60 | convolution fusion | flops 12233244672 | bytes 21233664 | tf_op jit(solution)/shard_map/cond/branch_1_fun/dot_general | solution.py:60
  584.7 75.4 %conditional.18 = (bf16[2304,1152]{1,0:T(8,128)(2,1)}, f32[288,2304]{1,0:T(8,128)}, bf16[288,2304]{1,0:T(8,128)(2,1)}, bf16[2304]{0:T(1024)(128)(2,1)S(1)}, bf16[2304,1024]{1,0:T(8,128)(2,1)}) conditional(s32[]{:T(128)} %convert_element_type.363, () %tuple.106, (bf16[2304,2304]{1,0:T(8,128)(2,1)}, bf16[2304,2304]{1,0:T(8,128)(2,1)}, ...), branch_computations={%region_23.24_spmd, %region_24.25_spmd} | conditional | flops 24507777024 | bytes 123176720 | solution.py:856
  587.0 17.4 %fusion.64 = bf16[1152,2304]{1,0:T(8,128)(2,1)S(1)} fusion(bf16[2304,2304]{1,0:T(8,128)(2,1)} %get-tuple-element.234, bf16[1152,2304]{1,0:T(8,128)(2,1)} %get-tuple-element.235, bf16[2304,2304]{1,0:T(8,128)(2,1)} %get-tuple-element.233), kind=kOutput, calls=%fused_computation.158 | convolution fusion | flops 12243861504 | bytes 26542080 | tf_op jit(solution)/shard_map/cond/branch_1_fun/dot_general | solution.py:66
  606.9 14.8 %collective-permute-done.39 = bf16[144,2304]{1,0:T(8,128)(2,1)S(1)} collective-permute-done((bf16[144,2304]{1,0:T(8,128)(2,1)S(1)}, bf16[144,2304]{1,0:T(8,128)(2,1)S(1)}, u32[]{:S(2)}, u32[]{:S(2)}) %collective-permute-start.39) | collective-permute-done | bytes 663584 | tf_op jit(solution)/shard_map/cond/branch_1_fun/ppermute | solution.py:351
  625.4 19.3 %convolution_convert_fusion.16 = bf16[2304,1152]{1,0:T(8,128)(2,1)} fusion(bf16[2304,2304]{1,0:T(8,128)(2,1)} %get-tuple-element.239, bf16[2304,2304]{1,0:T(8,128)(2,1)} %get-tuple-element.233), kind=kOutput, calls=%fused_computation.155 | convolution fusion | flops 12233244672 | bytes 21233664 | tf_op jit(solution)/shard_map/cond/branch_1_fun/dot_general | solution.py:60
  661.9 51.7 %conditional.19 = (bf16[1152,2304]{1,0:T(8,128)(2,1)}, bf16[4,8,768]{2,1,0:T(8,128)(2,1)}, bf16[2,144,2304]{2,1,0:T(8,128)(2,1)}) conditional(s32[]{:T(128)} %convert_element_type.363, () %tuple.105, (bf16[288,2304]{1,0:T(8,128)(2,1)}, f32[288,1]{0,1:T(1,128)}, f32[288,1536]{1,0:T(8,128)}, f32[1,1536]{1,0:T(1,128)}, f32[288,768]{1,0:T(8,128)S(1)}, ...), branch_computations={%region_25.26_spmd, %region_26.29_spmd} | conditional | flops 5551872 | bytes 71825208 | solution.py:856
  713.6 73.9 %conditional.20 = (bf16[1152,512]{1,0:T(8,128)(2,1)}, bf16[1152,512]{1,0:T(8,128)(2,1)}, bf16[2336,768]{1,0:T(8,128)(2,1)}, bf16[8,72,1152]{2,1,0:T(8,128)(2,1)}, bf16[8,72,1152]{2,1,0:T(8,128)(2,1)}) conditional(s32[]{:T(128)} %convert_element_type.363, () %tuple.127, (s32[]{:T(128)}, bf16[2304,768]{1,0:T(8,128)(2,1)}, ...), branch_computations={%region_32.33_spmd, %region_33.34_spmd} | conditional | flops 16364765184 | bytes 205447680 | solution.py:856
  729.3 17.6 %attend_back.1 = (bf16[2,1152,256]{2,1,0:T(8,128)(2,1)S(1)}, f32[2,1152,256]{2,1,0:T(8,128)S(1)}, bf16[2,1152,256]{2,1,0:T(8,128)(2,1)S(1)}) custom-call(bf16[2,1152,256]{2,1,0:T(8,128)(2,1)} %get-tuple-element.266.q_ref, bf16[2,1152,256]{2,1,0:T(8,128)(2,1)} %get-tuple-element.267.k_ref, bf16[2,1152,256]{2,1,0:T(8,128)(2,1)} %get-tuple-element.268.v_ref, ...), custom_call_target="tpu_custom_call" | custom-call | flops 5435817984 | bytes 9437184 | tf_op jit(solution)/shard_map/cond/branch_1_fun/attend_back/pallas_call | solution.py:832
  787.5 44.1 %conditional.21 = (bf16[288,2304]{1,0:T(8,128)(2,1)}, bf16[288,2304]{1,0:T(8,128)(2,1)}, bf16[288,2304]{1,0:T(8,128)(2,1)}, bf16[8,72,1152]{2,1,0:T(8,128)(2,1)}) conditional(s32[]{:T(128)} %convert_element_type.363, () %tuple.126, (bf16[1152,512]{1,0:T(8,128)(2,1)}, bf16[1152,512]{1,0:T(8,128)(2,1)}, bf16[2304,1024]{1,0:T(8,128)(2,1)}, ...), branch_computations={%region_34.35_spmd, %region_35.36_spmd} | conditional | flops 5451153408 | bytes 60162220 | solution.py:856
  835.0 18.4 %renew.2 = (f32[72,18432]{1,0:T(8,128)}, f32[72,18432]{1,0:T(8,128)}, f32[72,18432]{1,0:T(8,128)}, bf16[72,18432]{1,0:T(8,128)(2,1)}, f32[72,1]{1,0:T(8,128)S(1)}) custom-call(f32[72,18432]{1,0:T(8,128)S(1)} %copy-done, f32[72,18432]{1,0:T(8,128)} %m_ref.2, f32[72,18432]{1,0:T(8,128)} %a_ref.2, bf16[8,72,1152]{2,1,0:T(8,128)(2,1)} %get-tuple-element.472.refs_0_, ...), custom_call_target="tpu_custom_call" | custom-call | flops 10616832 | bytes 37158912 | tf_op jit(solution)/shard_map/renew/pallas_call | solution.py:495
  (533 shorter events, 604.2 us)
Async XLA Ops:
  15.8 110.4 %all-gather.5.cloned.1.call-start = ((), (), s32[]{:S(2)}) async-start(), calls=%async_computation.13 | async-start | bytes 4423680 | tf_op jit(solution)/shard_map/all_gather | solution.py:865
  31.1 31.6 %collective-permute-start.50 = (bf16[288,2304]{1,0:T(8,128)(2,1)S(1)}, bf16[288,2304]{1,0:T(8,128)(2,1)}, u32[]{:S(2)}, u32[]{:S(2)}) collective-permute-start(bf16[288,2304]{1,0:T(8,128)(2,1)S(1)} %bitcast.135), channel_id=1, source_target_pairs={{0,4},{1,5},{2,6},{3,7},{4,0},{5,1},{6,2},{7,3},{8,12},{9,13},{10,... | collective-permute-start | bytes 3981320 | tf_op jit(solution)/shard_map/ppermute | solution.py:351
  31.7 31.0 %collective-permute-start.49 = (bf16[288,2304]{1,0:T(8,128)(2,1)S(1)}, bf16[288,2304]{1,0:T(8,128)(2,1)}, u32[]{:S(2)}, u32[]{:S(2)}) collective-permute-start(bf16[288,2304]{1,0:T(8,128)(2,1)S(1)} %bitcast.136), channel_id=1, source_target_pairs={{0,2},{1,3},{2,0},{3,1},{4,6},{5,7},{6,4},{7,5},{8,10},{9,11},{10,... | collective-permute-start | bytes 3981320 | tf_op jit(solution)/shard_map/ppermute | solution.py:351
  45.3 276.0 %all-gather.7.cloned.1.call-start = ((), (), s32[]{:S(2)}) async-start(), calls=%async_computation.14 | async-start | bytes 13271040 | tf_op jit(solution)/shard_map/all_gather | solution.py:865
  101.3 255.9 %all-gather.11.cloned.1.call-start = ((), (), s32[]{:S(2)}) async-start(), calls=%async_computation.16 | async-start | bytes 4423680 | tf_op jit(solution)/shard_map/all_gather | solution.py:865
  191.0 216.7 %all-gather.9.cloned.1.call-start = ((), (), s32[]{:S(2)}) async-start(), calls=%async_computation.15 | async-start | bytes 2211840 | tf_op jit(solution)/shard_map/all_gather | solution.py:865
  191.6 332.5 %reduce-scatter.6.cloned.1.call-start = ((), (), s32[]{:S(2)}) async-start(), calls=%async_computation.17 | async-start | bytes 2211840 | tf_op jit(solution)/shard_map/reduce_scatter | solution.py:869
  226.6 30.4 %collective-permute-start.7 = (bf16[288,2304]{1,0:T(8,128)(2,1)}, bf16[288,2304]{1,0:T(8,128)(2,1)}, u32[]{:S(2)}, u32[]{:S(2)}) collective-permute-start(bf16[288,2304]{1,0:T(8,128)(2,1)} %pad_maximum_fusion), channel_id=1, source_target_pairs={{0,2},{1,3},{2,0},{3,1},{4,6},{5,7},{6,4},{7,5},{8,10},{9,11},{10,... | collective-permute-start | bytes 3981320 | tf_op jit(solution)/shard_map/cond/branch_1_fun/ppermute | solution.py:351
  228.1 30.4 %collective-permute-start.9 = (bf16[288,2304]{1,0:T(8,128)(2,1)}, bf16[288,2304]{1,0:T(8,128)(2,1)}, u32[]{:S(2)}, u32[]{:S(2)}) collective-permute-start(bf16[288,2304]{1,0:T(8,128)(2,1)} %pad_maximum_fusion.1), channel_id=1, source_target_pairs={{0,4},{1,5},{2,6},{3,7},{4,0},{5,1},{6,2},{7,3},{8,12},{9,13},{10,... | collective-permute-start | bytes 3981320 | tf_op jit(solution)/shard_map/cond/branch_1_fun/ppermute | solution.py:351
  263.8 29.2 %collective-permute-start.11 = (bf16[288,2304]{1,0:T(8,128)(2,1)S(1)}, bf16[288,2304]{1,0:T(8,128)(2,1)S(1)}, u32[]{:S(2)}, u32[]{:S(2)}) collective-permute-start(bf16[288,2304]{1,0:T(8,128)(2,1)S(1)} %get-tuple-element.205), channel_id=1, source_target_pairs={{0,4},{1,5},{2,6},{3,7},{4,0},{5,1},{6,2},{7,3},{8,12},{9,13},{10,... | collective-permute-start | bytes 3981320 | tf_op jit(solution)/shard_map/cond/branch_1_fun/ppermute | solution.py:351
  265.3 29.8 %collective-permute-start.10 = (bf16[288,2304]{1,0:T(8,128)(2,1)S(1)}, bf16[288,2304]{1,0:T(8,128)(2,1)S(1)}, u32[]{:S(2)}, u32[]{:S(2)}) collective-permute-start(bf16[288,2304]{1,0:T(8,128)(2,1)S(1)} %get-tuple-element.205), channel_id=1, source_target_pairs={{0,2},{1,3},{2,0},{3,1},{4,6},{5,7},{6,4},{7,5},{8,10},{9,11},{10,... | collective-permute-start | bytes 3981320 | tf_op jit(solution)/shard_map/cond/branch_1_fun/ppermute | solution.py:351
  484.8 228.8 %reduce-scatter.10.cloned.1.call-start = ((), (), s32[]{:S(2)}) async-start(), calls=%async_computation.19 | async-start | bytes 4423680 | tf_op jit(solution)/shard_map/reduce_scatter | solution.py:869
  524.0 189.6 %reduce-scatter.8.cloned.1.call-start = ((), (), s32[]{:S(2)}) async-start(), calls=%async_computation.18 | async-start | bytes 6635520 | tf_op jit(solution)/shard_map/reduce_scatter | solution.py:869
  584.0 203.5 %reduce-scatter.12.cloned.1.call-start = ((), (), s32[]{:S(2)}) async-start(), calls=%async_computation.20 | async-start | bytes 6635520 | tf_op jit(solution)/shard_map/reduce_scatter | solution.py:869
  586.6 58.1 %collective-permute-start.42 = (bf16[2304,512]{1,0:T(8,128)(2,1)S(1)}, bf16[2304,512]{1,0:T(8,128)(2,1)S(1)}, u32[]{:S(2)}, u32[]{:S(2)}) collective-permute-start(bf16[2304,512]{1,0:T(8,128)(2,1)S(1)} %slice.333), channel_id=1, source_target_pairs={{0,1},{1,0},{2,3},{3,2},{4,5},{5,4},{6,7},{7,6},{8,9},{9,8},{10,11... | collective-permute-start | bytes 7077896 | tf_op jit(solution)/shard_map/cond/branch_1_fun/ppermute | solution.py:351
  622.5 30.3 %collective-permute-start.40 = (bf16[288,2304]{1,0:T(8,128)(2,1)S(1)}, bf16[288,2304]{1,0:T(8,128)(2,1)S(1)}, u32[]{:S(2)}, u32[]{:S(2)}) collective-permute-start(bf16[288,2304]{1,0:T(8,128)(2,1)S(1)} %get-tuple-element.237), channel_id=1, source_target_pairs={{0,2},{1,3},{2,0},{3,1},{4,6},{5,7},{6,4},{7,5},{8,10},{9,11},{10,... | collective-permute-start | bytes 3981320 | tf_op jit(solution)/shard_map/cond/branch_1_fun/ppermute | solution.py:351
  624.0 29.9 %collective-permute-start.41 = (bf16[288,2304]{1,0:T(8,128)(2,1)S(1)}, bf16[288,2304]{1,0:T(8,128)(2,1)S(1)}, u32[]{:S(2)}, u32[]{:S(2)}) collective-permute-start(bf16[288,2304]{1,0:T(8,128)(2,1)S(1)} %get-tuple-element.238), channel_id=1, source_target_pairs={{0,4},{1,5},{2,6},{3,7},{4,0},{5,1},{6,2},{7,3},{8,12},{9,13},{10,... | collective-permute-start | bytes 3981320 | tf_op jit(solution)/shard_map/cond/branch_1_fun/ppermute | solution.py:351
  660.8 194.6 %reduce-scatter.14.cloned.1.call-start = ((), (), s32[]{:S(2)}) async-start(), calls=%async_computation.21 | async-start | bytes 4485120 | tf_op jit(solution)/shard_map/reduce_scatter | solution.py:869
  661.9 32.2 %collective-permute-start.1 = (bf16[288,2304]{1,0:T(8,128)(2,1)}, bf16[288,2304]{1,0:T(8,128)(2,1)}, u32[]{:S(2)}, u32[]{:S(2)}) collective-permute-start(bf16[288,2304]{1,0:T(8,128)(2,1)} %get-tuple-element.252), channel_id=1, source_target_pairs={{0,4},{1,5},{2,6},{3,7},{4,0},{5,1},{6,2},{7,3},{8,12},{9,13},{10,... | collective-permute-start | bytes 3981320 | tf_op jit(solution)/shard_map/cond/branch_1_fun/ppermute | solution.py:351
  663.4 30.7 %collective-permute-start = (bf16[288,2304]{1,0:T(8,128)(2,1)}, bf16[288,2304]{1,0:T(8,128)(2,1)}, u32[]{:S(2)}, u32[]{:S(2)}) collective-permute-start(bf16[288,2304]{1,0:T(8,128)(2,1)} %get-tuple-element.252), channel_id=1, source_target_pairs={{0,2},{1,3},{2,0},{3,1},{4,6},{5,7},{6,4},{7,5},{8,10},{9,11},{10,... | collective-permute-start | bytes 3981320 | tf_op jit(solution)/shard_map/cond/branch_1_fun/ppermute | solution.py:351
  713.6 36.8 %all-to-all-start = ((bf16[8,72,1152]{2,1,0:T(8,128)(2,1)}), bf16[8,72,1152]{2,1,0:T(8,128)(2,1)}, u32[]{:S(2)}, u32[]{:S(2)}) async-start(bf16[8,72,1152]{2,1,0:T(8,128)(2,1)} %bitcast.161), calls=%async_computation | async-start | bytes 2654208 | tf_op jit(solution)/shard_map/cond/branch_1_fun/all_to_all | solution.py:851
  750.4 37.1 %all-to-all-start.1 = ((bf16[8,72,1152]{2,1,0:T(8,128)(2,1)}), bf16[8,72,1152]{2,1,0:T(8,128)(2,1)}, u32[]{:S(2)}, u32[]{:S(2)}) async-start(bf16[8,72,1152]{2,1,0:T(8,128)(2,1)} %pad_maximum_fusion.20), calls=%async_computation.1 | async-start | bytes 2654208 | tf_op jit(solution)/shard_map/cond/branch_1_fun/all_to_all | solution.py:851
  831.7 40.6 %collective-permute-start.54 = (bf16[288,2304]{1,0:T(8,128)(2,1)}, bf16[288,2304]{1,0:T(8,128)(2,1)}, u32[]{:S(2)}, u32[]{:S(2)}) collective-permute-start(bf16[288,2304]{1,0:T(8,128)(2,1)} %get-tuple-element.469), channel_id=1, source_target_pairs={{0,2},{1,3},{2,0},{3,1},{4,6},{5,7},{6,4},{7,5},{8,10},{9,11},{10,... | collective-permute-start | bytes 3981320 | tf_op jit(solution)/shard_map/ppermute | solution.py:351
  832.0 40.3 %collective-permute-start.55 = (bf16[288,2304]{1,0:T(8,128)(2,1)}, bf16[288,2304]{1,0:T(8,128)(2,1)}, u32[]{:S(2)}, u32[]{:S(2)}) collective-permute-start(bf16[288,2304]{1,0:T(8,128)(2,1)} %get-tuple-element.470), channel_id=1, source_target_pairs={{0,4},{1,5},{2,6},{3,7},{4,0},{5,1},{6,2},{7,3},{8,12},{9,13},{10,... | collective-permute-start | bytes 3981320 | tf_op jit(solution)/shard_map/ppermute | solution.py:351
  (130 other events, 1331.6 us)
Sparse Core Ops, SparseCore 0:
  30.5 70.0 all-gather.4
  102.1 184.6 all-gather.6
  289.0 68.1 all-gather.10
  359.2 38.8 all-gather.8
  484.9 37.1 reduce-scatter.5
  524.4 65.4 reduce-scatter.9
  592.2 95.1 reduce-scatter.7
  689.7 95.3 reduce-scatter.11
  787.6 67.6 reduce-scatter.13

commit v4 on v3

--- a/solution.py
+++ b/solution.py
@@ -394,11 +394,13 @@
 
 def pair_products(mine, other, weight):
     rows = mine.shape[0] // 4
-    ends = []
-    for here in (slice(3 * rows, None), slice(None, 3 * rows)):
-        moved = permute(low(contract_cols(other[here], weight)), 1)
-        ends.append(add_low(low(contract_cols(mine[here], weight)), moved))
-    far, near = ends
+    start = 3 * rows
+    far_other = low(contract_cols(other[start:], weight))
+    later, far_other = lax.optimization_barrier((weight, far_other))
+    far_moved = permute(far_other, 1)
+    near_moved = permute(low(contract_cols(other[:start], later)), 1)
+    far = add_low(low(contract_cols(mine[start:], weight)), far_moved)
+    near = add_low(low(contract_cols(mine[:start], later)), near_moved)
     return near[:rows], near[rows : 2 * rows], near[2 * rows :], far
 
 

time: 905 us -> 912 us (level)
  transfers between devices with their start and end apart: 72 -> 72, of which waited for: 40 -> 39; matrix products, arithmetic and copies ran while one was open for 38% -> 37% of each run, Pallas kernels for 15% -> 15%
where the time goes in v4:
time: 912 us; the launch traced here: 901 us
  waiting for transfers between devices  251 us (28%)
  matrix products  173 us (19%)
  Pallas kernels  143 us (16%)
  local copies, waits for them, and re-layouts  141 us (15%)
  starting transfers between devices  79.8 us (9%)
  other arithmetic  61.3 us (7%)
  blocking collectives  35.8 us (4%)
  between operations  14.8 us (2%)
    ppermute x56, waiting for transfers between devices, permute(): return lax.ppermute(field, 'seq', [(i, i ^ offset) for i in range(count)])  211 us
    dot_general x8, matrix products, contract_rows(): lax.dot_general(left, right, (((0,), (0,)), ((), ())), preferred_element_...  81 us
    dot_general x15, matrix products, contract_cols(): lax.dot_general(left, right, (((1,), (1,)), ((), ())), preferred_element_...  72.6 us
    ppermute x56, starting transfers between devices, permute(): return lax.ppermute(field, 'seq', [(i, i ^ offset) for i in range(count)])  46.5 us
    cond x123, local copies, waits for them, and re-layouts  36.6 us
    all_to_all x1, blocking collectives, exchange(): return lax.all_to_all(field, 'seq', split_axis=0, concat_axis=0, tiled=True)  35.8 us
    pallas_call x1, Pallas kernels, glu_rows(): pl.pallas_call(glu_kernel, grid=(rows // tile,), in_specs=[pl.BlockSpec((...  32.9 us
    all_to_all x6, starting transfers between devices, exchange(): return lax.all_to_all(field, 'seq', split_axis=0, concat_axis=0, tiled=True)  27.3 us
  transfers between devices with their start and end apart: 72, of which 39 were waited for; matrix products, arithmetic and copies ran while one was open for 37% of the time, Pallas kernels for 15%

profile of v4, /device:TPU:0, one launch (start us, length us, event | category | flops | bytes accessed | tf_op | source)
XLA Modules:
  0.0 901.4 jit_solution(5121629871827019215)
XLA Ops:
  46.7 15.8 %all-to-all-done.5 = bf16[32,4,72]{2,1,0:T(4,128)(2,1)S(1)} async-done(((bf16[32,4,72]{2,1,0:T(4,128)(2,1)}), bf16[32,4,72]{2,1,0:T(4,128)(2,1)S(1)}, u32[]{:S(2)}, u32[]{:S(2)}) %all-to-all-start.5) | async-done | bytes 18464 | tf_op jit(solution)/shard_map/all_to_all | solution.py:974
  65.5 35.8 %all_to_all.36 = bf16[8,72,2304]{2,1,0:T(8,128)(2,1)} all-to-all(bf16[8,72,2304]{2,1,0:T(8,128)(2,1)S(1)} %spread.7), channel_id=1, replica_groups=mesh['grp'=4,'seq'=8] {'seq'}, dimensions={0} | all-to-all | bytes 5308416 | tf_op jit(solution)/shard_map/all_to_all | solution.py:853
  134.1 56.8 %conditional.11 = (bf16[384,1152]{1,0:T(8,128)(2,1)}, bf16[192,1152]{1,0:T(8,128)(2,1)}, f32[1152]{0:T(1024)S(1)}, f32[1152]{0:T(1024)}, bf16[2,1152,256]{2,1,0:...) conditional(s32[]{:T(128)} %convert_element_type.384, ...), branch_computations={%region_2.3_spmd, %region_3.6_spmd} | conditional | flops 8208287744 | bytes 155414144 | solution.py:858
  169.3 14.8 %attend.1 = (bf16[2,1152,256]{2,1,0:T(8,128)(2,1)S(1)}, bf16[2,1152,1152]{2,1,0:T(8,128)(2,1)}, bf16[2,1152,1152]{2,1,0:T(8,128)(2,1)}) custom-call(bf16[2,1152,256]{2,1,0:T(8,128)(2,1)} %bitcast.3.q_ref, bf16[2,1152,256]{2,1,0:T(8,128)(2,1)} %bitcast.8.k_ref, bf16[2,1152,256]{2,1,0:T(8,128)(2,1)} %bitcast.10.v_ref, s32[2,1152,128]{2,1,0:T(8,128)S(1)} %copy-done.49, ...), custom_call_target="tpu_custom_call" | custom-call | flops 2717908992 | bytes 4718592 | tf_op jit(solution)/shard_map/cond/branch_1_fun/attend/pallas_call | solution.py:810
  193.1 131.2 %conditional.12 = (f32[288,2304]{1,0:T(8,128)}, f32[288,2304]{1,0:T(8,128)}, bf16[2304,2304]{1,0:T(8,128)(2,1)}, bf16[288,1536]{0,1:T(8,128)(2,1)}, bf16[288,768]{0,1:T(8,128)(2,1)S(1)}) conditional(s32[]{:T(128)} %convert_element_type.384, () %tuple.114, (bf16[2304,768]{1,0:T(8,128)(2,1)}, bf16[1152,256]{1,0:T(8,128)(2,1)}, ...), branch_computations={%region_6.7_spmd, %region_7.8_spmd} | conditional | flops 2755067904 | bytes 185684480 | solution.py:858
  271.0 25.0 %collective-permute-done.11 = bf16[288,2304]{1,0:T(8,128)(2,1)S(1)} collective-permute-done((bf16[288,2304]{1,0:T(8,128)(2,1)S(1)}, bf16[288,2304]{1,0:T(8,128)(2,1)S(1)}, u32[]{:S(2)}, u32[]{:S(2)}) %collective-permute-start.11) | collective-permute-done | bytes 1327136 | tf_op jit(solution)/shard_map/cond/branch_1_fun/ppermute | solution.py:351
  324.4 32.9 %conditional.13 = ((f32[2304,2304]{1,0:T(8,128)}, bf16[2304,1152]{1,0:T(8,128)(2,1)})) conditional(s32[]{:T(128)} %convert_element_type.384, () %tuple.113, (bf16[2304,2304]{1,0:T(8,128)(2,1)}, bf16[2304,2304]{1,0:T(8,128)(2,1)}) %tuple.121), branch_computations={%region_8.9_spmd, %region_9.10_spmd} | conditional | flops 24461180928 | bytes 47775752 | solution.py:858
  324.4 32.9 %glu.1 = (f32[2304,2304]{1,0:T(8,128)}, bf16[2304,1152]{1,0:T(8,128)(2,1)}) custom-call(bf16[2304,2304]{1,0:T(8,128)(2,1)} %get-tuple-element.210.rows_ref, bf16[2304,2304]{1,0:T(8,128)(2,1)} %get-tuple-element.211.w_ref), custom_call_target="tpu_custom_call" | custom-call | flops 24461180928 | bytes 47775744 | tf_op jit(solution)/shard_map/cond/branch_1_fun/glu/pallas_call | solution.py:563
  357.3 53.2 %conditional.14 = (f32[288,1536]{1,0:T(8,128)}) conditional(s32[]{:T(128)} %convert_element_type.384, () %tuple.122, (bf16[2304,1152]{1,0:T(8,128)(2,1)}, bf16[1536,1152]{1,0:T(8,128)(2,1)}) %tuple.123), branch_computations={%region_10.11_spmd, %region_11.12_spmd} | conditional | flops 8171864064 | bytes 104399152 | solution.py:858
  390.0 18.5 %collective-permute-done.20 = bf16[288,1536]{1,0:T(8,128)(2,1)S(1)} collective-permute-done((bf16[288,1536]{1,0:T(8,128)(2,1)S(1)}, bf16[288,1536]{1,0:T(8,128)(2,1)S(1)}, u32[]{:S(2)}, u32[]{:S(2)}) %collective-permute-start.20) | collective-permute-done | bytes 884768 | tf_op jit(solution)/shard_map/cond/branch_1_fun/ppermute | solution.py:351
  410.5 79.1 %conditional.15 = (f32[288,768]{1,0:T(8,128)S(1)}, f32[288,1]{0,1:T(1,128)}, bf16[288,1536]{1,0:T(8,128)(2,1)}, bf16[288,1536]{1,0:T(8,128)(2,1)}, bf16[288,1536...) conditional(s32[]{:T(128)} %convert_element_type.384, () %tuple.112, ...), branch_computations={%region_12.13_spmd, %region_13.18_spmd} | conditional | flops 8171643904 | bytes 148310944 | solution.py:858
  490.5 38.2 %conditional.16 = (bf16[2304,1536]{1,0:T(8,128)(2,1)}, bf16[1536,1152]{1,0:T(8,128)(2,1)}) conditional(s32[]{:T(128)} %convert_element_type.384, () %tuple.111, (bf16[288,1536]{1,0:T(8,128)(2,1)}, bf16[288,1536]{1,0:T(8,128)(2,1)}, bf16[288,1536]{1,0:T(8,128)(2,1)}, bf16[2304,1152]{1,0:T(8,128)(2,1)}) %tuple.125), branch_computations={%region_18.19_spmd, %region_19.20_spmd} | conditional | flops 8155496448 | bytes 69009592 | solution.py:858
  528.9 60.0 %conditional.17 = (bf16[2304,2304]{1,0:T(8,128)(2,1)}, bf16[1152,2304]{1,0:T(8,128)(2,1)}, bf16[2304,1152]{1,0:T(8,128)(2,1)}, bf16[192,1152]{1,0:T(8,128)(2,1)}) conditional(s32[]{:T(128)} %convert_element_type.384, () %tuple.110, (bf16[2304,1536]{1,0:T(8,128)(2,1)}, bf16[192,1152]{1,0:T(8,128)(2,1)}, bf16[2304,768]{1,0:T(8,128)(2,1)}, ...), branch_computations={%region_21.22_spmd, %region_22.23_spmd} | conditional | flops 36697079808 | bytes 151289984 | solution.py:858
  528.9 25.2 %glu_back.1 = bf16[2304,2304]{1,0:T(8,128)(2,1)} custom-call(bf16[2304,1536]{1,0:T(8,128)(2,1)} %get-tuple-element.231.left0_ref, bf16[2304,768]{1,0:T(8,128)(2,1)} %get-tuple-element.232.left1_ref, bf16[1536,1152]{1,0:T(8,128)(2,1)} %get-tuple-element.233.w0_ref, bf16[768,1152]{1,0:T(8,128)(2,1)} %get-tuple-element.234.w1_ref, ...), custom_call_target="tpu_custom_call" | custom-call | flops 12230590464 | bytes 42467328 | tf_op jit(solution)/shard_map/cond/branch_1_fun/glu_back/pallas_call | solution.py:606
  554.1 14.5 %convolution_convert_fusion.10 = bf16[1152,2304]{1,0:T(8,128)(2,1)S(1)} fusion(bf16[2304,2304]{1,0:T(8,128)(2,1)S(1)} %copy-done.75, bf16[2304,2304]{1,0:T(8,128)(2,1)} %glu_back.1), kind=kOutput, calls=%fused_computation.61 | convolution fusion | flops 12233244672 | bytes 21233664 | tf_op jit(solution)/shard_map/cond/branch_1_fun/dot_general | solution.py:66
  569.6 19.3 %fusion.20 = bf16[2304,1152]{1,0:T(8,128)(2,1)} fusion(bf16[2304,2304]{1,0:T(8,128)(2,1)} %get-tuple-element.237, bf16[2304,2304]{1,0:T(8,128)(2,1)} %glu_back.1), kind=kOutput, calls=%fused_computation.62 | convolution fusion | flops 12233244672 | bytes 21233664 | tf_op jit(solution)/shard_map/cond/branch_1_fun/dot_general | solution.py:60
  589.7 75.6 %conditional.18 = (bf16[2304,1152]{1,0:T(8,128)(2,1)}, f32[288,2304]{1,0:T(8,128)}, bf16[288,2304]{1,0:T(8,128)(2,1)}, bf16[2304]{0:T(1024)(128)(2,1)S(1)}, bf16[2304,1024]{1,0:T(8,128)(2,1)}) conditional(s32[]{:T(128)} %convert_element_type.384, () %tuple.109, (bf16[2304,2304]{1,0:T(8,128)(2,1)}, bf16[2304,2304]{1,0:T(8,128)(2,1)}, ...), branch_computations={%region_23.24_spmd, %region_24.25_spmd} | conditional | flops 24507777024 | bytes 123176720 | solution.py:858
  591.9 17.6 %fusion.70 = bf16[1152,2304]{1,0:T(8,128)(2,1)S(1)} fusion(bf16[2304,2304]{1,0:T(8,128)(2,1)} %get-tuple-element.240, bf16[1152,2304]{1,0:T(8,128)(2,1)} %get-tuple-element.241, bf16[2304,2304]{1,0:T(8,128)(2,1)} %get-tuple-element.239), kind=kOutput, calls=%fused_computation.162 | convolution fusion | flops 12243861504 | bytes 26542080 | tf_op jit(solution)/shard_map/cond/branch_1_fun/dot_general | solution.py:66
  630.4 19.3 %convolution_convert_fusion.16 = bf16[2304,1152]{1,0:T(8,128)(2,1)} fusion(bf16[2304,2304]{1,0:T(8,128)(2,1)} %get-tuple-element.245, bf16[2304,2304]{1,0:T(8,128)(2,1)} %get-tuple-element.239), kind=kOutput, calls=%fused_computation.159 | convolution fusion | flops 12233244672 | bytes 21233664 | tf_op jit(solution)/shard_map/cond/branch_1_fun/dot_general | solution.py:60
  667.1 51.9 %conditional.19 = (bf16[1152,2304]{1,0:T(8,128)(2,1)}, bf16[4,8,768]{2,1,0:T(8,128)(2,1)}, bf16[2,144,2304]{2,1,0:T(8,128)(2,1)}) conditional(s32[]{:T(128)} %convert_element_type.384, () %tuple.108, (bf16[288,2304]{1,0:T(8,128)(2,1)}, f32[288,1]{0,1:T(1,128)}, f32[288,1536]{1,0:T(8,128)}, f32[1,1536]{1,0:T(1,128)}, f32[288,768]{1,0:T(8,128)S(1)}, ...), branch_computations={%region_25.26_spmd, %region_26.29_spmd} | conditional | flops 5551872 | bytes 71825208 | solution.py:858
  718.9 73.9 %conditional.20 = (bf16[1152,512]{1,0:T(8,128)(2,1)}, bf16[1152,512]{1,0:T(8,128)(2,1)}, bf16[2336,768]{1,0:T(8,128)(2,1)}, bf16[8,72,1152]{2,1,0:T(8,128)(2,1)}, bf16[8,72,1152]{2,1,0:T(8,128)(2,1)}) conditional(s32[]{:T(128)} %convert_element_type.384, () %tuple.130, (s32[]{:T(128)}, bf16[2304,768]{1,0:T(8,128)(2,1)}, ...), branch_computations={%region_32.33_spmd, %region_33.34_spmd} | conditional | flops 16364765184 | bytes 205447680 | solution.py:858
  734.7 17.6 %attend_back.1 = (bf16[2,1152,256]{2,1,0:T(8,128)(2,1)S(1)}, f32[2,1152,256]{2,1,0:T(8,128)S(1)}, bf16[2,1152,256]{2,1,0:T(8,128)(2,1)S(1)}) custom-call(bf16[2,1152,256]{2,1,0:T(8,128)(2,1)} %get-tuple-element.272.q_ref, bf16[2,1152,256]{2,1,0:T(8,128)(2,1)} %get-tuple-element.273.k_ref, bf16[2,1152,256]{2,1,0:T(8,128)(2,1)} %get-tuple-element.274.v_ref, ...), custom_call_target="tpu_custom_call" | custom-call | flops 5435817984 | bytes 9437184 | tf_op jit(solution)/shard_map/cond/branch_1_fun/attend_back/pallas_call | solution.py:834
  792.9 44.2 %conditional.21 = (bf16[288,2304]{1,0:T(8,128)(2,1)}, bf16[288,2304]{1,0:T(8,128)(2,1)}, bf16[288,2304]{1,0:T(8,128)(2,1)}, bf16[8,72,1152]{2,1,0:T(8,128)(2,1)}) conditional(s32[]{:T(128)} %convert_element_type.384, () %tuple.129, (bf16[1152,512]{1,0:T(8,128)(2,1)}, bf16[1152,512]{1,0:T(8,128)(2,1)}, bf16[2304,1024]{1,0:T(8,128)(2,1)}, ...), branch_computations={%region_34.35_spmd, %region_35.36_spmd} | conditional | flops 5451153408 | bytes 60162220 | solution.py:858
  840.3 18.4 %renew.2 = (f32[72,18432]{1,0:T(8,128)}, f32[72,18432]{1,0:T(8,128)}, f32[72,18432]{1,0:T(8,128)}, bf16[72,18432]{1,0:T(8,128)(2,1)}, f32[72,1]{1,0:T(8,128)S(1)}) custom-call(f32[72,18432]{1,0:T(8,128)S(1)} %copy-done, f32[72,18432]{1,0:T(8,128)} %m_ref.2, f32[72,18432]{1,0:T(8,128)} %a_ref.2, bf16[8,72,1152]{2,1,0:T(8,128)(2,1)} %get-tuple-element.478.refs_0_, ...), custom_call_target="tpu_custom_call" | custom-call | flops 10616832 | bytes 37158912 | tf_op jit(solution)/shard_map/renew/pallas_call | solution.py:497
  (535 shorter events, 610.8 us)
Async XLA Ops:
  15.8 110.4 %all-gather.5.cloned.1.call-start = ((), (), s32[]{:S(2)}) async-start(), calls=%async_computation.13 | async-start | bytes 4423680 | tf_op jit(solution)/shard_map/all_gather | solution.py:867
  31.1 31.6 %collective-permute-start.50 = (bf16[288,2304]{1,0:T(8,128)(2,1)S(1)}, bf16[288,2304]{1,0:T(8,128)(2,1)}, u32[]{:S(2)}, u32[]{:S(2)}) collective-permute-start(bf16[288,2304]{1,0:T(8,128)(2,1)S(1)} %bitcast.155), channel_id=1, source_target_pairs={{0,4},{1,5},{2,6},{3,7},{4,0},{5,1},{6,2},{7,3},{8,12},{9,13},{10,... | collective-permute-start | bytes 3981320 | tf_op jit(solution)/shard_map/ppermute | solution.py:351
  31.7 31.0 %collective-permute-start.49 = (bf16[288,2304]{1,0:T(8,128)(2,1)S(1)}, bf16[288,2304]{1,0:T(8,128)(2,1)}, u32[]{:S(2)}, u32[]{:S(2)}) collective-permute-start(bf16[288,2304]{1,0:T(8,128)(2,1)S(1)} %bitcast.156), channel_id=1, source_target_pairs={{0,2},{1,3},{2,0},{3,1},{4,6},{5,7},{6,4},{7,5},{8,10},{9,11},{10,... | collective-permute-start | bytes 3981320 | tf_op jit(solution)/shard_map/ppermute | solution.py:351
  45.3 279.1 %all-gather.7.cloned.1.call-start = ((), (), s32[]{:S(2)}) async-start(), calls=%async_computation.14 | async-start | bytes 13271040 | tf_op jit(solution)/shard_map/all_gather | solution.py:867
  101.3 256.0 %all-gather.11.cloned.1.call-start = ((), (), s32[]{:S(2)}) async-start(), calls=%async_computation.16 | async-start | bytes 4423680 | tf_op jit(solution)/shard_map/all_gather | solution.py:867
  190.9 219.6 %all-gather.9.cloned.1.call-start = ((), (), s32[]{:S(2)}) async-start(), calls=%async_computation.15 | async-start | bytes 2211840 | tf_op jit(solution)/shard_map/all_gather | solution.py:867
  191.5 337.4 %reduce-scatter.6.cloned.1.call-start = ((), (), s32[]{:S(2)}) async-start(), calls=%async_computation.17 | async-start | bytes 2211840 | tf_op jit(solution)/shard_map/reduce_scatter | solution.py:871
  229.7 30.5 %collective-permute-start.7 = (bf16[288,2304]{1,0:T(8,128)(2,1)}, bf16[288,2304]{1,0:T(8,128)(2,1)}, u32[]{:S(2)}, u32[]{:S(2)}) collective-permute-start(bf16[288,2304]{1,0:T(8,128)(2,1)} %pad_maximum_fusion), channel_id=1, source_target_pairs={{0,2},{1,3},{2,0},{3,1},{4,6},{5,7},{6,4},{7,5},{8,10},{9,11},{10,... | collective-permute-start | bytes 3981320 | tf_op jit(solution)/shard_map/cond/branch_1_fun/ppermute | solution.py:351
  231.2 30.4 %collective-permute-start.9 = (bf16[288,2304]{1,0:T(8,128)(2,1)}, bf16[288,2304]{1,0:T(8,128)(2,1)}, u32[]{:S(2)}, u32[]{:S(2)}) collective-permute-start(bf16[288,2304]{1,0:T(8,128)(2,1)} %pad_maximum_fusion.1), channel_id=1, source_target_pairs={{0,4},{1,5},{2,6},{3,7},{4,0},{5,1},{6,2},{7,3},{8,12},{9,13},{10,... | collective-permute-start | bytes 3981320 | tf_op jit(solution)/shard_map/cond/branch_1_fun/ppermute | solution.py:351
  266.9 29.2 %collective-permute-start.11 = (bf16[288,2304]{1,0:T(8,128)(2,1)S(1)}, bf16[288,2304]{1,0:T(8,128)(2,1)S(1)}, u32[]{:S(2)}, u32[]{:S(2)}) collective-permute-start(bf16[288,2304]{1,0:T(8,128)(2,1)S(1)} %get-tuple-element.207), channel_id=1, source_target_pairs={{0,4},{1,5},{2,6},{3,7},{4,0},{5,1},{6,2},{7,3},{8,12},{9,13},{10,... | collective-permute-start | bytes 3981320 | tf_op jit(solution)/shard_map/cond/branch_1_fun/ppermute | solution.py:351
  268.3 29.7 %collective-permute-start.10 = (bf16[288,2304]{1,0:T(8,128)(2,1)S(1)}, bf16[288,2304]{1,0:T(8,128)(2,1)S(1)}, u32[]{:S(2)}, u32[]{:S(2)}) collective-permute-start(bf16[288,2304]{1,0:T(8,128)(2,1)S(1)} %get-tuple-element.207), channel_id=1, source_target_pairs={{0,2},{1,3},{2,0},{3,1},{4,6},{5,7},{6,4},{7,5},{8,10},{9,11},{10,... | collective-permute-start | bytes 3981320 | tf_op jit(solution)/shard_map/cond/branch_1_fun/ppermute | solution.py:351
  489.6 229.3 %reduce-scatter.10.cloned.1.call-start = ((), (), s32[]{:S(2)}) async-start(), calls=%async_computation.19 | async-start | bytes 4423680 | tf_op jit(solution)/shard_map/reduce_scatter | solution.py:871
  528.8 190.1 %reduce-scatter.8.cloned.1.call-start = ((), (), s32[]{:S(2)}) async-start(), calls=%async_computation.18 | async-start | bytes 6635520 | tf_op jit(solution)/shard_map/reduce_scatter | solution.py:871
  588.9 203.9 %reduce-scatter.12.cloned.1.call-start = ((), (), s32[]{:S(2)}) async-start(), calls=%async_computation.20 | async-start | bytes 6635520 | tf_op jit(solution)/shard_map/reduce_scatter | solution.py:871
  591.5 58.3 %collective-permute-start.42 = (bf16[2304,512]{1,0:T(8,128)(2,1)S(1)}, bf16[2304,512]{1,0:T(8,128)(2,1)S(1)}, u32[]{:S(2)}, u32[]{:S(2)}) collective-permute-start(bf16[2304,512]{1,0:T(8,128)(2,1)S(1)} %slice.333), channel_id=1, source_target_pairs={{0,1},{1,0},{2,3},{3,2},{4,5},{5,4},{6,7},{7,6},{8,9},{9,8},{10,11... | collective-permute-start | bytes 7077896 | tf_op jit(solution)/shard_map/cond/branch_1_fun/ppermute | solution.py:351
  627.9 30.1 %collective-permute-start.40 = (bf16[288,2304]{1,0:T(8,128)(2,1)S(1)}, bf16[288,2304]{1,0:T(8,128)(2,1)S(1)}, u32[]{:S(2)}, u32[]{:S(2)}) collective-permute-start(bf16[288,2304]{1,0:T(8,128)(2,1)S(1)} %get-tuple-element.243), channel_id=1, source_target_pairs={{0,2},{1,3},{2,0},{3,1},{4,6},{5,7},{6,4},{7,5},{8,10},{9,11},{10,... | collective-permute-start | bytes 3981320 | tf_op jit(solution)/shard_map/cond/branch_1_fun/ppermute | solution.py:351
  629.1 29.9 %collective-permute-start.41 = (bf16[288,2304]{1,0:T(8,128)(2,1)S(1)}, bf16[288,2304]{1,0:T(8,128)(2,1)S(1)}, u32[]{:S(2)}, u32[]{:S(2)}) collective-permute-start(bf16[288,2304]{1,0:T(8,128)(2,1)S(1)} %get-tuple-element.244), channel_id=1, source_target_pairs={{0,4},{1,5},{2,6},{3,7},{4,0},{5,1},{6,2},{7,3},{8,12},{9,13},{10,... | collective-permute-start | bytes 3981320 | tf_op jit(solution)/shard_map/cond/branch_1_fun/ppermute | solution.py:351
  665.9 196.1 %reduce-scatter.14.cloned.1.call-start = ((), (), s32[]{:S(2)}) async-start(), calls=%async_computation.21 | async-start | bytes 4485120 | tf_op jit(solution)/shard_map/reduce_scatter | solution.py:871
  667.1 32.3 %collective-permute-start.1 = (bf16[288,2304]{1,0:T(8,128)(2,1)}, bf16[288,2304]{1,0:T(8,128)(2,1)}, u32[]{:S(2)}, u32[]{:S(2)}) collective-permute-start(bf16[288,2304]{1,0:T(8,128)(2,1)} %get-tuple-element.258), channel_id=1, source_target_pairs={{0,4},{1,5},{2,6},{3,7},{4,0},{5,1},{6,2},{7,3},{8,12},{9,13},{10,... | collective-permute-start | bytes 3981320 | tf_op jit(solution)/shard_map/cond/branch_1_fun/ppermute | solution.py:351
  668.5 30.9 %collective-permute-start = (bf16[288,2304]{1,0:T(8,128)(2,1)}, bf16[288,2304]{1,0:T(8,128)(2,1)}, u32[]{:S(2)}, u32[]{:S(2)}) collective-permute-start(bf16[288,2304]{1,0:T(8,128)(2,1)} %get-tuple-element.258), channel_id=1, source_target_pairs={{0,2},{1,3},{2,0},{3,1},{4,6},{5,7},{6,4},{7,5},{8,10},{9,11},{10,... | collective-permute-start | bytes 3981320 | tf_op jit(solution)/shard_map/cond/branch_1_fun/ppermute | solution.py:351
  718.9 36.8 %all-to-all-start = ((bf16[8,72,1152]{2,1,0:T(8,128)(2,1)}), bf16[8,72,1152]{2,1,0:T(8,128)(2,1)}, u32[]{:S(2)}, u32[]{:S(2)}) async-start(bf16[8,72,1152]{2,1,0:T(8,128)(2,1)} %bitcast.183), calls=%async_computation | async-start | bytes 2654208 | tf_op jit(solution)/shard_map/cond/branch_1_fun/all_to_all | solution.py:853
  755.7 37.1 %all-to-all-start.1 = ((bf16[8,72,1152]{2,1,0:T(8,128)(2,1)}), bf16[8,72,1152]{2,1,0:T(8,128)(2,1)}, u32[]{:S(2)}, u32[]{:S(2)}) async-start(bf16[8,72,1152]{2,1,0:T(8,128)(2,1)} %pad_maximum_fusion.20), calls=%async_computation.1 | async-start | bytes 2654208 | tf_op jit(solution)/shard_map/cond/branch_1_fun/all_to_all | solution.py:853
  837.1 41.8 %collective-permute-start.54 = (bf16[288,2304]{1,0:T(8,128)(2,1)}, bf16[288,2304]{1,0:T(8,128)(2,1)}, u32[]{:S(2)}, u32[]{:S(2)}) collective-permute-start(bf16[288,2304]{1,0:T(8,128)(2,1)} %get-tuple-element.475), channel_id=1, source_target_pairs={{0,2},{1,3},{2,0},{3,1},{4,6},{5,7},{6,4},{7,5},{8,10},{9,11},{10,... | collective-permute-start | bytes 3981320 | tf_op jit(solution)/shard_map/ppermute | solution.py:351
  837.5 41.5 %collective-permute-start.55 = (bf16[288,2304]{1,0:T(8,128)(2,1)}, bf16[288,2304]{1,0:T(8,128)(2,1)}, u32[]{:S(2)}, u32[]{:S(2)}) collective-permute-start(bf16[288,2304]{1,0:T(8,128)(2,1)} %get-tuple-element.476), channel_id=1, source_target_pairs={{0,4},{1,5},{2,6},{3,7},{4,0},{5,1},{6,2},{7,3},{8,12},{9,13},{10,... | collective-permute-start | bytes 3981320 | tf_op jit(solution)/shard_map/ppermute | solution.py:351
  (130 other events, 1340.2 us)
Sparse Core Ops, SparseCore 0:
  30.5 70.0 all-gather.4
  102.1 184.6 all-gather.6
  289.0 68.1 all-gather.10
  359.2 38.8 all-gather.8
  489.8 38.8 reduce-scatter.5
  531.0 65.4 reduce-scatter.9
  598.9 95.1 reduce-scatter.7
  696.4 95.3 reduce-scatter.11
  794.2 67.7 reduce-scatter.13
